TPU v7x, 32 devices: a whole 2x2x4 slice. The times are simulated.
32 devices in a mesh: seq: 8 (over y, x, core), stream: 4 (over z).
Axes of the slice: x: 2, y: 2, z: 4, core: 2. Of those that a mesh axis runs over, the one named last changes fastest.
Arguments:
- tokens: bfloat16 [32, 1024, 768], P('seq', 'stream'), may hold values from -6 to 6
- source_len: int32 [32], P('seq'), may hold values from 1 to 512, as said below
- target_len: int32 [32], P('seq'), may hold values from 1 to 512, as said below
- timesteps: int32 [32], P('seq'), may hold values from 0 to 1999
- cotangent: bfloat16 [32, 1024, 768], P('seq', 'stream'), may hold values from -6 to 6
- query_weight: float32 [768, 768], P(('seq', 'stream')), may hold values from -0.21875 to 0.21875
- query_bias: float32 [768], P(('seq', 'stream')), may hold values from -3 to 3
- key_weight: float32 [768, 768], P(('seq', 'stream')), may hold values from -0.21875 to 0.21875
- value_weight: float32 [768, 768], P(('seq', 'stream')), may hold values from -0.21875 to 0.21875
- value_bias: float32 [768], P(('seq', 'stream')), may hold values from -0.3 to 0.3
- out_weight: float32 [768, 768], P(('seq', 'stream')), may hold values from -3.5 to 3.5
- out_bias: float32 [768], P(('seq', 'stream')), may hold values from -3 to 3
- attn_gain: float32 [768], P(('seq', 'stream')), may hold values from 0.5 to 1.5
- attn_shift: float32 [768], P(('seq', 'stream')), may hold values from -2 to 2
- up_weight: float32 [768, 3072], P(('seq', 'stream')), may hold values from -0.21875 to 0.21875
- up_bias: float32 [3072], P(('seq', 'stream')), may hold values from -3 to 3
- down_weight: float32 [3072, 768], P(('seq', 'stream')), may hold values from -0.109375 to 0.109375
- down_bias: float32 [768], P(('seq', 'stream')), may hold values from -3 to 3
- ffn_gain: float32 [768], P(('seq', 'stream')), may hold values from 0.5 to 1.5
- ffn_shift: float32 [768], P(('seq', 'stream')), may hold values from -2 to 2
- stamp_weight: float32 [128, 768], P(('seq', 'stream')), may hold values from -0.5 to 0.5
- stamp_bias: float32 [768], P(('seq', 'stream')), may hold values from -3 to 3
- embed_weight: float32 [768, 768], P(('seq', 'stream')), may hold values from -0.21875 to 0.21875
- embed_bias: float32 [768], P(('seq', 'stream')), may hold values from -3 to 3
Outputs:
- output: bfloat16 [32, 1024, 768], P('seq', 'stream')
- token_grad: float32 [32, 1024, 768], P('seq', 'stream')
- query_weight_grad: float32 [768, 768], P(('seq', 'stream'))
- query_bias_grad: float32 [768], P(('seq', 'stream'))
- key_weight_grad: float32 [768, 768], P(('seq', 'stream'))
- value_weight_grad: float32 [768, 768], P(('seq', 'stream'))
- value_bias_grad: float32 [768], P(('seq', 'stream'))
- out_weight_grad: float32 [768, 768], P(('seq', 'stream'))
- out_bias_grad: float32 [768], P(('seq', 'stream'))
- attn_gain_grad: float32 [768], P(('seq', 'stream'))
- attn_shift_grad: float32 [768], P(('seq', 'stream'))
- up_weight_grad: float32 [768, 3072], P(('seq', 'stream'))
- up_bias_grad: float32 [3072], P(('seq', 'stream'))
- down_weight_grad: float32 [3072, 768], P(('seq', 'stream'))
- down_bias_grad: float32 [768], P(('seq', 'stream'))
- ffn_gain_grad: float32 [768], P(('seq', 'stream'))
- ffn_shift_grad: float32 [768], P(('seq', 'stream'))
- stamp_weight_grad: float32 [128, 768], P(('seq', 'stream'))
- stamp_bias_grad: float32 [768], P(('seq', 'stream'))
- embed_weight_grad: float32 [768, 768], P(('seq', 'stream'))
- embed_bias_grad: float32 [768], P(('seq', 'stream'))
Inputs may be any that keep to these rules, and one draw needn't show every extreme that they name: `source_len`: in each aligned block of 4 sequences (those of one index of seq) one, chosen by the seed, has the full source length 512. `target_len`: in each aligned block of 4 sequences (those of one index of seq) one, chosen by the seed, has the full target length 512.
All inputs are finite; a program needn't handle non-finite values.
Results may differ from a plain program's by a relative error of at most 0.015.
The roundings to bfloat16 on the way count: a program that leaves them out, or rounds other values in their place, can miss the bound.
Values may be sent and summed in bfloat16 or wider, within the bound.
No kernel may reach another device: no remote copies, remote signals or barrier semaphores. Data moves between devices by JAX's collectives and lax.ppermute only.
A program may use at most 384 MiB of HBM per device.

v0:
```python
import functools
import math

import jax
import jax.numpy as jnp
from jax import lax
from jax.experimental import pallas as pl
from jax.experimental.pallas import tpu as pltpu
from jax.sharding import PartitionSpec as P

F32=jnp.float32; BF=jnp.bfloat16
NT=(((1,),(1,)),((),())); NN=(((1,),(0,)),((),())); TN=(((0,),(0,)),((),()))
def mm(a,b,dims): return lax.dot_general(a,b,dims,preferred_element_type=F32)
def lanes(shape): return lax.broadcasted_iota(jnp.int32,shape,len(shape)-1)
def split3(x):
    hi=x.astype(BF).astype(F32); r=x-hi
    mid=r.astype(BF).astype(F32); lo=r-mid
    return hi,mid,lo
QB=256
def fwd_kernel(q_ref,k_ref,v_ref,auxk_ref,o_ref,auxq_ref,kaug,vm):
    L=q_ref.shape[0]
    k=k_ref[...]; v=v_ref[...]; ln=lanes(k.shape)
    for e in range(2):
        sel=(ln<64) if e==0 else (ln>=64)
        kaug[e,:,:128]=jnp.where(sel,k,jnp.zeros_like(k))
        kaug[e,:,128:]=auxk_ref[...]
        vm[e]=jnp.where(sel,v,(ln==64*(1-e)).astype(BF))
    ln=lanes((QB,128)); one=jnp.where(ln==64,1.0,0.0).astype(BF)
    steps=[(b,e) for b in range(L//QB) for e in range(2)]
    def score(b,e):
        return mm(jnp.concatenate([q_ref[pl.ds(b*QB,QB),:],one],axis=1),kaug[e],NT)
    s=score(*steps[0]); out=None; aux=None
    for t,(b,e) in enumerate(steps):
        later=score(*steps[t+1]) if t+1<len(steps) else None
        m=jnp.max(s,axis=1,keepdims=True)
        p=jnp.exp(s-m).astype(BF)
        o=mm(p,vm[e],NN)
        l=o[:,64*(1-e):64*(1-e)+1]
        o=jnp.where((ln<64) if e==0 else (ln>=64),o*(1.0/l),0.0)
        hi,mid,lo=split3(-(m+jnp.log(l)))
        if e==0: out=o; aux=jnp.where(ln==64,1.0,0.0)
        else: out=out+o
        aux=jnp.where(ln==3*e,hi,aux); aux=jnp.where(ln==3*e+1,mid,aux); aux=jnp.where(ln==3*e+2,lo,aux)
        if e==1:
            r=pl.ds(b*QB,QB)
            o_ref[r,:]=out.astype(BF); auxq_ref[0,r,:]=aux.astype(BF)
        s=later
def attn_fwd(q,k,v,auxk,p0,np_):
    L=q.shape[0]
    col=lambda: pl.BlockSpec((L,128),lambda p:(0,p0+p))
    return pl.pallas_call(fwd_kernel,grid=(np_,),
      in_specs=[col(),col(),col(),pl.BlockSpec((L,128),lambda p:(0,0))],
      out_specs=[pl.BlockSpec((L,128),lambda p:(0,p)),pl.BlockSpec((1,L,128),lambda p:(p,0,0))],
      out_shape=[jax.ShapeDtypeStruct((L,128*np_),BF),jax.ShapeDtypeStruct((np_,L,128),BF)],
      scratch_shapes=[pltpu.VMEM((2,L,256),BF),pltpu.VMEM((2,L,128),BF)],
      compiler_params=pltpu.CompilerParams(vmem_limit_bytes=60*2**20),
      cost_estimate=pl.CostEstimate(flops=np_*2*L*L*64*4,bytes_accessed=np_*L*128*2*5,transcendentals=np_*2*L*L),
      name="attn_fwd")(q,k,v,auxk)
def bwd_kernel(p0,q_ref,k_ref,v_ref,do_ref,auxk_ref,auxq_ref,auxd_ref,out_ref,kaug,vaug,qa,doa,qm,dom,dk_acc,dv_acc):
    pair=p0+pl.program_id(0)
    L=q_ref.shape[0]
    k=k_ref[...]; v=v_ref[...]; q=q_ref[...]; do=do_ref[...]
    ln=lanes(k.shape); z=jnp.zeros_like(k); auxk=auxk_ref[...]
    qa[:,:128]=q; qa[:,128:]=auxq_ref[0]
    doa[:,:128]=do; doa[:,128:]=auxd_ref[...]
    for e in range(2):
        sel=(ln<64) if e==0 else (ln>=64)
        on=(ln>=3*e)&(ln<3*e+3)
        kaug[e,:,:128]=jnp.where(sel,k,z)
        kaug[e,:,128:]=jnp.where(on,jnp.ones_like(k),auxk)
        vaug[e,:,:128]=jnp.where(sel,v,z)
        b=6*pair+3*e
        vaug[e,:,128:]=jnp.where((ln>=b)&(ln<b+3),jnp.ones_like(k),z)
        qm[e]=jnp.where(sel,q,z)
        dom[e]=jnp.where(sel,do,z)
    for i in range(L//QB):
        r=pl.ds(i*QB,QB)
        dq=None
        for e in range(2):
            p=jnp.exp(mm(kaug[e],qa[r,:],NT))
            dp=mm(vaug[e],doa[r,:],NT)
            ds=(p*dp).astype(BF)
            dv=mm(p.astype(BF),dom[e,r,:],NN)
            dk=mm(ds,qm[e,r,:],NN)
            if i==0 and e==0: dv_acc[...]=dv; dk_acc[...]=dk
            else: dv_acc[...]+=dv; dk_acc[...]+=dk
            d=mm(ds,kaug[e,:,:128],TN)
            dq=d if dq is None else dq+d
        out_ref[0,r,:]=(dq*0.125).astype(BF)
    out_ref[1]=dk_acc[...].astype(BF)
    out_ref[2]=dv_acc[...].astype(BF)
def attn_bwd(q,k,v,do,auxk,auxq,auxd,p0,np_,a0):
    L=q.shape[0]
    col=lambda: pl.BlockSpec((L,128),lambda p:(0,p0+p))
    con=lambda: pl.BlockSpec((L,128),lambda p:(0,0))
    return pl.pallas_call(functools.partial(bwd_kernel,p0),grid=(np_,),
      in_specs=[col(),col(),col(),col(),con(),pl.BlockSpec((1,L,128),lambda p:(a0+p,0,0)),con()],
      out_specs=pl.BlockSpec((3,L,128),lambda p:(0,0,p)),
      out_shape=jax.ShapeDtypeStruct((3,L,128*np_),BF),
      scratch_shapes=[pltpu.VMEM((2,L,256),BF),pltpu.VMEM((2,L,256),BF),pltpu.VMEM((L,256),BF),pltpu.VMEM((L,256),BF),
        pltpu.VMEM((2,L,128),BF),pltpu.VMEM((2,L,128),BF),pltpu.VMEM((L,128),F32),pltpu.VMEM((L,128),F32)],
      compiler_params=pltpu.CompilerParams(vmem_limit_bytes=60*2**20),
      cost_estimate=pl.CostEstimate(flops=np_*2*L*L*64*10,bytes_accessed=np_*L*128*2*9,transcendentals=np_*2*L*L),
      name="attn_bwd")(q,k,v,do,auxk,auxq,auxd)

SMALL=16; Q_B,V_B,OUT_B,ATT_G,ATT_S,DOWN_B,FFN_G,FFN_S,STAMP_B,EMBED_B=range(4,14); UP_B=14
def owner_of(rows,me,unit,width):
    r=lax.shift_right_logical(lax.broadcasted_iota(jnp.int32,(rows,width),0),SMALL.bit_length()-1)
    shift=unit.bit_length()-1
    t=lax.shift_right_logical(r,shift)
    g=jnp.bitwise_xor(jnp.bitwise_or(jnp.bitwise_and(t*2,7),lax.shift_right_logical(t,2)),me)
    return g*unit+jnp.bitwise_and(r,unit-1)
def repeats(width,shard):
    l=lax.broadcasted_iota(jnp.int32,(128,width),0).astype(F32); d=lax.broadcasted_iota(jnp.int32,(128,width),1).astype(F32)
    return (d-shard*jnp.floor((d+0.5)*(1.0/shard))==l).astype(BF)
def owned(owner,shard):
    d=lax.broadcasted_iota(jnp.int32,owner.shape,1)
    return (d>=owner*shard)&(d<owner*shard+shard)
def pack_kernel(*refs):
    *ins,first_ref,second_ref,scr=refs
    wq,wk,wv,we,st,wo,wd,wu=ins[:8]; vecs=ins[8:]
    scr[...]=jnp.zeros_like(scr)
    scr[:st.shape[0],:]=st[...]
    for r,v in enumerate(vecs):
        scr[4+r:5+r,:v.shape[0]]=v[...].reshape(1,-1)
    D=wq.shape[1]
    first_ref[...]=jnp.concatenate([wq[...],wk[...],wv[...],we[...],scr[...]],axis=0).astype(BF)
    up=[wu[:,c*D:(c+1)*D] for c in range(wu.shape[1]//D)]
    second_ref[...]=jnp.concatenate([wo[...],wd[...]]+up,axis=0).astype(BF)
def pack(mats,vecs):
    wq,wk,wv,we,st,wo,wd,wu=mats; n,D=wq.shape
    vm=pl.BlockSpec(memory_space=pltpu.VMEM)
    second=n+wd.shape[0]+n*(wu.shape[1]//D)
    if n%8:
        small=jnp.concatenate([st]+[jnp.zeros((4-st.shape[0],D),F32)]+[jnp.pad(v,(0,D-v.shape[0]))[None] for v in vecs]+[jnp.zeros((SMALL-4-len(vecs),D),F32)])
        up=[wu[:,c*D:(c+1)*D] for c in range(wu.shape[1]//D)]
        return jnp.concatenate([wq,wk,wv,we,small]).astype(BF),jnp.concatenate([wo,wd]+up).astype(BF)
    return pl.pallas_call(pack_kernel,in_specs=[vm]*(8+len(vecs)),out_specs=[vm]*2,
      out_shape=[sds((4*n+SMALL,D),BF),sds((second,D),BF)],scratch_shapes=[pltpu.VMEM((SMALL,D),F32)],name="pack")(*mats,*vecs)
ORDER=(0,2,4,6,1,3,5,7)
def rows_at(me,t,n):
    return pl.ds(pl.multiple_of(jnp.bitwise_xor(me,ORDER[t])*n,n),n)
def sds(*a): return jax.ShapeDtypeStruct(*a)
def once(s): return pl.BlockSpec(s.shape,lambda i:(0,)*len(s.shape),pipeline_mode=pl.Buffered(1))
def smem(): return pl.BlockSpec(memory_space=pltpu.SMEM)
def anyw(): return pl.BlockSpec(memory_space=pl.ANY)
def load_weights(me,pieces,base,n,dst,sem):
    return [pltpu.make_async_copy(p.at[pl.ds(base,n),:],dst.at[rows_at(me,t,n),:],sem) for t,p in enumerate(pieces)]
def in_kernel(nt,unit,me_ref,info_ref,feat_ref,*rest):
    toks=rest[:nt]; pieces=rest[nt:nt+8]
    mixed_ref,inp_ref,q_ref,k_ref,v_ref,auxk_ref,pre_ref,hid_ref,vec_ref,upb_ref,tok,wq,wk,wv,we,ws,emb,sems=rest[nt+8:]
    i=pl.program_id(0); me=me_ref[0]
    D=wq.shape[0]; n=D//8; ns=ws.shape[0]//8
    tcp=[pltpu.make_async_copy(t,tok.at[c],sems.at[5+c]) for c,t in enumerate(toks)]
    scp=[pltpu.make_async_copy(p.at[pl.ds(4*n,ns),:],ws.at[pl.ds(t*ns,ns),:],sems.at[0]) for t,p in enumerate(pieces)]
    wcp=[load_weights(me,pieces,w*n,n,dst,sems.at[1+w]) for w,dst in enumerate((wq,wk,wv,we))]
    vec=lambda r: vec_ref[pl.ds(r,1),:]
    @pl.when(i==0)
    def _():
        for c in scp+wcp[3]+tcp[:1]+wcp[0]+wcp[1]+wcp[2]+tcp[1:]: c.start()
        for c in scp: c.wait()
        rows=8*ns; total=8*unit; FF=upb_ref.shape[1]
        lead=ws[:,:128]
        spread=mm(lead,repeats(D,D//total),NN)
        spread=jnp.where(owned(owner_of(rows,me,unit,D),D//total),spread,0.0)
        vec_ref[...]=jnp.sum(spread.reshape(total,SMALL,D),axis=0)
        ups=lead.astype(F32).reshape(total,SMALL,128)[:,UP_B,:].astype(BF)
        ups=mm(ups,repeats(FF,FF//total),NN)
        own=owner_of(rows,me,unit,128).reshape(total,SMALL,128)[:,0,:1]
        upb_ref[...]=jnp.sum(jnp.where(owned(jnp.broadcast_to(own,(total,FF)),FF//total),ups,0.0),axis=0,keepdims=True)
        pre=mm(feat_ref[...],ws[...],NN)+vec(STAMP_B)
        pre_ref[...]=pre
        hid=(pre/(1.0+jnp.exp(-pre))).astype(BF)
        hid_ref[...]=hid
        for c in wcp[3]: c.wait()
        emb[...]=mm(hid,we[...],NN)+vec(EMBED_B)
    for c in range(nt):
        @pl.when(i==c)
        def _(): tcp[c].wait()
    flag=info_ref[i,0].astype(F32); nlive=info_ref[i,1]
    x=tok[i].astype(F32)+flag*emb[pl.ds(0,1),:]
    mixed_ref[...]=x
    xb=x.astype(BF); inp_ref[...]=xb
    R=x.shape[0]
    ln=lanes((R,128)); row=lax.broadcasted_iota(jnp.int32,(R,128),0)
    auxk_ref[...]=jnp.where((ln==64)&(row>=nlive),-1e30,0.0).astype(BF)
    @pl.when(i==0)
    def _():
        for w in range(3):
            for c in wcp[w]: c.wait()
    q=(mm(xb,wq[...],NN)+vec(Q_B)).astype(BF)
    q_ref[...]=(q.astype(F32)*0.125).astype(BF)
    k_ref[...]=mm(xb,wk[...],NN).astype(BF)
    v_ref[...]=(mm(xb,wv[...],NN)+vec(V_B)).astype(BF)
def project(me,info,feat,toks,pieces,unit,FF):
    nt=len(toks); R,D=toks[0].shape; n=D//8; ns=pieces[0].shape[0]-4*n; L=nt*R
    row=lambda w: pl.BlockSpec((R,w),lambda i:(i,0))
    full=lambda a: pl.BlockSpec(a.shape,lambda i:(0,)*a.ndim)
    outs=[sds((L,D),F32)]+[sds((L,D),BF)]*4+[sds((L,128),BF),sds((8,D),F32),sds((8,D),BF),sds((SMALL,D),F32),sds((1,FF),F32)]
    return pl.pallas_call(functools.partial(in_kernel,nt,unit),grid=(nt,),
      in_specs=[smem(),smem(),full(feat)]+[anyw()]*(nt+8),
      out_specs=[row(D)]*5+[row(128)]+[once(o) for o in outs[6:]],
      out_shape=outs,
      scratch_shapes=[pltpu.VMEM((nt,R,D),BF)]+[pltpu.VMEM((D,D),BF)]*4+[pltpu.VMEM((8*ns,D),BF),pltpu.VMEM((8,D),F32),pltpu.SemaphoreType.DMA((5+nt,))],
      compiler_params=pltpu.CompilerParams(vmem_limit_bytes=60*2**20),
      cost_estimate=pl.CostEstimate(flops=2*L*D*D*3,bytes_accessed=20_000_000,transcendentals=0),
      name="project")(me,info,feat,*toks,*pieces)

def spread3(row):
    hi,mid,lo=split3(row)
    r=lax.broadcasted_iota(jnp.int32,(8,row.shape[1]),0)
    return jnp.where(r==0,hi,jnp.where(r==1,mid,jnp.where(r==2,lo,0.0))).astype(BF)
def three(rows):
    r=lax.broadcasted_iota(jnp.int32,rows.shape,0)
    return jnp.where(r<3,jnp.broadcast_to(rows[0:1,:].astype(F32),rows.shape),0.0).astype(BF)
def token_kernel(nc,me_ref,info_ref,ga_ref,pre_ref,*rest):
    grads=rest[:nc]; pieces=rest[nc:nc+8]
    tg_ref,rows_ref,wq,wk,wv,we,sems=rest[nc+8:]
    i=pl.program_id(0); me=me_ref[0]
    D=wq.shape[0]; n=D//8
    wcp=[load_weights(me,pieces,w*n,n,dst,sems.at[w]) for w,dst in enumerate((wq,wk,wv,we))]
    @pl.when(i==0)
    def _():
        for w in wcp:
            for c in w: c.start()
        rows_ref[...]=jnp.zeros_like(rows_ref)
    g=ga_ref[...]
    for w,dst in enumerate((wq,wk,wv)):
        y=jnp.concatenate([s[w] for s in grads],axis=1)
        if w!=1: rows_ref[pl.ds(w//2,1),:]+=jnp.sum(y.astype(F32),axis=0,keepdims=True)
        @pl.when(i==0)
        def _():
            for c in wcp[w]: c.wait()
        g=g+mm(y,dst[...],NT)
    tg_ref[0]=g.astype(BF)
    rows_ref[pl.ds(3,1),:]+=info_ref[i,0].astype(F32)*jnp.sum(g,axis=0,keepdims=True)
    @pl.when(i==pl.num_programs(0)-1)
    def _():
        for c in wcp[3]: c.wait()
        gh=jnp.sum(mm(spread3(rows_ref[pl.ds(3,1),:]),we[...],NT),axis=0,keepdims=True)
        pre=pre_ref[0:1,:]
        sg=1.0/(1.0+jnp.exp(-pre))
        rows_ref[pl.ds(2,1),:]=gh*(sg*(1.0+pre*(1.0-sg)))
def token_grads(me,info,ga,pre,grads,pieces,R):
    L,D=ga.shape; nt=L//R; nc=len(grads); W=grads[0].shape[2]
    outs=[sds((nt,R,D),BF),sds((8,D),F32)]
    return pl.pallas_call(functools.partial(token_kernel,nc),grid=(nt,),
      in_specs=[smem(),smem(),pl.BlockSpec((R,D),lambda i:(i,0)),pl.BlockSpec((8,D),lambda i:(0,0))]+[pl.BlockSpec((3,R,W),lambda i:(0,i,0))]*nc+[anyw()]*8,
      out_specs=[pl.BlockSpec((1,R,D),lambda i:(i,0,0)),once(outs[1])],
      out_shape=outs,
      scratch_shapes=[pltpu.VMEM((D,D),BF)]*4+[pltpu.SemaphoreType.DMA((4,))],
      compiler_params=pltpu.CompilerParams(vmem_limit_bytes=60*2**20),
      cost_estimate=pl.CostEstimate(flops=2*L*D*D*3,bytes_accessed=15_000_000,transcendentals=0),
      name="token_grads")(me,info,ga,pre,*grads,*pieces)
def weight_kernel(nc,unit,me_ref,inp_ref,rows_ref,hid_ref,feat_ref,dvec_ref,dupb_ref,*rest):
    grads=rest[:nc]
    mine_ref,theirs_ref,acc=rest[nc:]
    i=pl.program_id(0); me=me_ref[0]
    D=inp_ref.shape[1]; n=D//8; rows=feat_ref.shape[1]; ns=rows//8
    def to(t): return mine_ref if t<4 else theirs_ref
    @pl.when(i==0)
    def _():
        acc[:,3*D:]=mm(three(hid_ref[...]),spread3(rows_ref[3:4,:]),TN)
        total=8*unit; FF=dupb_ref.shape[1]
        r=lax.broadcasted_iota(jnp.int32,(SMALL,D),0)
        vec=dvec_ref[...]
        for at,row in ((Q_B,0),(V_B,1),(STAMP_B,2),(EMBED_B,3)):
            vec=jnp.where(r==at,rows_ref[row:row+1,:],vec)
        vec=jnp.broadcast_to(vec[None],(total,SMALL,D)).reshape(rows,D)
        vec=jnp.where(owned(owner_of(rows,me,unit,D),D//total),vec,0.0).astype(BF)
        vec=mm(vec,repeats(D,D//total),NT)
        own=owner_of(rows,me,unit,128).reshape(total,SMALL,128)[:,0,:1]
        ups=jnp.where(owned(jnp.broadcast_to(own,(total,FF)),FF//total),dupb_ref[...],0.0).astype(BF)
        ups=mm(ups,repeats(FF,FF//total),NT)
        line=jnp.bitwise_and(lax.broadcasted_iota(jnp.int32,(rows,128),0),SMALL-1)
        ups=jnp.broadcast_to(ups[:,None,:],(total,SMALL,128)).reshape(rows,128)
        vec=jnp.where(line==UP_B,ups,jnp.where((line>=4)&(line<UP_B),vec,0.0))
        small=mm(three(feat_ref[...]),spread3(rows_ref[2:3,:]),TN)
        small=small+jnp.concatenate([vec,jnp.zeros((rows,D-128),F32)],axis=1)
        small=small.astype(BF)
        for t in range(8): to(t)[t%4,4*n:,:]=small[t*ns:(t+1)*ns]
    part=mm(inp_ref[...],jnp.concatenate([s[w] for w in range(3) for s in grads],axis=1),TN)
    @pl.when(i==0)
    def _(): acc[:,:3*D]=part
    @pl.when(i>0)
    def _(): acc[:,:3*D]+=part
    @pl.when(i==pl.num_programs(0)-1)
    def _():
        for t in range(8):
            for w in range(4): to(t)[t%4,w*n:(w+1)*n,:]=acc[rows_at(me,t,n),w*D:(w+1)*D].astype(BF)
def weight_grads(me,inp,rows,hid,feat,dvec,dupb,grads,unit,R):
    L,D=inp.shape; n=D//8; nc=len(grads); W=grads[0].shape[2]
    outs=[sds((4,4*n+feat.shape[1]//8,D),BF)]*2
    full=lambda a: pl.BlockSpec(a.shape,lambda i:(0,)*a.ndim)
    return pl.pallas_call(functools.partial(weight_kernel,nc,unit),grid=(L//R,),
      in_specs=[smem(),pl.BlockSpec((R,D),lambda i:(i,0))]+[full(a) for a in (rows,hid,feat,dvec,dupb)]+[pl.BlockSpec((3,R,W),lambda i:(0,i,0))]*nc,
      out_specs=[once(o) for o in outs],out_shape=outs,
      scratch_shapes=[pltpu.VMEM((D,4*D),F32)],
      compiler_params=pltpu.CompilerParams(vmem_limit_bytes=60*2**20),
      cost_estimate=pl.CostEstimate(flops=2*L*D*D*3,bytes_accessed=12_000_000,transcendentals=0),
      name="weight_grads")(me,inp,rows,hid,feat,dvec,dupb,*grads)
LB=384
def take(k,R): return pl.BlockSpec((1,R,LB),lambda i:(k,0,i))
def flat(R): return pl.BlockSpec((R,LB),lambda i:(0,i))
def total_of(refs):
    out=refs[0].astype(F32)
    for r in refs[1:]: out=out+r.astype(F32)
    return out
def diag_kernel(cut,a,b,low,high):
    x=total_of((a[0],b[0])).astype(BF)
    low[...]=x[:cut]; high[...]=x[cut:]
def sum_diag(mine,got,cut):
    _,R,D=mine.shape
    return pl.pallas_call(functools.partial(diag_kernel,cut),grid=(D//LB,),in_specs=[take(3,R)]*2,out_specs=[flat(cut),flat(R-cut)],
      out_shape=[sds((cut,D),BF),sds((R-cut,D),BF)],name="sum_diag")(mine,got)
def near_kernel(cut,a1,b1,a2,b2,low,high,fx,fy):
    fx[:cut,:]=total_of((a1[0,:cut],b1[0,:cut])).astype(BF)
    fx[cut:,:]=total_of((a1[0,cut:],b1[0,cut:],high[...])).astype(BF)
    fy[:cut,:]=total_of((a2[0,:cut],b2[0,:cut],low[...])).astype(BF)
    fy[cut:,:]=total_of((a2[0,cut:],b2[0,cut:])).astype(BF)
def sum_near(mine,got,low,high):
    _,R,D=mine.shape; cut=low.shape[0]
    return pl.pallas_call(functools.partial(near_kernel,cut),grid=(D//LB,),in_specs=[take(1,R)]*2+[take(2,R)]*2+[flat(cut),flat(R-cut)],
      out_specs=[flat(R)]*2,out_shape=[sds((R,D),BF)]*2,name="sum_near")(mine,got,mine,got,low,high)
def three_kernel(a1,b1,a2,b2,a3,b3,o1,o2,o3):
    for a,b,o in ((a1,b1,o1),(a2,b2,o2),(a3,b3,o3)): o[...]=total_of((a[0],b[0])).astype(BF)
def sum_three(mine,got):
    _,R,D=mine.shape
    return pl.pallas_call(three_kernel,grid=(D//LB,),in_specs=[take(1,R)]*2+[take(2,R)]*2+[take(3,R)]*2,
      out_specs=[flat(R)]*3,out_shape=[sds((R,D),BF)]*3,name="sum_three")(mine,got,mine,got,mine,got)
def own_kernel(sizes,unit,nx,inner_ref,a,b,*rest):
    more=rest[:nx]; keep,send,scr=rest[nx:]
    inner=inner_ref[0]
    scr[...]=total_of((a[0],b[0])+tuple(x[...] for x in more))
    for j in range(unit):
        k=jnp.bitwise_xor(inner,j); at=0; out=0
        for count,size in sizes:
            for c in range(count):
                x=scr[pl.ds(pl.multiple_of(at+k*size,8),size),:]
                if j%2: send[j//2,out:out+size,:]=x.astype(BF)
                else: keep[j//2,out:out+size,:]=x
                at+=unit*size; out+=size
def sum_own(inner,mine,got,more,sizes,unit,total):
    _,R,D=mine.shape; rows=R//unit
    if any(size%8 for _,size in sizes):
        x=mine[0].astype(F32)+got[0].astype(F32)+sum(m.astype(F32) for m in more); at=0; parts=[]
        for count,size in sizes:
            for c in range(count):
                parts.append(x[at:at+unit*size].reshape(unit,size,D)); at+=unit*size
        return split_send(in_order(jnp.concatenate(parts,1),inner),1,total)
    blk=pl.BlockSpec((unit//2,rows,LB),lambda i:(0,0,i))
    keep,send=pl.pallas_call(functools.partial(own_kernel,sizes,unit,len(more)),grid=(D//LB,),
      in_specs=[smem()]+[take(0,R)]*2+[flat(R)]*len(more),out_specs=[blk]*2,
      out_shape=[sds((unit//2,rows,D),F32),sds((unit//2,rows,D),BF)],scratch_shapes=[pltpu.VMEM((R,LB),F32)],name="sum_own")(inner.reshape(1).astype(jnp.int32),mine,got,*more)
    return keep,flip(send,1,total)
def last1_kernel(keep_ref,got_ref,*outs):
    x=keep_ref[...]+got_ref[...].astype(F32)
    *mats,st=outs[:5]; n=mats[0].shape[0]
    for w,o in enumerate(mats): o[...]=x[w*n:(w+1)*n]
    st[...]=x[4*n:4*n+st.shape[0]]
    for r,o in enumerate(outs[5:]):
        o[...]=x[4*n+4+r:4*n+5+r,:o.shape[0]].reshape(o.shape)
def last1(keep,got,n,stamp_rows,sizes):
    D=keep.shape[1]
    vm=pl.BlockSpec(memory_space=pltpu.VMEM)
    outs=[sds((n,D),F32)]*4+[sds((stamp_rows,D),F32)]+[sds((k,),F32) for k in sizes]
    if n%8:
        x=keep+got.astype(F32)
        return [x[w*n:(w+1)*n] for w in range(4)]+[x[4*n:4*n+stamp_rows]]+[x[4*n+4+r,:k] for r,k in enumerate(sizes)]
    return pl.pallas_call(last1_kernel,in_specs=[vm]*2,out_specs=[vm]*len(outs),out_shape=outs,name="last_attn")(keep,got)
def last2_kernel(keep_ref,got_ref,wo,wd,wu):
    x=keep_ref[...]+got_ref[...].astype(F32); n,D=wo.shape; m=wd.shape[0]
    wo[...]=x[:n]; wd[...]=x[n:n+m]
    for c in range(wu.shape[1]//D): wu[:,c*D:(c+1)*D]=x[n+m+c*n:n+m+(c+1)*n]
def last2(keep,got,n,m,FF):
    D=keep.shape[1]
    vm=pl.BlockSpec(memory_space=pltpu.VMEM)
    outs=[sds((n,D),F32),sds((m,D),F32),sds((n,FF),F32)]
    if n%8:
        x=keep+got.astype(F32)
        return x[:n],x[n:n+m],jnp.concatenate([x[n+m+c*n:n+m+(c+1)*n] for c in range(FF//D)],1)
    return pl.pallas_call(last2_kernel,in_specs=[vm]*2,out_specs=[vm]*3,out_shape=outs,name="last_ffn")(keep,got)

INV_SQRT2=0.7071067811865476; INV_SQRT2PI=0.3989422804014327
HEAD=64
RB=256; FC=768
def norm_stats(x):
    mu=jnp.mean(x,axis=1,keepdims=True); c=x-mu
    r=lax.rsqrt(jnp.mean(c*c,axis=1,keepdims=True)+1e-5)
    return c*r,r
def norm_back(e,n,r):
    return r*(e-jnp.mean(e,axis=1,keepdims=True)-n*jnp.mean(e*n,axis=1,keepdims=True))
def colsum(x): return jnp.sum(x,axis=0,keepdims=True)
def mid_kernel(nblk,me_ref,info_ref,mix_ref,cot_ref,att_refs,vec_ref,upb_ref,pieces,
        out_ref,gas_ref,gatt_ref,auxd_ref,mine_ref,theirs_ref,dvec_ref,dupb_ref,
        wo,wd,wu,awo,awd,awu,gel,dgel,sems):
    i=pl.program_id(0); nb=pl.num_programs(0)
    D=wo.shape[0]; FF=wd.shape[0]; ro=D//nblk; rd=FF//nblk
    me=me_ref[0]
    lower=[p[0] if isinstance(p,tuple) else p for p in pieces]
    upper=[(p[1],0) if isinstance(p,tuple) else (p,ro+rd) for p in pieces]
    cps=[load_weights(me,lower,0,ro,wo,sems.at[0]),
        [pltpu.make_async_copy(p.at[pl.ds(at+b*ro,ro),:],wu.at[rows_at(me,t,ro),pl.ds(b*D,D)],sems.at[1])
            for b in range(FF//D) for t,(p,at) in enumerate(upper)],
        load_weights(me,lower,ro,rd,wd,sems.at[2])]
    def wait(which):
        @pl.when(i==0)
        def _():
            for c in cps[which]: c.wait()
    @pl.when(i==0)
    def _():
        for w in cps:
            for c in w: c.start()
        awo[...]=jnp.zeros_like(awo); awd[...]=jnp.zeros_like(awd); awu[...]=jnp.zeros_like(awu)
        dvec_ref[...]=jnp.zeros_like(dvec_ref); dupb_ref[...]=jnp.zeros_like(dupb_ref)
    vec=lambda r: vec_ref[pl.ds(r,1),:].astype(F32)
    nlive=info_ref[i,1]
    x0=mix_ref[...]
    live=(lax.broadcasted_iota(jnp.int32,(RB,1),0)<nlive).astype(F32)
    wait(0)
    att=jnp.concatenate([a[...] for a in att_refs],axis=1)
    asum=x0+(mm(att,wo[...],NN)+vec(OUT_B))
    n1,r1=norm_stats(asum)
    normed=n1*vec(ATT_G)+vec(ATT_S)
    hid=normed.astype(BF)
    wait(1); wait(2)
    down=None
    for f in range(FF//FC):
        c=slice(f*FC,(f+1)*FC)
        u=mm(hid,wu[:,c],NN)+upb_ref[:,c].astype(F32)
        ph=0.5+0.5*lax.erf(u*INV_SQRT2)
        pd=jnp.exp(u*u*-0.5)*INV_SQRT2PI
        g=(u*ph).astype(BF)
        gel[:,c]=g
        dgel[:,c]=ph+u*pd
        t=mm(g,wd[c,:],NN)
        down=t if down is None else down+t
    fsum=normed+(down+vec(DOWN_B))
    n2,r2=norm_stats(fsum)
    g2=vec(FFN_G)
    out_ref[0]=((n2*g2+vec(FFN_S))*live).astype(BF)
    og=cot_ref[0].astype(F32)*live
    dvec_ref[pl.ds(FFN_G,1),:]+=colsum(og*n2)
    dvec_ref[pl.ds(FFN_S,1),:]+=colsum(og)
    gf=norm_back(og*g2,n2,r2)
    gd=gf.astype(BF)
    dvec_ref[pl.ds(DOWN_B,1),:]+=colsum(gd.astype(F32))
    gn=gf
    for f in range(FF//FC):
        c=slice(f*FC,(f+1)*FC)
        gu=(mm(gd,wd[c,:],NT)*dgel[:,c]).astype(BF)
        dupb_ref[:,c]+=colsum(gu.astype(F32))
        awd[c,:]+=mm(gel[:,c],gd,TN)
        awu[:,c]+=mm(hid,gu,TN)
        gn=gn+mm(gu,wu[:,c],NT)
    dvec_ref[pl.ds(ATT_G,1),:]+=colsum(gn*n1)
    dvec_ref[pl.ds(ATT_S,1),:]+=colsum(gn)
    ga=norm_back(gn*vec(ATT_G),n1,r1)
    gas_ref[...]=ga
    gb=ga.astype(BF)
    dvec_ref[pl.ds(OUT_B,1),:]+=colsum(gb.astype(F32))
    awo[...]+=mm(att,gb,TN)
    gatt=mm(gb,wo[...],NT).astype(BF)
    gatt_ref[...]=gatt
    pr=-(gatt.astype(F32)*att.astype(F32))
    hi,mid,lo=split3(pr)
    hrow=lax.broadcasted_iota(jnp.int32,(D,128),0)//64
    hcol=lax.broadcasted_iota(jnp.int32,(D,128),1)
    ind=((hcol>=3*hrow)&(hcol<3*hrow+3)).astype(BF)
    dl=mm(hi.astype(BF),ind,NN)+mm(mid.astype(BF),ind,NN)
    h2,m2,l2=split3(dl)
    ln=lanes(dl.shape)%3
    auxd_ref[...]=jnp.where(ln==0,h2,jnp.where(ln==1,m2,l2)).astype(BF)
    @pl.when(i==nb-1)
    def _():
        def send(src,at,n):
            cps=[pltpu.make_async_copy(src.at[rows_at(me,t,n),:],(mine_ref if t<4 else theirs_ref).at[t%4,pl.ds(at,n),:],sems.at[3]) for t in range(8)]
            for c in cps: c.start()
            return cps
        wo[...]=awo[...].astype(BF)
        out=send(wo,0,ro)
        wd[...]=awd[...].astype(BF)
        out+=send(wd,ro,rd)
        wu[...]=awu[...].astype(BF)
        for b in range(FF//D): out+=send(wu.at[:,pl.ds(b*D,D)],ro+rd+b*ro,ro)
        for c in out: c.wait()
def middle(me,info,mixed,cot,atts,vec,upb,pieces):
    nblk=8; L,D=mixed.shape; FF=upb.shape[1]; ro=D//8; rd=FF//8
    nb=L//RB; na=len(atts)
    flat_pieces=jax.tree.leaves(pieces)
    def kern(me_ref,info_ref,mix_ref,cot_ref,*rest):
        att=rest[:na]; rest=rest[na:]
        given=iter(rest[2:2+len(flat_pieces)])
        blocks=[(next(given),next(given)) if isinstance(p,tuple) else next(given) for p in pieces]
        mid_kernel(nblk,me_ref,info_ref,mix_ref,cot_ref,att,rest[0],rest[1],blocks,*rest[2+len(flat_pieces):])
    full=lambda a: pl.BlockSpec(a.shape,lambda i:(0,)*a.ndim)
    blk=pl.BlockSpec((1,RB,D),lambda i:(i,0,0)); row=pl.BlockSpec((RB,D),lambda i:(i,0))
    outs=[sds((nb,RB,D),BF),sds((L,D),F32),sds((L,D),BF),sds((L,128),BF)]+[sds((4,)+pieces[0].shape,BF)]*2+[sds((16,D),F32),sds((1,FF),F32)]
    return pl.pallas_call(kern,grid=(nb,),
      in_specs=[smem(),smem(),row,blk]+[pl.BlockSpec((RB,a.shape[1]),lambda i:(i,0)) for a in atts]+[full(vec),full(upb)]+[anyw()]*len(flat_pieces),
      out_specs=[blk,row,row,pl.BlockSpec((RB,128),lambda i:(i,0)),anyw(),anyw()]+[once(s) for s in outs[6:]],
      out_shape=outs,
      scratch_shapes=[pltpu.VMEM((D,D),BF),pltpu.VMEM((FF,D),BF),pltpu.VMEM((D,FF),BF),
        pltpu.VMEM((D,D),F32),pltpu.VMEM((FF,D),F32),pltpu.VMEM((D,FF),F32),
        pltpu.VMEM((RB,FF),BF),pltpu.VMEM((RB,FF),F32),pltpu.SemaphoreType.DMA((4,))],
      compiler_params=pltpu.CompilerParams(vmem_limit_bytes=61*2**20),
      cost_estimate=pl.CostEstimate(flops=2*L*D*(3*D+6*FF),bytes_accessed=60_000_000,transcendentals=2*L*FF),
      name="middle")(me,info,mixed,cot,*atts,vec,upb,*flat_pieces)

GROUPS=8
AXES=("seq","stream")
def flip(x,mask,total):
    return lax.ppermute(x,AXES,[(i,i^mask) for i in range(total)])
def far_first(count):
    bits=[]; bit=count//2
    while bit: bits.append(bit); bit//=2
    return bits
def widen(x,bit,total): return jnp.concatenate([x,flip(x,bit,total)])
def settle(x,inner,count):
    ids=[0]
    for bit in far_first(count): ids=ids+[i^bit for i in ids]
    return in_order(jnp.stack([x[ids.index(k)] for k in range(count)]),inner)
def in_order(x,index):
    n=x.shape[0]; bit=1
    while bit<n:
        turned=jnp.concatenate([x[k^bit][None] for k in range(n)])
        x=jnp.where((index&bit)!=0,turned,x); bit*=2
    return x
def after(x,*deps):
    return lax.optimization_barrier((x,)+deps)[0]
def sync(*xs): return lax.optimization_barrier(xs)
def spread_start(own,unit,total):
    across=lambda x,g: flip(x,g*unit,total)
    return [own,across(own,2),across(own,4)]
def split_send(x,bit,total):
    send=jnp.stack([x[j] for j in range(1,x.shape[0],2)]).astype(BF)
    return jnp.stack([x[j] for j in range(0,x.shape[0],2)]),flip(send,bit,total)
def finish2(keep,got,total):
    bit=2
    while keep.shape[0]>1:
        keep,got=split_send(keep+got.astype(F32),bit,total); bit*=2
    return keep[0],got[0]
def on_device(tokens,source_len,target_len,timesteps,cotangent,query_weight,query_bias,key_weight,value_weight,value_bias,
        out_weight,out_bias,attn_gain,attn_shift,up_weight,up_bias,down_weight,down_bias,ffn_gain,ffn_shift,
        stamp_weight,stamp_bias,embed_weight,embed_bias):
    seqs,R,D=tokens.shape
    streams=lax.axis_size("stream"); seq_size=lax.axis_size("seq"); total=seq_size*streams
    s0=lax.axis_index("stream"); flat=lax.axis_index("seq")*streams+s0
    unit=total//GROUPS
    inner=flat%unit; group=flat//unit
    me=group.astype(jnp.int32).reshape(1)
    n=D//GROUPS; shard=D//total; stamp_rows=stamp_weight.shape[0]; FF=up_weight.shape[1]; ff_shard=FF//total
    vecs=(query_bias,value_bias,out_bias,attn_gain,attn_shift,down_bias,ffn_gain,ffn_shift,stamp_bias,embed_bias,up_bias)
    first,second=pack((query_weight,key_weight,value_weight,embed_weight,stamp_weight,out_weight,down_weight,up_weight),vecs)
    def rowwise(x,sizes):
        at=0; out=[]
        for count,size in sizes:
            part=x[:,at:at+count*size].reshape(unit,count,size,x.shape[2])
            out.append(part.transpose(1,0,2,3).reshape(count*unit*size,x.shape[2])); at+=count*size
        return jnp.concatenate(out) if len(out)>1 else out[0]
    def exchange(chunks):
        return [x if c==0 else flip(x,c,total) for c,x in enumerate(chunks)]
    def chunks_of(x): return [lax.dynamic_index_in_dim(x,s0^c,0,keepdims=False) for c in range(streams)]
    order=jnp.asarray(ORDER,jnp.int32)
    source=source_len[s0]; target=target_len[s0]; stamp=timesteps[s0]
    half=R*streams//2
    place=(s0^jnp.arange(streams))*R
    flag=(place>=half).astype(jnp.int32)
    nlive=jnp.clip(jnp.where(flag==1,target-(place-half),source-place),0,R).astype(jnp.int32)
    info=jnp.stack([flag,nlive],1)
    tdim=stamp_rows*total; halfway=tdim//2
    t_ids=(((order^group)[:,None,None]*unit+jnp.arange(unit)[None,:,None])*stamp_rows+jnp.arange(SMALL)[None,None,:])
    valid=(jnp.arange(SMALL)<stamp_rows)[None,None,:]
    t_ids=jnp.where(valid,t_ids,0).reshape(-1)
    rates=jnp.exp(-math.log(10000.0)*(t_ids%halfway).astype(F32)/halfway)
    angle=stamp.astype(F32)*rates
    feats=jnp.where(t_ids<halfway,jnp.sin(angle),jnp.cos(angle))
    feats=jnp.where(jnp.broadcast_to(valid,(GROUPS,unit,SMALL)).reshape(-1),feats,0.0)
    feat=jnp.broadcast_to(feats.astype(BF)[None],(8,feats.shape[0]))
    bits=far_first(unit)
    first=widen(first[None],bits[0],total)
    first,second=sync(first,second)
    second=widen(second[None],bits[0],total)
    for bit in bits[1:]: first=widen(first,bit,total)
    first=rowwise(settle(first,inner,unit),((4,shard),(1,SMALL)))
    cells=chunks_of(tokens)
    first,second,feat,info,*cells=sync(first,second,feat,info,*cells)
    for bit in bits[1:]: second=widen(second,bit,total)
    n1=[first]+[flip(first,g*unit,total) for g in (2,4,6)]
    toks=[cells[0]]+[None]*(streams-1)
    early,late=list(range(2,streams)),[1]
    for c in early: toks[c]=flip(cells[c],c,total)
    n1[1],n1[2],toks[2],second=sync(n1[1],n1[2],toks[2],second)
    second=rowwise(settle(second,inner,unit),((1,shard),(1,ff_shard),(FF//D,shard)))
    for c in late: toks[c]=flip(after(cells[c],second),c,total)
    n2=spread_start(second,unit,total)
    p1=n1+[flip(x,unit,total) for x in n1]
    *cells,_=sync(*chunks_of(cotangent),toks)
    far=[flip(n2[0],unit,total)]
    cots=[cells[0]]+[flip(cells[c],c,total) for c in range(1,streams-1)]
    mixed,inputs,q,k,v,auxk,pre,hid,vec,upb=project(me,info,feat,toks,p1,unit,FF)
    pairs=D//(2*HEAD); parts=(2,pairs-2)
    atts=[];auxq=[]
    def forward(c,q):
        a,x=attn_fwd(q,k,v,auxk,sum(parts[:c]),parts[c]); atts.append(a); auxq.append(x)
    forward(0,q)
    q,n2,far,cots,cells,atts=sync(q,n2,far,cots,cells,atts)
    cut=n+FF//GROUPS
    low=flip(n2[2][:cut],2*unit,total); high=flip(n2[1][cut:],4*unit,total)
    cots.append(flip(cells[streams-1],streams-1,total))
    far+=[flip(n2[1],unit,total),flip(n2[2],unit,total)]
    forward(1,q)
    low,high,far,atts,cots=sync(low,high,far,atts,cots)
    diag=(low,high)
    p2=n2+[diag]+far+[tuple(flip(x,unit,total) for x in diag)]
    cot=jnp.stack(cots)
    output,ga,gatt,auxd,mine2,theirs2,dvec,dupb=sync(*middle(me,info,mixed,cot,atts,vec,upb,p2))
    grads=[]
    per=pairs//3
    def backward(c,q):
        grads.append(attn_bwd(q,k,v,gatt,auxk,auxq[min(c,1)],auxd,c*per,per,c*per-sum(parts[:min(c,1)])))
    got=flip(theirs2,unit,total)
    backs=[output[0],flip(output[1],1,total)]
    backward(0,q)
    got,q,output,backs,grads=sync(got,q,output,backs,grads)
    low,high=sum_diag(mine2,got,cut)
    low=flip(low,2*unit,total); high=flip(high,4*unit,total)
    backs.append(flip(output[2],2,total))
    backward(1,q)
    held=backs.pop()
    low,high,q,output,backs,grads=sync(low,high,q,output,backs,grads)
    fx,fy,held=sync(*sum_near(mine2,got,low,high),held)
    backs.append(held)
    fx=flip(fx,2*unit,total); fy=flip(fy,4*unit,total)
    backs.append(flip(output[3],3,total))
    backward(2,q)
    backs,grads=sync(backs,grads)
    def place(chunks,dtype):
        out=jnp.zeros((seqs,R,D),dtype)
        for c,part in enumerate(chunks):
            out=lax.dynamic_update_index_in_dim(out,part.astype(dtype),s0^c,0)
        return out
    tg,rows4=token_grads(me,info,ga,pre,grads,p1,R)
    tg,rows4,fx,fy=sync(tg,rows4,fx,fy)
    keep2,got2=sum_own(inner,mine2,got,(fx,fy),((1,shard),(1,ff_shard),(FF//D,shard)),unit,total)
    tgs=[tg[0],None,flip(tg[2],2,total)]
    rows4,keep2,tg=sync(rows4,keep2,tg)
    mine1,theirs1=weight_grads(me,inputs,rows4,hid,feat,dvec,dupb,grads,unit,R)
    mine1,theirs1,got2,tg,tgs=sync(mine1,theirs1,got2,tg,tgs)
    got1=flip(theirs1,unit,total)
    tgs[1]=flip(tg[1],1,total)
    blocks=sum_three(mine1,got1)
    blocks,tgs,tg,keep2,got2=sync(blocks,tgs,tg,keep2,got2)
    fx,fy,fd=(flip(x,g*unit,total) for x,g in zip(blocks,(2,4,6)))
    tgs.append(flip(tg[3],3,total))
    keep2,got2=finish2(keep2,got2,total)
    fx,fy,fd,keep2,got2,tgs,backs=sync(fx,fy,fd,keep2,got2,tgs,backs)
    output=place(backs,BF)
    dwo,dwd,dwu=last2(keep2,got2,shard,ff_shard,FF)
    keep1,got1=finish2(*sum_own(inner,mine1,got1,(fx,fy,fd),((4,shard),(1,SMALL)),unit,total),total)
    dwq,dwk,dwv,dwe,dws,bq,bv,bo,ag,as_,bd,fg,fs,bs,be,bu=last1(keep1,got1,shard,stamp_rows,[shard]*10+[ff_shard])
    token_grad=place(tgs,F32)
    return (output,token_grad,dwq,bq,dwk,dwv,bv,dwo,bo,ag,as_,dwu,bu,dwd,bd,fg,fs,dws,bs,dwe,be)

def solution(mesh):
    cells=P("seq","stream",None); per=P("seq"); mat=P(("seq","stream"),None); row=P(("seq","stream"))
    return jax.shard_map(on_device,mesh=mesh,
        in_specs=(cells,per,per,per,cells,mat,row,mat,mat,row,mat,row,row,row,mat,row,mat,row,row,row,mat,row,mat,row),
        out_specs=(cells,cells,mat,row,mat,mat,row,mat,row,row,row,mat,row,mat,row,row,row,mat,row,mat,row),
        check_vma=False)
```

profile of v0, /device:TPU:0, one launch (start us, length us, event | category | flops | bytes accessed | tf_op | source)
XLA Modules:
  0.0 379.1 jit_solution(1329261755104303400)
XLA Ops:
  0.7 2.1 pack.1
  2.8 4.0 %collective-permute-start = (bf16[1,112,768]{2,1,0:T(8,128)(2,1)}, bf16[1,112,768]{2,1,0:T(8,128)(2,1)S(1)}, u32[]{:S(2)}, u32[]{:S(2)}) collective-permute-start(bf16[1,112,768]{2,1,0:T(8,128)(2,1)} %bitcast.93), channel_id=1, source_target_pairs={{0,2},{1,3},{2,0},{3,1},{4,6},{5,7},{6,4},{7,5},{8,10},{9,11},{10,... | collective-permute-start | bytes 516104 | tf_op jit(solution)/shard_map/ppermute | solution.py:513
  13.7 2.3 dynamic-slice_bitcast_fusion.4
  16.7 3.2 collective-permute-start.1
  20.0 13.4 %collective-permute-done.2 = bf16[1,216,768]{2,1,0:T(8,128)(2,1)S(1)} collective-permute-done((bf16[1,216,768]{2,1,0:T(8,128)(2,1)S(1)}, bf16[1,216,768]{2,1,0:T(8,128)(2,1)S(1)}, u32[]{:S(2)}, u32[]{:S(2)}) %collective-permute-start.2) | collective-permute-done | bytes 331808 | tf_op jit(solution)/shard_map/ppermute | solution.py:513
  36.7 1.5 collective-permute-start.4
  38.2 3.6 collective-permute-start.5
  42.3 16.6 %collective-permute-done.6 = bf16[2,216,768]{2,1,0:T(8,128)(2,1)S(1)} collective-permute-done((bf16[2,216,768]{2,1,0:T(8,128)(2,1)S(1)}, bf16[2,216,768]{2,1,0:T(8,128)(2,1)S(1)}, u32[]{:S(2)}, u32[]{:S(2)}) %collective-permute-start.6) | collective-permute-done | bytes 663584 | tf_op jit(solution)/shard_map/ppermute | solution.py:513
  59.1 3.1 collective-permute-start.8
  62.1 4.8 %collective-permute-done.4.rest_6_.rest_5_ = bf16[448,768]{1,0:T(8,128)(2,1)S(1)} collective-permute-done((bf16[448,768]{1,0:T(8,128)(2,1)S(1)}, bf16[448,768]{1,0:T(8,128)(2,1)S(1)}, u32[]{:S(2)}, u32[]{:S(2)}) %collective-permute-start.4) | collective-permute-done | bytes 688160 | tf_op jit(solution)/shard_map/ppermute | solution.py:513
  68.8 1.8 collective-permute-start.7
  70.7 2.0 collective-permute-done.8.rest_3_
  72.6 1.5 collective-permute-start.14
  74.2 1.5 collective-permute-start.15
  75.7 5.4 %collective-permute-done.7.rest_1_ = bf16[256,768]{1,0:T(8,128)(2,1)} collective-permute-done((bf16[256,768]{1,0:T(8,128)(2,1)S(1)}, bf16[256,768]{1,0:T(8,128)(2,1)}, u32[]{:S(2)}, u32[]{:S(2)}) %collective-permute-start.7) | collective-permute-done | bytes 393248 | tf_op jit(solution)/shard_map/ppermute | solution.py:513
  83.2 2.8 collective-permute-start.17
  86.1 2.2 collective-permute-start.18
  88.2 9.6 %project.1 = (f32[1024,768]{1,0:T(8,128)}, bf16[1024,768]{1,0:T(8,128)(2,1)}, bf16[1024,768]{1,0:T(8,128)(2,1)}, bf16[1024,768]{1,0:T(8,128)(2,1)}, bf16[1024,76...) custom-call(s32[1]{0:T(128)} %bitcast.me_ref, ...), custom_call_target="tpu_custom_call" | custom-call | flops 3623878656 | bytes 20000000 | tf_op jit(solution)/shard_map/project/pallas_call | solution.py:200
  97.8 8.7 %attn_fwd.2 = (bf16[1024,256]{1,0:T(8,128)(2,1)}, bf16[2,1024,128]{2,1,0:T(8,128)(2,1)}) custom-call(bf16[1024,768]{1,0:T(8,128)(2,1)} %get-tuple-element.257.q_ref, bf16[1024,768]{1,0:T(8,128)(2,1)} %get-tuple-element.202.k_ref, bf16[1024,768]{1,0:T(8,128)(2,1)} %get-tuple-element.203.v_ref, bf16[1024,128]{1,0:T(8,128)(2,1)} %get-tuple-element.204.auxk_ref), custom_call_target="tpu_custom_call" | custom-call | flops 1073741824 | bytes 2621440 | tf_op jit(solution)/shard_map/attn_fwd/pallas_call | solution.py:51
  110.1 2.7 collective-permute-start.23
  112.8 15.1 %attn_fwd.3 = (bf16[1024,512]{1,0:T(8,128)(2,1)}, bf16[4,1024,128]{2,1,0:T(8,128)(2,1)}) custom-call(bf16[1024,768]{1,0:T(8,128)(2,1)} %get-tuple-element.257.q_ref, bf16[1024,768]{1,0:T(8,128)(2,1)} %get-tuple-element.202.k_ref, bf16[1024,768]{1,0:T(8,128)(2,1)} %get-tuple-element.203.v_ref, bf16[1024,128]{1,0:T(8,128)(2,1)} %get-tuple-element.204.auxk_ref), custom_call_target="tpu_custom_call" | custom-call | flops 2147483648 | bytes 5242880 | tf_op jit(solution)/shard_map/attn_fwd/pallas_call | solution.py:51
  128.6 2.4 pad_maximum_fusion.cot_ref
  132.5 54.5 %middle.1 = (bf16[4,256,768]{2,1,0:T(8,128)(2,1)}, f32[1024,768]{1,0:T(8,128)}, bf16[1024,768]{1,0:T(8,128)(2,1)}, bf16[1024,128]{1,0:T(8,128)(2,1)}, bf16[4,864...) custom-call(s32[1]{0:T(128)} %bitcast.me_ref, ...), custom_call_target="tpu_custom_call" | custom-call | flops 32614907904 | bytes 60000000 | tf_op jit(solution)/shard_map/middle/pallas_call | solution.py:499
  188.3 3.9 %collective-permute-start.27 = (bf16[256,768]{1,0:T(8,128)(2,1)S(1)}, bf16[256,768]{1,0:T(8,128)(2,1)S(1)}, u32[]{:S(2)}, u32[]{:S(2)}) collective-permute-start(bf16[256,768]{1,0:T(8,128)(2,1)S(1)} %get-tuple-element.337), channel_id=1, source_target_pairs={{0,1},{1,0},{2,3},{3,2},{4,5},{5,4},{6,7},{7,6},{8,9},{9,8},{10,11... | collective-permute-start | bytes 1179656 | tf_op jit(solution)/shard_map/ppermute | solution.py:513
  192.2 14.6 %attn_bwd.3.rest_0_ = bf16[3,1024,256]{2,1,0:T(8,128)(2,1)} custom-call(bf16[1024,768]{1,0:T(8,128)(2,1)} %get-tuple-element.257.q_ref, bf16[1024,768]{1,0:T(8,128)(2,1)} %get-tuple-element.202.k_ref, bf16[1024,768]{1,0:T(8,128)(2,1)} %get-tuple-element.203.v_ref, bf16[1024,768]{1,0:T(8,128)(2,1)} %get-tuple-element.235.do_ref, ...), custom_call_target="tpu_custom_call" | custom-call | flops 2684354560 | bytes 4718592 | tf_op jit(solution)/shard_map/attn_bwd/pallas_call | solution.py:96
  207.6 2.8 sum_diag.1
  214.7 14.6 %attn_bwd.4.rest_1_ = bf16[3,1024,256]{2,1,0:T(8,128)(2,1)} custom-call(bf16[1024,768]{1,0:T(8,128)(2,1)} %get-tuple-element.257.q_ref, bf16[1024,768]{1,0:T(8,128)(2,1)} %get-tuple-element.202.k_ref, bf16[1024,768]{1,0:T(8,128)(2,1)} %get-tuple-element.203.v_ref, bf16[1024,768]{1,0:T(8,128)(2,1)} %get-tuple-element.235.do_ref, ...), custom_call_target="tpu_custom_call" | custom-call | flops 2684354560 | bytes 4718592 | tf_op jit(solution)/shard_map/attn_bwd/pallas_call | solution.py:96
  231.0 4.2 %sum_near.1 = (bf16[864,768]{1,0:T(8,128)(2,1)}, bf16[864,768]{1,0:T(8,128)(2,1)}) custom-call(bf16[4,864,768]{2,1,0:T(8,128)(2,1)} %get-tuple-element.232.a.a1.a2, bf16[4,864,768]{2,1,0:T(8,128)(2,1)} %collective-permute-done.26.b.b1.b2, bf16[4,864,768]{2,1,0:T(8,128)(2,1)} %get-tuple-element.232.a.a1.a2, ...), custom_call_target="tpu_custom_call" | custom-call | tf_op jit(solution)/shard_map/sum_near/pallas_call | solution.py:323
  237.0 2.2 collective-permute-start.31
  239.2 14.8 %attn_bwd.5.rest_2_ = bf16[3,1024,256]{2,1,0:T(8,128)(2,1)} custom-call(bf16[1024,768]{1,0:T(8,128)(2,1)} %get-tuple-element.257.q_ref, bf16[1024,768]{1,0:T(8,128)(2,1)} %get-tuple-element.202.k_ref, bf16[1024,768]{1,0:T(8,128)(2,1)} %get-tuple-element.203.v_ref, bf16[1024,768]{1,0:T(8,128)(2,1)} %get-tuple-element.235.do_ref, ...), custom_call_target="tpu_custom_call" | custom-call | flops 2684354560 | bytes 4718592 | tf_op jit(solution)/shard_map/attn_bwd/pallas_call | solution.py:96
  254.1 12.0 %token_grads.1 = (bf16[4,256,768]{2,1,0:T(8,128)(2,1)}, f32[8,768]{1,0:T(8,128)}) custom-call(s32[1]{0:T(128)} %bitcast.me_ref, s32[4,2]{1,0:T(4,128)} %pad_add_fusion.info_ref, f32[1024,768]{1,0:T(8,128)} %get-tuple-element.230.ga_ref, f32[8,768]{1,0:T(8,128)} %get-tuple-element.231.pre_ref, bf16[3,1024,256]{2,1,0:T(8,128)(2,1)} %attn_bwd.3.rest_0_, ...), custom_call_target="tpu_custom_call" | custom-call | flops 3623878656 | bytes 15000000 | tf_op jit(solution)/shard_map/token_grads/pallas_call | solution.py:247
  267.2 4.2 %sum_own.2 = (f32[2,216,768]{2,1,0:T(8,128)}, bf16[2,216,768]{2,1,0:T(8,128)(2,1)}) custom-call(s32[1]{0:T(128)} %bitcast.31.inner_ref, bf16[4,864,768]{2,1,0:T(8,128)(2,1)} %get-tuple-element.232.a.a1.a2, bf16[4,864,768]{2,1,0:T(8,128)(2,1)} %collective-permute-done.26.b.b1.b2, bf16[864,768]{1,0:T(8,128)(2,1)} %copy-done.6, ...), custom_call_target="tpu_custom_call" | custom-call | tf_op jit(solution)/shard_map/sum_own/pallas_call | solution.py:352
  271.4 3.1 collective-permute-start.34
  275.3 13.0 %weight_grads.1 = (bf16[4,448,768]{2,1,0:T(8,128)(2,1)}, bf16[4,448,768]{2,1,0:T(8,128)(2,1)}) custom-call(s32[1]{0:T(128)} %bitcast.me_ref, bf16[1024,768]{1,0:T(8,128)(2,1)} %get-tuple-element.195.inp_ref, f32[8,768]{1,0:T(8,128)} %get-tuple-element.270.rows_ref, bf16[8,768]{1,0:T(8,128)(2,1)} %get-tuple-element.271.hid_ref, ...), custom_call_target="tpu_custom_call" | custom-call | flops 3623878656 | bytes 12000000 | tf_op jit(solution)/shard_map/weight_grads/pallas_call | solution.py:295
  288.3 8.6 %collective-permute-done.35 = bf16[256,768]{1,0:T(8,128)(2,1)S(1)} collective-permute-done((bf16[256,768]{1,0:T(8,128)(2,1)S(1)}, bf16[256,768]{1,0:T(8,128)(2,1)S(1)}, u32[]{:S(2)}, u32[]{:S(2)}) %collective-permute-start.35) | collective-permute-done | bytes 393248 | tf_op jit(solution)/shard_map/ppermute | solution.py:513
  300.3 3.5 collective-permute-done.36.b1.b2.b3.b
  303.8 1.5 copy-done
  305.3 3.2 sum_three.1
  308.6 2.7 collective-permute-done.37
  315.8 2.5 collective-permute-start.42
  318.2 1.6 convert_add_fusion
  321.1 28.2 %collective-permute-done.41 = bf16[1,216,768]{2,1,0:T(8,128)(2,1)S(1)} collective-permute-done((bf16[1,216,768]{2,1,0:T(8,128)(2,1)S(1)}, bf16[1,216,768]{2,1,0:T(8,128)(2,1)S(1)}, u32[]{:S(2)}, u32[]{:S(2)}) %collective-permute-start.41) | collective-permute-done | bytes 331808 | tf_op jit(solution)/shard_map/ppermute | solution.py:513
  351.1 3.1 sum_own.3
  359.2 1.8 bitcast_dynamic-update-slice_fusion.1
  361.8 2.0 last_ffn.1
  366.3 2.6 collective-permute-start.44
  369.6 6.7 %collective-permute-done.44 = bf16[1,112,768]{2,1,0:T(8,128)(2,1)S(1)} collective-permute-done((bf16[1,112,768]{2,1,0:T(8,128)(2,1)S(1)}, bf16[1,112,768]{2,1,0:T(8,128)(2,1)S(1)}, u32[]{:S(2)}, u32[]{:S(2)}) %collective-permute-start.44) | collective-permute-done | bytes 172064 | tf_op jit(solution)/shard_map/ppermute | solution.py:513
  377.0 1.8 last_attn.1
  (201 shorter events, 52.6 us)
Async XLA Ops:
  2.8 13.1 %collective-permute-start = (bf16[1,112,768]{2,1,0:T(8,128)(2,1)}, bf16[1,112,768]{2,1,0:T(8,128)(2,1)S(1)}, u32[]{:S(2)}, u32[]{:S(2)}) collective-permute-start(bf16[1,112,768]{2,1,0:T(8,128)(2,1)} %bitcast.93), channel_id=1, source_target_pairs={{0,2},{1,3},{2,0},{3,1},{4,6},{5,7},{6,4},{7,5},{8,10},{9,11},{10,... | collective-permute-start | bytes 516104 | tf_op jit(solution)/shard_map/ppermute | solution.py:513
  16.0 17.4 %collective-permute-start.2 = (bf16[1,216,768]{2,1,0:T(8,128)(2,1)S(1)}, bf16[1,216,768]{2,1,0:T(8,128)(2,1)S(1)}, u32[]{:S(2)}, u32[]{:S(2)}) collective-permute-start(bf16[1,216,768]{2,1,0:T(8,128)(2,1)S(1)} %bitcast.90), channel_id=1, source_target_pairs={{0,2},{1,3},{2,0},{3,1},{4,6},{5,7},{6,4},{7,5},{8,10},{9,11},{10,... | collective-permute-start | bytes 995336 | tf_op jit(solution)/shard_map/ppermute | solution.py:513
  16.7 17.2 %collective-permute-start.1 = (bf16[2,112,768]{2,1,0:T(8,128)(2,1)S(1)}, bf16[2,112,768]{2,1,0:T(8,128)(2,1)S(1)}, u32[]{:S(2)}, u32[]{:S(2)}) collective-permute-start(bf16[2,112,768]{2,1,0:T(8,128)(2,1)S(1)} %pad_maximum_fusion.5), channel_id=1, source_target_pairs={{0,1},{1,0},{2,3},{3,2},{4,5},{5,4},{6,7},{7,6},{8,9},{9,8},{10,11... | collective-permute-start | bytes 1032200 | tf_op jit(solution)/shard_map/ppermute | solution.py:513
  34.5 32.5 %copy-start.9 = (bf16[448,768]{1,0:T(8,128)(2,1)}, bf16[448,768]{1,0:T(8,128)(2,1)S(1)}, u32[]{:S(2)}) copy-start(bf16[448,768]{1,0:T(8,128)(2,1)S(1)} %pad_maximum_fusion.3.rest_4_.rest_3_) | copy-start | bytes 2064388
  35.2 23.7 %collective-permute-start.6 = (bf16[2,216,768]{2,1,0:T(8,128)(2,1)S(1)}, bf16[2,216,768]{2,1,0:T(8,128)(2,1)S(1)}, u32[]{:S(2)}, u32[]{:S(2)}) collective-permute-start(bf16[2,216,768]{2,1,0:T(8,128)(2,1)S(1)} %pad_maximum_fusion.4), channel_id=1, source_target_pairs={{0,1},{1,0},{2,3},{3,2},{4,5},{5,4},{6,7},{7,6},{8,9},{9,8},{10,11... | collective-permute-start | bytes 1990664 | tf_op jit(solution)/shard_map/ppermute | solution.py:513
  35.2 26.9 %collective-permute-start.3 = (bf16[448,768]{1,0:T(8,128)(2,1)S(1)}, bf16[448,768]{1,0:T(8,128)(2,1)S(1)}, u32[]{:S(2)}, u32[]{:S(2)}) collective-permute-start(bf16[448,768]{1,0:T(8,128)(2,1)S(1)} %pad_maximum_fusion.3.rest_4_.rest_3_), channel_id=1, source_target_pairs={{0,8},{1,9},{2,10},{3,11},{4,12},{5,13},{6,14},{7,15},{8,0},{9,1},... | collective-permute-start | bytes 2064392 | tf_op jit(solution)/shard_map/ppermute | solution.py:513
  36.7 30.3 %collective-permute-start.4 = (bf16[448,768]{1,0:T(8,128)(2,1)S(1)}, bf16[448,768]{1,0:T(8,128)(2,1)S(1)}, u32[]{:S(2)}, u32[]{:S(2)}) collective-permute-start(bf16[448,768]{1,0:T(8,128)(2,1)S(1)} %pad_maximum_fusion.3.rest_4_.rest_3_), channel_id=1, source_target_pairs={{0,16},{1,17},{2,18},{3,19},{4,20},{5,21},{6,22},{7,23},{8,24},{9,... | collective-permute-start | bytes 2064392 | tf_op jit(solution)/shard_map/ppermute | solution.py:513
  38.2 20.8 %collective-permute-start.5 = (bf16[256,768]{1,0:T(8,128)(2,1)S(1)}, bf16[256,768]{1,0:T(8,128)(2,1)S(1)}, u32[]{:S(2)}, u32[]{:S(2)}) collective-permute-start(bf16[256,768]{1,0:T(8,128)(2,1)S(1)} %get-tuple-element.187), channel_id=1, source_target_pairs={{0,2},{1,3},{2,0},{3,1},{4,6},{5,7},{6,4},{7,5},{8,10},{9,11},{10,... | collective-permute-start | bytes 1179656 | tf_op jit(solution)/shard_map/ppermute | solution.py:513
  41.8 32.3 %collective-permute-start.9 = (bf16[448,768]{1,0:T(8,128)(2,1)S(1)}, bf16[448,768]{1,0:T(8,128)(2,1)S(1)}, u32[]{:S(2)}, u32[]{:S(2)}) collective-permute-start(bf16[448,768]{1,0:T(8,128)(2,1)S(1)} %pad_maximum_fusion.3.rest_4_.rest_3_), channel_id=1, source_target_pairs={{0,24},{1,25},{2,26},{3,27},{4,28},{5,29},{6,30},{7,31},{8,16},{9,... | collective-permute-start | bytes 2064392 | tf_op jit(solution)/shard_map/ppermute | solution.py:513
  58.9 16.8 %collective-permute-start.10 = (bf16[448,768]{1,0:T(8,128)(2,1)S(1)}, bf16[448,768]{1,0:T(8,128)(2,1)S(1)}, u32[]{:S(2)}, u32[]{:S(2)}) collective-permute-start(bf16[448,768]{1,0:T(8,128)(2,1)S(1)} %pad_maximum_fusion.3.rest_4_.rest_3_), channel_id=1, source_target_pairs={{0,4},{1,5},{2,6},{3,7},{4,0},{5,1},{6,2},{7,3},{8,12},{9,13},{10,... | collective-permute-start | bytes 2064392 | tf_op jit(solution)/shard_map/ppermute | solution.py:513
  59.1 13.6 %collective-permute-start.8 = (bf16[256,768]{1,0:T(8,128)(2,1)S(1)}, bf16[256,768]{1,0:T(8,128)(2,1)S(1)}, u32[]{:S(2)}, u32[]{:S(2)}) collective-permute-start(bf16[256,768]{1,0:T(8,128)(2,1)S(1)} %get-tuple-element.192), channel_id=1, source_target_pairs={{0,3},{1,2},{2,1},{3,0},{4,7},{5,6},{6,5},{7,4},{8,11},{9,10},{10,... | collective-permute-start | bytes 1179656 | tf_op jit(solution)/shard_map/ppermute | solution.py:513
  67.5 13.6 %collective-permute-start.11 = (bf16[448,768]{1,0:T(8,128)(2,1)S(1)}, bf16[448,768]{1,0:T(8,128)(2,1)S(1)}, u32[]{:S(2)}, u32[]{:S(2)}) collective-permute-start(bf16[448,768]{1,0:T(8,128)(2,1)S(1)} %collective-permute-done.3.rest_5_.rest_4_), channel_id=1, source_target_pairs={{0,4},{1,5},{2,6},{3,7},{4,0},{5,1},{6,2},{7,3},{8,12},{9,13},{10,... | collective-permute-start | bytes 2064392 | tf_op jit(solution)/shard_map/ppermute | solution.py:513
  68.8 12.2 %collective-permute-start.7 = (bf16[256,768]{1,0:T(8,128)(2,1)S(1)}, bf16[256,768]{1,0:T(8,128)(2,1)}, u32[]{:S(2)}, u32[]{:S(2)}) collective-permute-start(bf16[256,768]{1,0:T(8,128)(2,1)S(1)} %get-tuple-element.190), channel_id=1, source_target_pairs={{0,1},{1,0},{2,3},{3,2},{4,5},{5,4},{6,7},{7,6},{8,9},{9,8},{10,11... | collective-permute-start | bytes 1179656 | tf_op jit(solution)/shard_map/ppermute | solution.py:513
  72.6 34.0 %collective-permute-start.14 = (bf16[864,768]{1,0:T(8,128)(2,1)S(1)}, bf16[864,768]{1,0:T(8,128)(2,1)}, u32[]{:S(2)}, u32[]{:S(2)}) collective-permute-start(bf16[864,768]{1,0:T(8,128)(2,1)S(1)} %pad_maximum_fusion.2.rest_4_), channel_id=1, source_target_pairs={{0,8},{1,9},{2,10},{3,11},{4,12},{5,13},{6,14},{7,15},{8,0},{9,1},... | collective-permute-start | bytes 3981320 | tf_op jit(solution)/shard_map/ppermute | solution.py:513
  74.2 32.4 %collective-permute-start.15 = (bf16[864,768]{1,0:T(8,128)(2,1)S(1)}, bf16[864,768]{1,0:T(8,128)(2,1)S(1)}, u32[]{:S(2)}, u32[]{:S(2)}) collective-permute-start(bf16[864,768]{1,0:T(8,128)(2,1)S(1)} %pad_maximum_fusion.2.rest_4_), channel_id=1, source_target_pairs={{0,16},{1,17},{2,18},{3,19},{4,20},{5,21},{6,22},{7,23},{8,24},{9,... | collective-permute-start | bytes 3981320 | tf_op jit(solution)/shard_map/ppermute | solution.py:513
  75.7 30.9 %collective-permute-start.16 = (bf16[864,768]{1,0:T(8,128)(2,1)S(1)}, bf16[864,768]{1,0:T(8,128)(2,1)}, u32[]{:S(2)}, u32[]{:S(2)}) collective-permute-start(bf16[864,768]{1,0:T(8,128)(2,1)S(1)} %pad_maximum_fusion.2.rest_4_), channel_id=1, source_target_pairs={{0,4},{1,5},{2,6},{3,7},{4,0},{5,1},{6,2},{7,3},{8,12},{9,13},{10,... | collective-permute-start | bytes 3981320 | tf_op jit(solution)/shard_map/ppermute | solution.py:513
  81.1 2.1 collective-permute-start.12
  81.2 4.9 %collective-permute-start.13 = (bf16[448,768]{1,0:T(8,128)(2,1)S(1)}, bf16[448,768]{1,0:T(8,128)(2,1)S(1)}, u32[]{:S(2)}, u32[]{:S(2)}) collective-permute-start(bf16[448,768]{1,0:T(8,128)(2,1)S(1)} %collective-permute-done.9.rest_7_.rest_6_), channel_id=1, source_target_pairs={{0,4},{1,5},{2,6},{3,7},{4,0},{5,1},{6,2},{7,3},{8,12},{9,13},{10,... | collective-permute-start | bytes 2064392 | tf_op jit(solution)/shard_map/ppermute | solution.py:513
  83.2 23.3 %collective-permute-start.17 = (bf16[256,768]{1,0:T(8,128)(2,1)}, bf16[256,768]{1,0:T(8,128)(2,1)S(1)}, u32[]{:S(2)}, u32[]{:S(2)}) collective-permute-start(bf16[256,768]{1,0:T(8,128)(2,1)} %get-tuple-element.199), channel_id=1, source_target_pairs={{0,1},{1,0},{2,3},{3,2},{4,5},{5,4},{6,7},{7,6},{8,9},{9,8},{10,11... | collective-permute-start | bytes 1179656 | tf_op jit(solution)/shard_map/ppermute | solution.py:513
  86.1 20.5 %collective-permute-start.18 = (bf16[256,768]{1,0:T(8,128)(2,1)}, bf16[256,768]{1,0:T(8,128)(2,1)S(1)}, u32[]{:S(2)}, u32[]{:S(2)}) collective-permute-start(bf16[256,768]{1,0:T(8,128)(2,1)} %get-tuple-element.200), channel_id=1, source_target_pairs={{0,2},{1,3},{2,0},{3,1},{4,6},{5,7},{6,4},{7,5},{8,10},{9,11},{10,... | collective-permute-start | bytes 1179656 | tf_op jit(solution)/shard_map/ppermute | solution.py:513
  106.6 21.4 %copy-start.16 = (bf16[864,768]{1,0:T(8,128)(2,1)}, bf16[864,768]{1,0:T(8,128)(2,1)S(1)}, u32[]{:S(2)}) copy-start(bf16[864,768]{1,0:T(8,128)(2,1)S(1)} %collective-permute-done.15.rest_6_) | copy-start | bytes 3981316
  106.6 21.4 %collective-permute-start.21 = (bf16[864,768]{1,0:T(8,128)(2,1)}, bf16[864,768]{1,0:T(8,128)(2,1)}, u32[]{:S(2)}, u32[]{:S(2)}) collective-permute-start(bf16[864,768]{1,0:T(8,128)(2,1)} %collective-permute-done.14.rest_5_), channel_id=1, source_target_pairs={{0,4},{1,5},{2,6},{3,7},{4,0},{5,1},{6,2},{7,3},{8,12},{9,13},{10,... | collective-permute-start | bytes 3981320 | tf_op jit(solution)/shard_map/ppermute | solution.py:513
  106.7 21.3 %collective-permute-start.22 = (bf16[864,768]{1,0:T(8,128)(2,1)S(1)}, bf16[864,768]{1,0:T(8,128)(2,1)}, u32[]{:S(2)}, u32[]{:S(2)}) collective-permute-start(bf16[864,768]{1,0:T(8,128)(2,1)S(1)} %collective-permute-done.15.rest_6_), channel_id=1, source_target_pairs={{0,4},{1,5},{2,6},{3,7},{4,0},{5,1},{6,2},{7,3},{8,12},{9,13},{10,... | collective-permute-start | bytes 3981320 | tf_op jit(solution)/shard_map/ppermute | solution.py:513
  107.2 20.8 %collective-permute-start.19 = (bf16[480,768]{1,0:T(8,128)(2,1)S(1)}, bf16[480,768]{1,0:T(8,128)(2,1)}, u32[]{:S(2)}, u32[]{:S(2)}) collective-permute-start(bf16[480,768]{1,0:T(8,128)(2,1)S(1)} %slice.120), channel_id=1, source_target_pairs={{0,8},{1,9},{2,10},{3,11},{4,12},{5,13},{6,14},{7,15},{8,0},{9,1},... | collective-permute-start | bytes 2211848 | tf_op jit(solution)/shard_map/ppermute | solution.py:513
  108.9 19.1 %collective-permute-start.20 = (bf16[384,768]{1,0:T(8,128)(2,1)S(1)}, bf16[384,768]{1,0:T(8,128)(2,1)}, u32[]{:S(2)}, u32[]{:S(2)}) collective-permute-start(bf16[384,768]{1,0:T(8,128)(2,1)S(1)} %slice.121), channel_id=1, source_target_pairs={{0,16},{1,17},{2,18},{3,19},{4,20},{5,21},{6,22},{7,23},{8,24},{9,... | collective-permute-start | bytes 1769480 | tf_op jit(solution)/shard_map/ppermute | solution.py:513
  110.1 17.9 %collective-permute-start.23 = (bf16[256,768]{1,0:T(8,128)(2,1)}, bf16[256,768]{1,0:T(8,128)(2,1)}, u32[]{:S(2)}, u32[]{:S(2)}) collective-permute-start(bf16[256,768]{1,0:T(8,128)(2,1)} %get-tuple-element.215), channel_id=1, source_target_pairs={{0,3},{1,2},{2,1},{3,0},{4,7},{5,6},{6,5},{7,4},{8,11},{9,10},{10,... | collective-permute-start | bytes 1179656 | tf_op jit(solution)/shard_map/ppermute | solution.py:513
  128.0 3.3 collective-permute-start.24
  128.1 3.3 collective-permute-start.25
  186.9 19.9 %collective-permute-start.26 = (bf16[4,864,768]{2,1,0:T(8,128)(2,1)}, bf16[4,864,768]{2,1,0:T(8,128)(2,1)}, u32[]{:S(2)}, u32[]{:S(2)}) collective-permute-start(bf16[4,864,768]{2,1,0:T(8,128)(2,1)} %get-tuple-element.233), channel_id=1, source_target_pairs={{0,4},{1,5},{2,6},{3,7},{4,0},{5,1},{6,2},{7,3},{8,12},{9,13},{10,... | collective-permute-start | bytes 15925256 | tf_op jit(solution)/shard_map/ppermute | solution.py:513
  188.3 18.5 %collective-permute-start.27 = (bf16[256,768]{1,0:T(8,128)(2,1)S(1)}, bf16[256,768]{1,0:T(8,128)(2,1)S(1)}, u32[]{:S(2)}, u32[]{:S(2)}) collective-permute-start(bf16[256,768]{1,0:T(8,128)(2,1)S(1)} %get-tuple-element.337), channel_id=1, source_target_pairs={{0,1},{1,0},{2,3},{3,2},{4,5},{5,4},{6,7},{7,6},{8,9},{9,8},{10,11... | collective-permute-start | bytes 1179656 | tf_op jit(solution)/shard_map/ppermute | solution.py:513
  210.4 18.9 %collective-permute-start.28 = (bf16[480,768]{1,0:T(8,128)(2,1)}, bf16[480,768]{1,0:T(8,128)(2,1)S(1)}, u32[]{:S(2)}, u32[]{:S(2)}) collective-permute-start(bf16[480,768]{1,0:T(8,128)(2,1)} %get-tuple-element.239), channel_id=1, source_target_pairs={{0,8},{1,9},{2,10},{3,11},{4,12},{5,13},{6,14},{7,15},{8,0},{9,1},... | collective-permute-start | bytes 2211848 | tf_op jit(solution)/shard_map/ppermute | solution.py:513
  211.8 17.4 %collective-permute-start.29 = (bf16[384,768]{1,0:T(8,128)(2,1)}, bf16[384,768]{1,0:T(8,128)(2,1)S(1)}, u32[]{:S(2)}, u32[]{:S(2)}) collective-permute-start(bf16[384,768]{1,0:T(8,128)(2,1)} %get-tuple-element.240), channel_id=1, source_target_pairs={{0,16},{1,17},{2,18},{3,19},{4,20},{5,21},{6,22},{7,23},{8,24},{9,... | collective-permute-start | bytes 1769480 | tf_op jit(solution)/shard_map/ppermute | solution.py:513
  213.5 21.7 %collective-permute-start.30 = (bf16[256,768]{1,0:T(8,128)(2,1)}, bf16[256,768]{1,0:T(8,128)(2,1)}, u32[]{:S(2)}, u32[]{:S(2)}) collective-permute-start(bf16[256,768]{1,0:T(8,128)(2,1)} %slice_bitcast_fusion.6), channel_id=1, source_target_pairs={{0,2},{1,3},{2,0},{3,1},{4,6},{5,7},{6,4},{7,5},{8,10},{9,11},{10,... | collective-permute-start | bytes 1179656 | tf_op jit(solution)/shard_map/ppermute | solution.py:513
  235.2 30.9 %collective-permute-start.32 = (bf16[864,768]{1,0:T(8,128)(2,1)}, bf16[864,768]{1,0:T(8,128)(2,1)S(1)}, u32[]{:S(2)}, u32[]{:S(2)}) collective-permute-start(bf16[864,768]{1,0:T(8,128)(2,1)} %get-tuple-element.263), channel_id=1, source_target_pairs={{0,8},{1,9},{2,10},{3,11},{4,12},{5,13},{6,14},{7,15},{8,0},{9,1},... | collective-permute-start | bytes 3981320 | tf_op jit(solution)/shard_map/ppermute | solution.py:513
  235.8 30.6 %collective-permute-start.33 = (bf16[864,768]{1,0:T(8,128)(2,1)}, bf16[864,768]{1,0:T(8,128)(2,1)}, u32[]{:S(2)}, u32[]{:S(2)}) collective-permute-start(bf16[864,768]{1,0:T(8,128)(2,1)} %get-tuple-element.264), channel_id=1, source_target_pairs={{0,16},{1,17},{2,18},{3,19},{4,20},{5,21},{6,22},{7,23},{8,24},{9,... | collective-permute-start | bytes 3981320 | tf_op jit(solution)/shard_map/ppermute | solution.py:513
  237.0 17.0 %collective-permute-start.31 = (bf16[256,768]{1,0:T(8,128)(2,1)S(1)}, bf16[256,768]{1,0:T(8,128)(2,1)S(1)}, u32[]{:S(2)}, u32[]{:S(2)}) collective-permute-start(bf16[256,768]{1,0:T(8,128)(2,1)S(1)} %slice_bitcast_fusion.5), channel_id=1, source_target_pairs={{0,3},{1,2},{2,1},{3,0},{4,7},{5,6},{6,5},{7,4},{8,11},{9,10},{10,... | collective-permute-start | bytes 1179656 | tf_op jit(solution)/shard_map/ppermute | solution.py:513
  271.4 26.3 %collective-permute-start.34 = (bf16[2,216,768]{2,1,0:T(8,128)(2,1)}, bf16[2,216,768]{2,1,0:T(8,128)(2,1)S(1)}, u32[]{:S(2)}, u32[]{:S(2)}) collective-permute-start(bf16[2,216,768]{2,1,0:T(8,128)(2,1)} %get-tuple-element.276), channel_id=1, source_target_pairs={{0,1},{1,0},{2,3},{3,2},{4,5},{5,4},{6,7},{7,6},{8,9},{9,8},{10,11... | collective-permute-start | bytes 1990664 | tf_op jit(solution)/shard_map/ppermute | solution.py:513
  275.3 21.6 %collective-permute-start.35 = (bf16[256,768]{1,0:T(8,128)(2,1)S(1)}, bf16[256,768]{1,0:T(8,128)(2,1)S(1)}, u32[]{:S(2)}, u32[]{:S(2)}) collective-permute-start(bf16[256,768]{1,0:T(8,128)(2,1)S(1)} %get-tuple-element.335), channel_id=1, source_target_pairs={{0,2},{1,3},{2,0},{3,1},{4,6},{5,7},{6,4},{7,5},{8,10},{9,11},{10,... | collective-permute-start | bytes 1179656 | tf_op jit(solution)/shard_map/ppermute | solution.py:513
  298.5 5.3 %collective-permute-start.36 = (bf16[4,448,768]{2,1,0:T(8,128)(2,1)}, bf16[4,448,768]{2,1,0:T(8,128)(2,1)S(1)}, u32[]{:S(2)}, u32[]{:S(2)}) collective-permute-start(bf16[4,448,768]{2,1,0:T(8,128)(2,1)} %get-tuple-element.279), channel_id=1, source_target_pairs={{0,4},{1,5},{2,6},{3,7},{4,0},{5,1},{6,2},{7,3},{8,12},{9,13},{10,... | collective-permute-start | bytes 8257544 | tf_op jit(solution)/shard_map/ppermute | solution.py:513
  299.6 11.7 %collective-permute-start.37 = (bf16[256,768]{1,0:T(8,128)(2,1)S(1)}, bf16[256,768]{1,0:T(8,128)(2,1)}, u32[]{:S(2)}, u32[]{:S(2)}) collective-permute-start(bf16[256,768]{1,0:T(8,128)(2,1)S(1)} %slice_bitcast_fusion.2), channel_id=1, source_target_pairs={{0,1},{1,0},{2,3},{3,2},{4,5},{5,4},{6,7},{7,6},{8,9},{9,8},{10,11... | collective-permute-start | bytes 1179656 | tf_op jit(solution)/shard_map/ppermute | solution.py:513
  311.2 38.1 %collective-permute-start.38 = (bf16[448,768]{1,0:T(8,128)(2,1)}, bf16[448,768]{1,0:T(8,128)(2,1)S(1)}, u32[]{:S(2)}, u32[]{:S(2)}) collective-permute-start(bf16[448,768]{1,0:T(8,128)(2,1)} %get-tuple-element.288), channel_id=1, source_target_pairs={{0,8},{1,9},{2,10},{3,11},{4,12},{5,13},{6,14},{7,15},{8,0},{9,1},... | collective-permute-start | bytes 2064392 | tf_op jit(solution)/shard_map/ppermute | solution.py:513
  312.5 36.9 %collective-permute-start.39 = (bf16[448,768]{1,0:T(8,128)(2,1)}, bf16[448,768]{1,0:T(8,128)(2,1)S(1)}, u32[]{:S(2)}, u32[]{:S(2)}) collective-permute-start(bf16[448,768]{1,0:T(8,128)(2,1)} %get-tuple-element.289), channel_id=1, source_target_pairs={{0,16},{1,17},{2,18},{3,19},{4,20},{5,21},{6,22},{7,23},{8,24},{9,... | collective-permute-start | bytes 2064392 | tf_op jit(solution)/shard_map/ppermute | solution.py:513
  313.5 35.8 %collective-permute-start.40 = (bf16[448,768]{1,0:T(8,128)(2,1)}, bf16[448,768]{1,0:T(8,128)(2,1)S(1)}, u32[]{:S(2)}, u32[]{:S(2)}) collective-permute-start(bf16[448,768]{1,0:T(8,128)(2,1)} %get-tuple-element.290), channel_id=1, source_target_pairs={{0,24},{1,25},{2,26},{3,27},{4,28},{5,29},{6,30},{7,31},{8,16},{9,... | collective-permute-start | bytes 2064392 | tf_op jit(solution)/shard_map/ppermute | solution.py:513
  315.8 33.6 %collective-permute-start.42 = (bf16[256,768]{1,0:T(8,128)(2,1)S(1)}, bf16[256,768]{1,0:T(8,128)(2,1)S(1)}, u32[]{:S(2)}, u32[]{:S(2)}) collective-permute-start(bf16[256,768]{1,0:T(8,128)(2,1)S(1)} %slice_bitcast_fusion.1), channel_id=1, source_target_pairs={{0,3},{1,2},{2,1},{3,0},{4,7},{5,6},{6,5},{7,4},{8,11},{9,10},{10,... | collective-permute-start | bytes 1179656 | tf_op jit(solution)/shard_map/ppermute | solution.py:513
  319.9 29.4 %collective-permute-start.41 = (bf16[1,216,768]{2,1,0:T(8,128)(2,1)S(1)}, bf16[1,216,768]{2,1,0:T(8,128)(2,1)S(1)}, u32[]{:S(2)}, u32[]{:S(2)}) collective-permute-start(bf16[1,216,768]{2,1,0:T(8,128)(2,1)S(1)} %slice.161), channel_id=1, source_target_pairs={{0,2},{1,3},{2,0},{3,1},{4,6},{5,7},{6,4},{7,5},{8,10},{9,11},{10,... | collective-permute-start | bytes 995336 | tf_op jit(solution)/shard_map/ppermute | solution.py:513
  354.2 9.7 %collective-permute-start.43 = (bf16[2,112,768]{2,1,0:T(8,128)(2,1)}, bf16[2,112,768]{2,1,0:T(8,128)(2,1)}, u32[]{:S(2)}, u32[]{:S(2)}) collective-permute-start(bf16[2,112,768]{2,1,0:T(8,128)(2,1)} %get-tuple-element.313), channel_id=1, source_target_pairs={{0,1},{1,0},{2,3},{3,2},{4,5},{5,4},{6,7},{7,6},{8,9},{9,8},{10,11... | collective-permute-start | bytes 1032200 | tf_op jit(solution)/shard_map/ppermute | solution.py:513
  363.9 14.9 %copy-start.1 = (f32[4,256,768]{2,1,0:T(8,128)}, f32[4,256,768]{2,1,0:T(8,128)S(1)}, u32[]{:S(2)}) copy-start(f32[4,256,768]{2,1,0:T(8,128)S(1)} %convert_dynamic-update-slice_fusion) | copy-start | bytes 9437188
  366.3 10.0 %collective-permute-start.44 = (bf16[1,112,768]{2,1,0:T(8,128)(2,1)S(1)}, bf16[1,112,768]{2,1,0:T(8,128)(2,1)S(1)}, u32[]{:S(2)}, u32[]{:S(2)}) collective-permute-start(bf16[1,112,768]{2,1,0:T(8,128)(2,1)S(1)} %slice.162), channel_id=1, source_target_pairs={{0,2},{1,3},{2,0},{3,1},{4,6},{5,7},{6,4},{7,5},{8,10},{9,11},{10,... | collective-permute-start | bytes 516104 | tf_op jit(solution)/shard_map/ppermute | solution.py:513
  (37 other events, 147.1 us)
where the time goes:
time: 383 us; the launch traced here: 379 us
  Pallas kernels  180 us (47%)
  waiting for transfers between devices  94.3 us (25%)
  starting transfers between devices  58 us (15%)
  local copies, waits for them, and re-layouts  32.8 us (9%)
  other arithmetic  11.2 us (3%)
    ppermute x45, waiting for transfers between devices, flip(): return lax.ppermute(x, AXES, [(i, i ^ mask) for i in range(total)])  94.3 us
    ppermute x45, starting transfers between devices, flip(): return lax.ppermute(x, AXES, [(i, i ^ mask) for i in range(total)])  58 us
    pallas_call x1, Pallas kernels, middle(): pl.pallas_call(kern, grid=(nb,), in_specs=[smem(), smem(), row, blk] + [p...  54.5 us
    pallas_call x3, Pallas kernels, attn_bwd(): pl.pallas_call(functools.partial(bwd_kernel, p0), grid=(np_,), in_specs=[...  44.1 us
    pallas_call x2, Pallas kernels, attn_fwd(): pl.pallas_call(fwd_kernel, grid=(np_,), in_specs=[col(), col(), col(), pl...  23.9 us
    pallas_call x1, Pallas kernels, weight_grads(): pl.pallas_call(functools.partial(weight_kernel, nc, unit), grid=(L // R,)...  13 us
    pallas_call x1, Pallas kernels, token_grads(): pl.pallas_call(functools.partial(token_kernel, nc), grid=(nt,), in_specs=...  12 us
    unnamed x80, local copies, waits for them, and re-layouts  11.3 us
  transfers between devices with their start and end apart: 45, of which 15 were waited for; matrix products, arithmetic and copies ran while one was open for 8% of the time, Pallas kernels for 30%

commit v1 on v0

--- a/solution.py
+++ b/solution.py
@@ -136,7 +136,7 @@
         up=[wu[:,c*D:(c+1)*D] for c in range(wu.shape[1]//D)]
         return jnp.concatenate([wq,wk,wv,we,small]).astype(BF),jnp.concatenate([wo,wd]+up).astype(BF)
     return pl.pallas_call(pack_kernel,in_specs=[vm]*(8+len(vecs)),out_specs=[vm]*2,
-      out_shape=[sds((4*n+SMALL,D),BF),sds((second,D),BF)],scratch_shapes=[pltpu.VMEM((SMALL,D),F32)],name="pack")(*mats,*vecs)
+      out_shape=[sds((4*n+SMALL,D),BF),sds((second,D),BF)],scratch_shapes=[pltpu.VMEM((SMALL,D),F32)],compiler_params=pltpu.CompilerParams(vmem_limit_bytes=60*2**20),name="pack")(*mats,*vecs)
 ORDER=(0,2,4,6,1,3,5,7)
 def rows_at(me,t,n):
     return pl.ds(pl.multiple_of(jnp.bitwise_xor(me,ORDER[t])*n,n),n)
@@ -215,7 +215,7 @@
     return jnp.where(r<3,jnp.broadcast_to(rows[0:1,:].astype(F32),rows.shape),0.0).astype(BF)
 def token_kernel(nc,me_ref,info_ref,ga_ref,pre_ref,*rest):
     grads=rest[:nc]; pieces=rest[nc:nc+8]
-    tg_ref,rows_ref,wq,wk,wv,we,sems=rest[nc+8:]
+    *tg_refs,rows_ref,wq,wk,wv,we,sems=rest[nc+8:]
     i=pl.program_id(0); me=me_ref[0]
     D=wq.shape[0]; n=D//8
     wcp=[load_weights(me,pieces,w*n,n,dst,sems.at[w]) for w,dst in enumerate((wq,wk,wv,we))]
@@ -232,8 +232,12 @@
         def _():
             for c in wcp[w]: c.wait()
         g=g+mm(y,dst[...],NT)
-    tg_ref[0]=g.astype(BF)
-    rows_ref[pl.ds(3,1),:]+=info_ref[i,0].astype(F32)*jnp.sum(g,axis=0,keepdims=True)
+    R=tg_refs[0].shape[0]; per=g.shape[0]//R
+    for c in range(per):
+        rows_ref[pl.ds(3,1),:]+=info_ref[i*per+c,0].astype(F32)*jnp.sum(g[c*R:(c+1)*R],axis=0,keepdims=True)
+    for c,ref in enumerate(tg_refs):
+        @pl.when(i==c//per)
+        def _(): ref[...]=g[c%per*R:(c%per+1)*R].astype(BF)
     @pl.when(i==pl.num_programs(0)-1)
     def _():
         for c in wcp[3]: c.wait()
@@ -241,12 +245,13 @@
         pre=pre_ref[0:1,:]
         sg=1.0/(1.0+jnp.exp(-pre))
         rows_ref[pl.ds(2,1),:]=gh*(sg*(1.0+pre*(1.0-sg)))
-def token_grads(me,info,ga,pre,grads,pieces,R):
-    L,D=ga.shape; nt=L//R; nc=len(grads); W=grads[0].shape[2]
-    outs=[sds((nt,R,D),BF),sds((8,D),F32)]
+STEP=512
+def token_grads(me,info,ga,pre,grads,pieces,C):
+    L,D=ga.shape; R=max(STEP,C); nt=L//R; nc=len(grads)
+    outs=[sds((C,D),BF)]*(L//C)+[sds((8,D),F32)]
     return pl.pallas_call(functools.partial(token_kernel,nc),grid=(nt,),
-      in_specs=[smem(),smem(),pl.BlockSpec((R,D),lambda i:(i,0)),pl.BlockSpec((8,D),lambda i:(0,0))]+[pl.BlockSpec((3,R,W),lambda i:(0,i,0))]*nc+[anyw()]*8,
-      out_specs=[pl.BlockSpec((1,R,D),lambda i:(i,0,0)),once(outs[1])],
+      in_specs=[smem(),smem(),pl.BlockSpec((R,D),lambda i:(i,0)),pl.BlockSpec((8,D),lambda i:(0,0))]+[pl.BlockSpec((3,R,a.shape[2]),lambda i:(0,i,0)) for a in grads]+[anyw()]*8,
+      out_specs=[once(o) for o in outs],
       out_shape=outs,
       scratch_shapes=[pltpu.VMEM((D,D),BF)]*4+[pltpu.SemaphoreType.DMA((4,))],
       compiler_params=pltpu.CompilerParams(vmem_limit_bytes=60*2**20),
@@ -288,12 +293,12 @@
     def _():
         for t in range(8):
             for w in range(4): to(t)[t%4,w*n:(w+1)*n,:]=acc[rows_at(me,t,n),w*D:(w+1)*D].astype(BF)
-def weight_grads(me,inp,rows,hid,feat,dvec,dupb,grads,unit,R):
-    L,D=inp.shape; n=D//8; nc=len(grads); W=grads[0].shape[2]
+def weight_grads(me,inp,rows,hid,feat,dvec,dupb,grads,unit):
+    L,D=inp.shape; R=STEP; n=D//8; nc=len(grads)
     outs=[sds((4,4*n+feat.shape[1]//8,D),BF)]*2
     full=lambda a: pl.BlockSpec(a.shape,lambda i:(0,)*a.ndim)
     return pl.pallas_call(functools.partial(weight_kernel,nc,unit),grid=(L//R,),
-      in_specs=[smem(),pl.BlockSpec((R,D),lambda i:(i,0))]+[full(a) for a in (rows,hid,feat,dvec,dupb)]+[pl.BlockSpec((3,R,W),lambda i:(0,i,0))]*nc,
+      in_specs=[smem(),pl.BlockSpec((R,D),lambda i:(i,0))]+[full(a) for a in (rows,hid,feat,dvec,dupb)]+[pl.BlockSpec((3,R,a.shape[2]),lambda i:(0,i,0)) for a in grads],
       out_specs=[once(o) for o in outs],out_shape=outs,
       scratch_shapes=[pltpu.VMEM((D,4*D),F32)],
       compiler_params=pltpu.CompilerParams(vmem_limit_bytes=60*2**20),
@@ -306,28 +311,12 @@
     out=refs[0].astype(F32)
     for r in refs[1:]: out=out+r.astype(F32)
     return out
-def diag_kernel(cut,a,b,low,high):
-    x=total_of((a[0],b[0])).astype(BF)
-    low[...]=x[:cut]; high[...]=x[cut:]
-def sum_diag(mine,got,cut):
-    _,R,D=mine.shape
-    return pl.pallas_call(functools.partial(diag_kernel,cut),grid=(D//LB,),in_specs=[take(3,R)]*2,out_specs=[flat(cut),flat(R-cut)],
-      out_shape=[sds((cut,D),BF),sds((R-cut,D),BF)],name="sum_diag")(mine,got)
-def near_kernel(cut,a1,b1,a2,b2,low,high,fx,fy):
-    fx[:cut,:]=total_of((a1[0,:cut],b1[0,:cut])).astype(BF)
-    fx[cut:,:]=total_of((a1[0,cut:],b1[0,cut:],high[...])).astype(BF)
-    fy[:cut,:]=total_of((a2[0,:cut],b2[0,:cut],low[...])).astype(BF)
-    fy[cut:,:]=total_of((a2[0,cut:],b2[0,cut:])).astype(BF)
-def sum_near(mine,got,low,high):
-    _,R,D=mine.shape; cut=low.shape[0]
-    return pl.pallas_call(functools.partial(near_kernel,cut),grid=(D//LB,),in_specs=[take(1,R)]*2+[take(2,R)]*2+[flat(cut),flat(R-cut)],
-      out_specs=[flat(R)]*2,out_shape=[sds((R,D),BF)]*2,name="sum_near")(mine,got,mine,got,low,high)
 def three_kernel(a1,b1,a2,b2,a3,b3,o1,o2,o3):
     for a,b,o in ((a1,b1,o1),(a2,b2,o2),(a3,b3,o3)): o[...]=total_of((a[0],b[0])).astype(BF)
 def sum_three(mine,got):
     _,R,D=mine.shape
     return pl.pallas_call(three_kernel,grid=(D//LB,),in_specs=[take(1,R)]*2+[take(2,R)]*2+[take(3,R)]*2,
-      out_specs=[flat(R)]*3,out_shape=[sds((R,D),BF)]*3,name="sum_three")(mine,got,mine,got,mine,got)
+      out_specs=[flat(R)]*3,out_shape=[sds((R,D),BF)]*3,compiler_params=pltpu.CompilerParams(vmem_limit_bytes=60*2**20),name="sum_three")(mine,got,mine,got,mine,got)
 def own_kernel(sizes,unit,nx,inner_ref,a,b,*rest):
     more=rest[:nx]; keep,send,scr=rest[nx:]
     inner=inner_ref[0]
@@ -340,19 +329,20 @@
                 if j%2: send[j//2,out:out+size,:]=x.astype(BF)
                 else: keep[j//2,out:out+size,:]=x
                 at+=unit*size; out+=size
-def sum_own(inner,mine,got,more,sizes,unit,total):
+def sum_own(inner,mine,got,more,sizes,unit):
     _,R,D=mine.shape; rows=R//unit
     if any(size%8 for _,size in sizes):
         x=mine[0].astype(F32)+got[0].astype(F32)+sum(m.astype(F32) for m in more); at=0; parts=[]
         for count,size in sizes:
             for c in range(count):
                 parts.append(x[at:at+unit*size].reshape(unit,size,D)); at+=unit*size
-        return split_send(in_order(jnp.concatenate(parts,1),inner),1,total)
+        x=in_order(jnp.concatenate(parts,1),inner)
+        return jnp.stack([x[j] for j in range(0,unit,2)]),jnp.stack([x[j] for j in range(1,unit,2)]).astype(BF)
     blk=pl.BlockSpec((unit//2,rows,LB),lambda i:(0,0,i))
     keep,send=pl.pallas_call(functools.partial(own_kernel,sizes,unit,len(more)),grid=(D//LB,),
       in_specs=[smem()]+[take(0,R)]*2+[flat(R)]*len(more),out_specs=[blk]*2,
-      out_shape=[sds((unit//2,rows,D),F32),sds((unit//2,rows,D),BF)],scratch_shapes=[pltpu.VMEM((R,LB),F32)],name="sum_own")(inner.reshape(1).astype(jnp.int32),mine,got,*more)
-    return keep,flip(send,1,total)
+      out_shape=[sds((unit//2,rows,D),F32),sds((unit//2,rows,D),BF)],scratch_shapes=[pltpu.VMEM((R,LB),F32)],compiler_params=pltpu.CompilerParams(vmem_limit_bytes=60*2**20),name="sum_own")(inner.reshape(1).astype(jnp.int32),mine,got,*more)
+    return keep,send
 def last1_kernel(keep_ref,got_ref,*outs):
     x=keep_ref[...]+got_ref[...].astype(F32)
     *mats,st=outs[:5]; n=mats[0].shape[0]
@@ -367,7 +357,7 @@
     if n%8:
         x=keep+got.astype(F32)
         return [x[w*n:(w+1)*n] for w in range(4)]+[x[4*n:4*n+stamp_rows]]+[x[4*n+4+r,:k] for r,k in enumerate(sizes)]
-    return pl.pallas_call(last1_kernel,in_specs=[vm]*2,out_specs=[vm]*len(outs),out_shape=outs,name="last_attn")(keep,got)
+    return pl.pallas_call(last1_kernel,in_specs=[vm]*2,out_specs=[vm]*len(outs),out_shape=outs,compiler_params=pltpu.CompilerParams(vmem_limit_bytes=60*2**20),name="last_attn")(keep,got)
 def last2_kernel(keep_ref,got_ref,wo,wd,wu):
     x=keep_ref[...]+got_ref[...].astype(F32); n,D=wo.shape; m=wd.shape[0]
     wo[...]=x[:n]; wd[...]=x[n:n+m]
@@ -379,7 +369,7 @@
     if n%8:
         x=keep+got.astype(F32)
         return x[:n],x[n:n+m],jnp.concatenate([x[n+m+c*n:n+m+(c+1)*n] for c in range(FF//D)],1)
-    return pl.pallas_call(last2_kernel,in_specs=[vm]*2,out_specs=[vm]*3,out_shape=outs,name="last_ffn")(keep,got)
+    return pl.pallas_call(last2_kernel,in_specs=[vm]*2,out_specs=[vm]*3,out_shape=outs,compiler_params=pltpu.CompilerParams(vmem_limit_bytes=60*2**20),name="last_ffn")(keep,got)
 
 INV_SQRT2=0.7071067811865476; INV_SQRT2PI=0.3989422804014327
 HEAD=64
@@ -616,48 +606,38 @@
     cot=jnp.stack(cots)
     output,ga,gatt,auxd,mine2,theirs2,dvec,dupb=sync(*middle(me,info,mixed,cot,atts,vec,upb,p2))
     grads=[]
-    per=pairs//3
     def backward(c,q):
-        grads.append(attn_bwd(q,k,v,gatt,auxk,auxq[min(c,1)],auxd,c*per,per,c*per-sum(parts[:min(c,1)])))
+        grads.append(attn_bwd(q,k,v,gatt,auxk,auxq[c],auxd,sum(parts[:c]),parts[c],0))
     got=flip(theirs2,unit,total)
     backs=[output[0],flip(output[1],1,total)]
     backward(0,q)
     got,q,output,backs,grads=sync(got,q,output,backs,grads)
-    low,high=sum_diag(mine2,got,cut)
-    low=flip(low,2*unit,total); high=flip(high,4*unit,total)
-    backs.append(flip(output[2],2,total))
+    fx,fy,fd=(flip(x,g*unit,total) for x,g in zip(sum_three(mine2,got),(2,4,6)))
+    backs+=[flip(output[c],c,total) for c in range(2,streams)]
     backward(1,q)
-    held=backs.pop()
-    low,high,q,output,backs,grads=sync(low,high,q,output,backs,grads)
-    fx,fy,held=sync(*sum_near(mine2,got,low,high),held)
-    backs.append(held)
-    fx=flip(fx,2*unit,total); fy=flip(fy,4*unit,total)
-    backs.append(flip(output[3],3,total))
-    backward(2,q)
-    backs,grads=sync(backs,grads)
     def place(chunks,dtype):
         out=jnp.zeros((seqs,R,D),dtype)
         for c,part in enumerate(chunks):
             out=lax.dynamic_update_index_in_dim(out,part.astype(dtype),s0^c,0)
         return out
-    tg,rows4=token_grads(me,info,ga,pre,grads,p1,R)
-    tg,rows4,fx,fy=sync(tg,rows4,fx,fy)
-    keep2,got2=sum_own(inner,mine2,got,(fx,fy),((1,shard),(1,ff_shard),(FF//D,shard)),unit,total)
-    tgs=[tg[0],None,flip(tg[2],2,total)]
-    rows4,keep2,tg=sync(rows4,keep2,tg)
-    mine1,theirs1=weight_grads(me,inputs,rows4,hid,feat,dvec,dupb,grads,unit,R)
-    mine1,theirs1,got2,tg,tgs=sync(mine1,theirs1,got2,tg,tgs)
+    *tg,rows4=token_grads(me,info,ga,pre,grads,p1,R)
+    tg,rows4,backs=sync(tg,rows4,backs)
+    held=[flip(tg[c],c,total) for c in range(1,streams-1)]
+    mine1,theirs1=weight_grads(me,inputs,rows4,hid,feat,dvec,dupb,grads,unit)
+    mine1,theirs1,fx,fy,fd=sync(mine1,theirs1,fx,fy,fd)
+    keep2,send2=sum_own(inner,mine2,got,(fx,fy,fd),((1,shard),(1,ff_shard),(FF//D,shard)),unit)
+    keep2,send2,theirs1,held,tg=sync(keep2,send2,theirs1,held,tg)
+    got2=flip(send2,1,total)
     got1=flip(theirs1,unit,total)
-    tgs[1]=flip(tg[1],1,total)
+    tgs=[tg[0]]+held+[flip(tg[streams-1],streams-1,total)]
     blocks=sum_three(mine1,got1)
-    blocks,tgs,tg,keep2,got2=sync(blocks,tgs,tg,keep2,got2)
     fx,fy,fd=(flip(x,g*unit,total) for x,g in zip(blocks,(2,4,6)))
-    tgs.append(flip(tg[3],3,total))
     keep2,got2=finish2(keep2,got2,total)
-    fx,fy,fd,keep2,got2,tgs,backs=sync(fx,fy,fd,keep2,got2,tgs,backs)
+    fx,fy,fd,keep2,got2,tgs=sync(fx,fy,fd,keep2,got2,tgs)
     output=place(backs,BF)
     dwo,dwd,dwu=last2(keep2,got2,shard,ff_shard,FF)
-    keep1,got1=finish2(*sum_own(inner,mine1,got1,(fx,fy,fd),((4,shard),(1,SMALL)),unit,total),total)
+    keep1,send1=sum_own(inner,mine1,got1,(fx,fy,fd),((4,shard),(1,SMALL)),unit)
+    keep1,got1=finish2(keep1,flip(send1,1,total),total)
     dwq,dwk,dwv,dwe,dws,bq,bv,bo,ag,as_,bd,fg,fs,bs,be,bu=last1(keep1,got1,shard,stamp_rows,[shard]*10+[ff_shard])
     token_grad=place(tgs,F32)
     return (output,token_grad,dwq,bq,dwk,dwv,bv,dwo,bo,ag,as_,dwu,bu,dwd,bd,fg,fs,dws,bs,dwe,be)

time: 383 us -> 352 us (0.919)
  waiting for transfers between devices: 94.3 us -> 82.1 us
  local copies, waits for them, and re-layouts: 32.8 us -> 23 us
  Pallas kernels: 180 us -> 175 us
    ppermute x45 -> x44, waiting for transfers between devices: 94.3 us -> 82.1 us  [flip(): return lax.ppermute(x, AXES, [(i, i ^ mask) for i in range(total)])]
    pallas_call x2 -> x0, Pallas kernels: 6.98 us -> none  [the longest x1 4.18 us: sum_near(): pl.pallas_call(functools.partial(near_kernel, cut), grid=(D // LB,), in_s...]
    pallas_call x1 -> x2, Pallas kernels: 3.23 us -> 8.29 us  [sum_three(): pl.pallas_call(three_kernel, grid=(D // LB,), in_specs=[take(1, R)] * 2 +...]
    pallas_call x3 -> x2, Pallas kernels: 44.1 us -> 41.3 us  [attn_bwd(): pl.pallas_call(functools.partial(bwd_kernel, p0), grid=(np_,), in_specs=[...]
    unnamed x80 -> x68, local copies, waits for them, and re-layouts: 11.3 us -> 9.21 us
    ppermute x45 -> x44, starting transfers between devices: 58 us -> 56.4 us  [flip(): return lax.ppermute(x, AXES, [(i, i ^ mask) for i in range(total)])]
  transfers between devices with their start and end apart: 45 -> 44, of which waited for: 15 -> 17; matrix products, arithmetic and copies ran while one was open for 8% -> 6% of each run, Pallas kernels for 30% -> 31%
where the time goes in v1:
time: 352 us; the launch traced here: 349 us
  Pallas kernels  175 us (50%)
  waiting for transfers between devices  82.1 us (23%)
  starting transfers between devices  56.4 us (16%)
  local copies, waits for them, and re-layouts  23 us (7%)
  other arithmetic  9.85 us (3%)
    ppermute x44, waiting for transfers between devices, flip(): return lax.ppermute(x, AXES, [(i, i ^ mask) for i in range(total)])  82.1 us
    ppermute x44, starting transfers between devices, flip(): return lax.ppermute(x, AXES, [(i, i ^ mask) for i in range(total)])  56.4 us
    pallas_call x1, Pallas kernels, middle(): pl.pallas_call(kern, grid=(nb,), in_specs=[smem(), smem(), row, blk] + [p...  54.7 us
    pallas_call x2, Pallas kernels, attn_bwd(): pl.pallas_call(functools.partial(bwd_kernel, p0), grid=(np_,), in_specs=[...  41.3 us
    pallas_call x2, Pallas kernels, attn_fwd(): pl.pallas_call(fwd_kernel, grid=(np_,), in_specs=[col(), col(), col(), pl...  23.9 us
    pallas_call x1, Pallas kernels, token_grads(): pl.pallas_call(functools.partial(token_kernel, nc), grid=(nt,), in_specs=...  12.3 us
    pallas_call x1, Pallas kernels, weight_grads(): pl.pallas_call(functools.partial(weight_kernel, nc, unit), grid=(L // R,)...  11.5 us
    pallas_call x1, Pallas kernels, project(): pl.pallas_call(functools.partial(in_kernel, nt, unit), grid=(nt,), in_spe...  9.61 us
  transfers between devices with their start and end apart: 44, of which 17 were waited for; matrix products, arithmetic and copies ran while one was open for 6% of the time, Pallas kernels for 31%

profile of v1, /device:TPU:0, one launch (start us, length us, event | category | flops | bytes accessed | tf_op | source)
XLA Modules:
  0.0 348.8 jit_solution(10776288101744968955)
XLA Ops:
  0.7 2.1 pack.1
  2.8 4.0 %collective-permute-start = (bf16[1,112,768]{2,1,0:T(8,128)(2,1)}, bf16[1,112,768]{2,1,0:T(8,128)(2,1)S(1)}, u32[]{:S(2)}, u32[]{:S(2)}) collective-permute-start(bf16[1,112,768]{2,1,0:T(8,128)(2,1)} %bitcast.86), channel_id=1, source_target_pairs={{0,2},{1,3},{2,0},{3,1},{4,6},{5,7},{6,4},{7,5},{8,10},{9,11},{10,... | collective-permute-start | bytes 516104 | tf_op jit(solution)/shard_map/ppermute | solution.py:503
  13.7 2.3 dynamic-slice_bitcast_fusion.4
  16.7 3.2 collective-permute-start.1
  20.0 13.4 %collective-permute-done.2 = bf16[1,216,768]{2,1,0:T(8,128)(2,1)S(1)} collective-permute-done((bf16[1,216,768]{2,1,0:T(8,128)(2,1)S(1)}, bf16[1,216,768]{2,1,0:T(8,128)(2,1)S(1)}, u32[]{:S(2)}, u32[]{:S(2)}) %collective-permute-start.2) | collective-permute-done | bytes 331808 | tf_op jit(solution)/shard_map/ppermute | solution.py:503
  35.2 1.5 collective-permute-start.3
  36.7 1.5 collective-permute-start.4
  38.2 3.6 %collective-permute-start.5 = (bf16[256,768]{1,0:T(8,128)(2,1)S(1)}, bf16[256,768]{1,0:T(8,128)(2,1)S(1)}, u32[]{:S(2)}, u32[]{:S(2)}) collective-permute-start(bf16[256,768]{1,0:T(8,128)(2,1)S(1)} %get-tuple-element.166), channel_id=1, source_target_pairs={{0,2},{1,3},{2,0},{3,1},{4,6},{5,7},{6,4},{7,5},{8,10},{9,11},{10,... | collective-permute-start | bytes 1179656 | tf_op jit(solution)/shard_map/ppermute | solution.py:503
  42.3 16.6 %collective-permute-done.6 = bf16[2,216,768]{2,1,0:T(8,128)(2,1)S(1)} collective-permute-done((bf16[2,216,768]{2,1,0:T(8,128)(2,1)S(1)}, bf16[2,216,768]{2,1,0:T(8,128)(2,1)S(1)}, u32[]{:S(2)}, u32[]{:S(2)}) %collective-permute-start.6) | collective-permute-done | bytes 663584 | tf_op jit(solution)/shard_map/ppermute | solution.py:503
  59.1 3.1 collective-permute-start.8
  62.1 4.8 %collective-permute-done.4.rest_6_.rest_4_ = bf16[448,768]{1,0:T(8,128)(2,1)S(1)} collective-permute-done((bf16[448,768]{1,0:T(8,128)(2,1)S(1)}, bf16[448,768]{1,0:T(8,128)(2,1)S(1)}, u32[]{:S(2)}, u32[]{:S(2)}) %collective-permute-start.4) | collective-permute-done | bytes 688160 | tf_op jit(solution)/shard_map/ppermute | solution.py:503
  69.0 1.8 collective-permute-start.7
  70.8 1.8 collective-permute-done.8.rest_3_
  72.6 1.5 collective-permute-start.14
  74.2 1.5 collective-permute-start.15
  75.7 5.3 %collective-permute-done.7.rest_1_ = bf16[256,768]{1,0:T(8,128)(2,1)S(1)} collective-permute-done((bf16[256,768]{1,0:T(8,128)(2,1)S(1)}, bf16[256,768]{1,0:T(8,128)(2,1)S(1)}, u32[]{:S(2)}, u32[]{:S(2)}) %collective-permute-start.7) | collective-permute-done | bytes 393248 | tf_op jit(solution)/shard_map/ppermute | solution.py:503
  83.3 3.9 %collective-permute-start.17 = (bf16[256,768]{1,0:T(8,128)(2,1)S(1)}, bf16[256,768]{1,0:T(8,128)(2,1)S(1)}, u32[]{:S(2)}, u32[]{:S(2)}) collective-permute-start(bf16[256,768]{1,0:T(8,128)(2,1)S(1)} %get-tuple-element.177), channel_id=1, source_target_pairs={{0,1},{1,0},{2,3},{3,2},{4,5},{5,4},{6,7},{7,6},{8,9},{9,8},{10,11... | collective-permute-start | bytes 1179656 | tf_op jit(solution)/shard_map/ppermute | solution.py:503
  88.4 9.6 %project.1 = (f32[1024,768]{1,0:T(8,128)}, bf16[1024,768]{1,0:T(8,128)(2,1)}, bf16[1024,768]{1,0:T(8,128)(2,1)}, bf16[1024,768]{1,0:T(8,128)(2,1)}, bf16[1024,76...) custom-call(s32[1]{0:T(128)} %bitcast.me_ref, ...), custom_call_target="tpu_custom_call" | custom-call | flops 3623878656 | bytes 20000000 | tf_op jit(solution)/shard_map/project/pallas_call | solution.py:200
  98.1 8.7 %attn_fwd.2 = (bf16[1024,256]{1,0:T(8,128)(2,1)}, bf16[2,1024,128]{2,1,0:T(8,128)(2,1)}) custom-call(bf16[1024,768]{1,0:T(8,128)(2,1)} %get-tuple-element.216.q_ref, bf16[1024,768]{1,0:T(8,128)(2,1)} %get-tuple-element.180.k_ref, bf16[1024,768]{1,0:T(8,128)(2,1)} %get-tuple-element.181.v_ref, bf16[1024,128]{1,0:T(8,128)(2,1)} %get-tuple-element.182.auxk_ref), custom_call_target="tpu_custom_call" | custom-call | flops 1073741824 | bytes 2621440 | tf_op jit(solution)/shard_map/attn_fwd/pallas_call | solution.py:51
  111.1 2.5 collective-permute-start.23
  113.7 15.2 %attn_fwd.3 = (bf16[1024,512]{1,0:T(8,128)(2,1)}, bf16[4,1024,128]{2,1,0:T(8,128)(2,1)}) custom-call(bf16[1024,768]{1,0:T(8,128)(2,1)} %get-tuple-element.216.q_ref, bf16[1024,768]{1,0:T(8,128)(2,1)} %get-tuple-element.180.k_ref, bf16[1024,768]{1,0:T(8,128)(2,1)} %get-tuple-element.181.v_ref, bf16[1024,128]{1,0:T(8,128)(2,1)} %get-tuple-element.182.auxk_ref), custom_call_target="tpu_custom_call" | custom-call | flops 2147483648 | bytes 5242880 | tf_op jit(solution)/shard_map/attn_fwd/pallas_call | solution.py:51
  129.5 1.4 pad_maximum_fusion.cot_ref
  133.4 54.7 %middle.1 = (bf16[4,256,768]{2,1,0:T(8,128)(2,1)}, f32[1024,768]{1,0:T(8,128)}, bf16[1024,768]{1,0:T(8,128)(2,1)}, bf16[1024,128]{1,0:T(8,128)(2,1)}, bf16[4,864...) custom-call(s32[1]{0:T(128)} %bitcast.me_ref, ...), custom_call_target="tpu_custom_call" | custom-call | flops 32614907904 | bytes 60000000 | tf_op jit(solution)/shard_map/middle/pallas_call | solution.py:489
  189.4 4.2 %collective-permute-start.27 = (bf16[256,768]{1,0:T(8,128)(2,1)S(1)}, bf16[256,768]{1,0:T(8,128)(2,1)S(1)}, u32[]{:S(2)}, u32[]{:S(2)}) collective-permute-start(bf16[256,768]{1,0:T(8,128)(2,1)S(1)} %get-tuple-element.295), channel_id=1, source_target_pairs={{0,1},{1,0},{2,3},{3,2},{4,5},{5,4},{6,7},{7,6},{8,9},{9,8},{10,11... | collective-permute-start | bytes 1179656 | tf_op jit(solution)/shard_map/ppermute | solution.py:503
  193.6 14.6 %attn_bwd.2.rest_0_ = bf16[3,1024,256]{2,1,0:T(8,128)(2,1)} custom-call(bf16[1024,768]{1,0:T(8,128)(2,1)} %get-tuple-element.216.q_ref, bf16[1024,768]{1,0:T(8,128)(2,1)} %get-tuple-element.180.k_ref, bf16[1024,768]{1,0:T(8,128)(2,1)} %get-tuple-element.181.v_ref, bf16[1024,768]{1,0:T(8,128)(2,1)} %get-tuple-element.212.do_ref, ...), custom_call_target="tpu_custom_call" | custom-call | flops 2684354560 | bytes 4718592 | tf_op jit(solution)/shard_map/attn_bwd/pallas_call | solution.py:96
  208.2 5.1 %sum_three.2 = (bf16[864,768]{1,0:T(8,128)(2,1)}, bf16[864,768]{1,0:T(8,128)(2,1)}, bf16[864,768]{1,0:T(8,128)(2,1)}) custom-call(bf16[4,864,768]{2,1,0:T(8,128)(2,1)} %get-tuple-element.237.a1.a2.a3.a, bf16[4,864,768]{2,1,0:T(8,128)(2,1)} %collective-permute-done.26.b1.b2.b3.b, bf16[4,864,768]{2,1,0:T(8,128)(2,1)} %get-tuple-element.237.a1.a2.a3.a, ...), custom_call_target="tpu_custom_call" | custom-call | tf_op jit(solution)/shard_map/sum_three/pallas_call | solution.py:318
  213.3 1.5 collective-permute-start.30
  217.8 1.6 collective-permute-start.29
  219.3 26.7 %attn_bwd.3.rest_1_ = bf16[3,1024,512]{2,1,0:T(8,128)(2,1)} custom-call(bf16[1024,768]{1,0:T(8,128)(2,1)} %get-tuple-element.216.q_ref, bf16[1024,768]{1,0:T(8,128)(2,1)} %get-tuple-element.180.k_ref, bf16[1024,768]{1,0:T(8,128)(2,1)} %get-tuple-element.181.v_ref, bf16[1024,768]{1,0:T(8,128)(2,1)} %get-tuple-element.212.do_ref, ...), custom_call_target="tpu_custom_call" | custom-call | flops 5368709120 | bytes 9437184 | tf_op jit(solution)/shard_map/attn_bwd/pallas_call | solution.py:96
  246.1 12.3 %token_grads.1 = (bf16[256,768]{1,0:T(8,128)(2,1)}, bf16[256,768]{1,0:T(8,128)(2,1)}, bf16[256,768]{1,0:T(8,128)(2,1)}, bf16[256,768]{1,0:T(8,128)(2,1)}, f32[8,768]{1,0:T(8,128)}) custom-call(s32[1]{0:T(128)} %bitcast.me_ref, s32[4,2]{1,0:T(4,128)} %pad_add_fusion.info_ref, f32[1024,768]{1,0:T(8,128)} %get-tuple-element.208.ga_ref, ...), custom_call_target="tpu_custom_call" | custom-call | flops 3623878656 | bytes 15000000 | tf_op jit(solution)/shard_map/token_grads/pallas_call | solution.py:252
  260.2 1.7 collective-permute-start.34
  262.0 11.5 %weight_grads.1 = (bf16[4,448,768]{2,1,0:T(8,128)(2,1)}, bf16[4,448,768]{2,1,0:T(8,128)(2,1)}) custom-call(s32[1]{0:T(128)} %bitcast.me_ref, bf16[1024,768]{1,0:T(8,128)(2,1)} %get-tuple-element.230.inp_ref, f32[8,768]{1,0:T(8,128)} %get-tuple-element.231.rows_ref, bf16[8,768]{1,0:T(8,128)(2,1)} %get-tuple-element.232.hid_ref, ...), custom_call_target="tpu_custom_call" | custom-call | flops 3623878656 | bytes 12000000 | tf_op jit(solution)/shard_map/weight_grads/pallas_call | solution.py:300
  274.4 4.7 %sum_own.2 = (f32[2,216,768]{2,1,0:T(8,128)}, bf16[2,216,768]{2,1,0:T(8,128)(2,1)}) custom-call(s32[1]{0:T(128)} %bitcast.35.inner_ref, bf16[4,864,768]{2,1,0:T(8,128)(2,1)} %get-tuple-element.237.a1.a2.a3.a, bf16[4,864,768]{2,1,0:T(8,128)(2,1)} %collective-permute-done.26.b1.b2.b3.b, bf16[864,768]{1,0:T(8,128)(2,1)} %collective-permute-done.30.rest_0_, ...), custom_call_target="tpu_custom_call" | custom-call | tf_op jit(solution)/shard_map/sum_own/pallas_call | solution.py:342
  281.7 2.3 collective-permute-start.41
  285.3 1.5 copy-done
  286.8 3.2 sum_three.3
  290.0 1.5 collective-permute-start.36
  293.5 4.1 %collective-permute-done.39 = bf16[2,216,768]{2,1,0:T(8,128)(2,1)} collective-permute-done((bf16[2,216,768]{2,1,0:T(8,128)(2,1)}, bf16[2,216,768]{2,1,0:T(8,128)(2,1)}, u32[]{:S(2)}, u32[]{:S(2)}) %collective-permute-start.39) | collective-permute-done | bytes 663584 | tf_op jit(solution)/shard_map/ppermute | solution.py:503
  298.9 1.6 collective-permute-start.40
  302.1 5.0 %collective-permute-done.41 = bf16[256,768]{1,0:T(8,128)(2,1)} collective-permute-done((bf16[256,768]{1,0:T(8,128)(2,1)}, bf16[256,768]{1,0:T(8,128)(2,1)}, u32[]{:S(2)}, u32[]{:S(2)}) %collective-permute-start.41) | collective-permute-done | bytes 393248 | tf_op jit(solution)/shard_map/ppermute | solution.py:503
  307.1 13.6 %collective-permute-done.40 = bf16[1,216,768]{2,1,0:T(8,128)(2,1)S(1)} collective-permute-done((bf16[1,216,768]{2,1,0:T(8,128)(2,1)S(1)}, bf16[1,216,768]{2,1,0:T(8,128)(2,1)S(1)}, u32[]{:S(2)}, u32[]{:S(2)}) %collective-permute-start.40) | collective-permute-done | bytes 331808 | tf_op jit(solution)/shard_map/ppermute | solution.py:503
  320.7 2.9 collective-permute-done.37.rest_1_
  324.8 3.1 sum_own.3
  330.0 2.1 last_ffn.1
  333.2 3.0 collective-permute-done.42
  337.3 2.1 collective-permute-start.43
  340.1 5.9 %collective-permute-done.43 = bf16[1,112,768]{2,1,0:T(8,128)(2,1)S(1)} collective-permute-done((bf16[1,112,768]{2,1,0:T(8,128)(2,1)S(1)}, bf16[1,112,768]{2,1,0:T(8,128)(2,1)S(1)}, u32[]{:S(2)}, u32[]{:S(2)}) %collective-permute-start.43) | collective-permute-done | bytes 172064 | tf_op jit(solution)/shard_map/ppermute | solution.py:503
  346.7 1.8 last_attn.1
  (181 shorter events, 44.9 us)
Async XLA Ops:
  2.8 13.1 %collective-permute-start = (bf16[1,112,768]{2,1,0:T(8,128)(2,1)}, bf16[1,112,768]{2,1,0:T(8,128)(2,1)S(1)}, u32[]{:S(2)}, u32[]{:S(2)}) collective-permute-start(bf16[1,112,768]{2,1,0:T(8,128)(2,1)} %bitcast.86), channel_id=1, source_target_pairs={{0,2},{1,3},{2,0},{3,1},{4,6},{5,7},{6,4},{7,5},{8,10},{9,11},{10,... | collective-permute-start | bytes 516104 | tf_op jit(solution)/shard_map/ppermute | solution.py:503
  16.0 17.4 %collective-permute-start.2 = (bf16[1,216,768]{2,1,0:T(8,128)(2,1)S(1)}, bf16[1,216,768]{2,1,0:T(8,128)(2,1)S(1)}, u32[]{:S(2)}, u32[]{:S(2)}) collective-permute-start(bf16[1,216,768]{2,1,0:T(8,128)(2,1)S(1)} %bitcast.83), channel_id=1, source_target_pairs={{0,2},{1,3},{2,0},{3,1},{4,6},{5,7},{6,4},{7,5},{8,10},{9,11},{10,... | collective-permute-start | bytes 995336 | tf_op jit(solution)/shard_map/ppermute | solution.py:503
  16.7 17.2 %collective-permute-start.1 = (bf16[2,112,768]{2,1,0:T(8,128)(2,1)S(1)}, bf16[2,112,768]{2,1,0:T(8,128)(2,1)S(1)}, u32[]{:S(2)}, u32[]{:S(2)}) collective-permute-start(bf16[2,112,768]{2,1,0:T(8,128)(2,1)S(1)} %pad_maximum_fusion.5), channel_id=1, source_target_pairs={{0,1},{1,0},{2,3},{3,2},{4,5},{5,4},{6,7},{7,6},{8,9},{9,8},{10,11... | collective-permute-start | bytes 1032200 | tf_op jit(solution)/shard_map/ppermute | solution.py:503
  34.6 24.5 %copy-start.7 = (bf16[448,768]{1,0:T(8,128)(2,1)}, bf16[448,768]{1,0:T(8,128)(2,1)S(1)}, u32[]{:S(2)}) copy-start(bf16[448,768]{1,0:T(8,128)(2,1)S(1)} %pad_maximum_fusion.3.rest_4_.rest_2_) | copy-start | bytes 2064388
  35.2 23.7 %collective-permute-start.6 = (bf16[2,216,768]{2,1,0:T(8,128)(2,1)S(1)}, bf16[2,216,768]{2,1,0:T(8,128)(2,1)S(1)}, u32[]{:S(2)}, u32[]{:S(2)}) collective-permute-start(bf16[2,216,768]{2,1,0:T(8,128)(2,1)S(1)} %pad_maximum_fusion.4), channel_id=1, source_target_pairs={{0,1},{1,0},{2,3},{3,2},{4,5},{5,4},{6,7},{7,6},{8,9},{9,8},{10,11... | collective-permute-start | bytes 1990664 | tf_op jit(solution)/shard_map/ppermute | solution.py:503
  35.2 26.9 %collective-permute-start.3 = (bf16[448,768]{1,0:T(8,128)(2,1)S(1)}, bf16[448,768]{1,0:T(8,128)(2,1)S(1)}, u32[]{:S(2)}, u32[]{:S(2)}) collective-permute-start(bf16[448,768]{1,0:T(8,128)(2,1)S(1)} %pad_maximum_fusion.3.rest_4_.rest_2_), channel_id=1, source_target_pairs={{0,8},{1,9},{2,10},{3,11},{4,12},{5,13},{6,14},{7,15},{8,0},{9,1},... | collective-permute-start | bytes 2064392 | tf_op jit(solution)/shard_map/ppermute | solution.py:503
  36.7 30.3 %collective-permute-start.4 = (bf16[448,768]{1,0:T(8,128)(2,1)S(1)}, bf16[448,768]{1,0:T(8,128)(2,1)S(1)}, u32[]{:S(2)}, u32[]{:S(2)}) collective-permute-start(bf16[448,768]{1,0:T(8,128)(2,1)S(1)} %pad_maximum_fusion.3.rest_4_.rest_2_), channel_id=1, source_target_pairs={{0,16},{1,17},{2,18},{3,19},{4,20},{5,21},{6,22},{7,23},{8,24},{9,... | collective-permute-start | bytes 2064392 | tf_op jit(solution)/shard_map/ppermute | solution.py:503
  38.2 20.8 %collective-permute-start.5 = (bf16[256,768]{1,0:T(8,128)(2,1)S(1)}, bf16[256,768]{1,0:T(8,128)(2,1)S(1)}, u32[]{:S(2)}, u32[]{:S(2)}) collective-permute-start(bf16[256,768]{1,0:T(8,128)(2,1)S(1)} %get-tuple-element.166), channel_id=1, source_target_pairs={{0,2},{1,3},{2,0},{3,1},{4,6},{5,7},{6,4},{7,5},{8,10},{9,11},{10,... | collective-permute-start | bytes 1179656 | tf_op jit(solution)/shard_map/ppermute | solution.py:503
  41.8 32.3 %collective-permute-start.9 = (bf16[448,768]{1,0:T(8,128)(2,1)S(1)}, bf16[448,768]{1,0:T(8,128)(2,1)S(1)}, u32[]{:S(2)}, u32[]{:S(2)}) collective-permute-start(bf16[448,768]{1,0:T(8,128)(2,1)S(1)} %pad_maximum_fusion.3.rest_4_.rest_2_), channel_id=1, source_target_pairs={{0,24},{1,25},{2,26},{3,27},{4,28},{5,29},{6,30},{7,31},{8,16},{9,... | collective-permute-start | bytes 2064392 | tf_op jit(solution)/shard_map/ppermute | solution.py:503
  58.9 16.8 %collective-permute-start.10 = (bf16[448,768]{1,0:T(8,128)(2,1)S(1)}, bf16[448,768]{1,0:T(8,128)(2,1)S(1)}, u32[]{:S(2)}, u32[]{:S(2)}) collective-permute-start(bf16[448,768]{1,0:T(8,128)(2,1)S(1)} %pad_maximum_fusion.3.rest_4_.rest_2_), channel_id=1, source_target_pairs={{0,4},{1,5},{2,6},{3,7},{4,0},{5,1},{6,2},{7,3},{8,12},{9,13},{10,... | collective-permute-start | bytes 2064392 | tf_op jit(solution)/shard_map/ppermute | solution.py:503
  59.1 13.5 %collective-permute-start.8 = (bf16[256,768]{1,0:T(8,128)(2,1)S(1)}, bf16[256,768]{1,0:T(8,128)(2,1)S(1)}, u32[]{:S(2)}, u32[]{:S(2)}) collective-permute-start(bf16[256,768]{1,0:T(8,128)(2,1)S(1)} %get-tuple-element.171), channel_id=1, source_target_pairs={{0,3},{1,2},{2,1},{3,0},{4,7},{5,6},{6,5},{7,4},{8,11},{9,10},{10,... | collective-permute-start | bytes 1179656 | tf_op jit(solution)/shard_map/ppermute | solution.py:503
  67.0 14.0 %copy-start.25 = (bf16[448,768]{1,0:T(8,128)(2,1)}, bf16[448,768]{1,0:T(8,128)(2,1)S(1)}, u32[]{:S(2)}) copy-start(bf16[448,768]{1,0:T(8,128)(2,1)S(1)} %collective-permute-done.4.rest_6_.rest_4_) | copy-start | bytes 2064388
  67.5 13.7 %collective-permute-start.11 = (bf16[448,768]{1,0:T(8,128)(2,1)S(1)}, bf16[448,768]{1,0:T(8,128)(2,1)S(1)}, u32[]{:S(2)}, u32[]{:S(2)}) collective-permute-start(bf16[448,768]{1,0:T(8,128)(2,1)S(1)} %collective-permute-done.3.rest_5_.rest_3_), channel_id=1, source_target_pairs={{0,4},{1,5},{2,6},{3,7},{4,0},{5,1},{6,2},{7,3},{8,12},{9,13},{10,... | collective-permute-start | bytes 2064392 | tf_op jit(solution)/shard_map/ppermute | solution.py:503
  69.0 12.0 %collective-permute-start.7 = (bf16[256,768]{1,0:T(8,128)(2,1)S(1)}, bf16[256,768]{1,0:T(8,128)(2,1)S(1)}, u32[]{:S(2)}, u32[]{:S(2)}) collective-permute-start(bf16[256,768]{1,0:T(8,128)(2,1)S(1)} %get-tuple-element.169), channel_id=1, source_target_pairs={{0,1},{1,0},{2,3},{3,2},{4,5},{5,4},{6,7},{7,6},{8,9},{9,8},{10,11... | collective-permute-start | bytes 1179656 | tf_op jit(solution)/shard_map/ppermute | solution.py:503
  72.6 34.1 %collective-permute-start.14 = (bf16[864,768]{1,0:T(8,128)(2,1)S(1)}, bf16[864,768]{1,0:T(8,128)(2,1)}, u32[]{:S(2)}, u32[]{:S(2)}) collective-permute-start(bf16[864,768]{1,0:T(8,128)(2,1)S(1)} %pad_maximum_fusion.2.rest_4_), channel_id=1, source_target_pairs={{0,8},{1,9},{2,10},{3,11},{4,12},{5,13},{6,14},{7,15},{8,0},{9,1},... | collective-permute-start | bytes 3981320 | tf_op jit(solution)/shard_map/ppermute | solution.py:503
  74.2 32.6 %collective-permute-start.15 = (bf16[864,768]{1,0:T(8,128)(2,1)S(1)}, bf16[864,768]{1,0:T(8,128)(2,1)}, u32[]{:S(2)}, u32[]{:S(2)}) collective-permute-start(bf16[864,768]{1,0:T(8,128)(2,1)S(1)} %pad_maximum_fusion.2.rest_4_), channel_id=1, source_target_pairs={{0,16},{1,17},{2,18},{3,19},{4,20},{5,21},{6,22},{7,23},{8,24},{9,... | collective-permute-start | bytes 3981320 | tf_op jit(solution)/shard_map/ppermute | solution.py:503
  75.7 31.1 %collective-permute-start.16 = (bf16[864,768]{1,0:T(8,128)(2,1)S(1)}, bf16[864,768]{1,0:T(8,128)(2,1)}, u32[]{:S(2)}, u32[]{:S(2)}) collective-permute-start(bf16[864,768]{1,0:T(8,128)(2,1)S(1)} %pad_maximum_fusion.2.rest_4_), channel_id=1, source_target_pairs={{0,4},{1,5},{2,6},{3,7},{4,0},{5,1},{6,2},{7,3},{8,12},{9,13},{10,... | collective-permute-start | bytes 3981320 | tf_op jit(solution)/shard_map/ppermute | solution.py:503
  81.0 2.3 collective-permute-start.12
  81.8 5.4 %collective-permute-start.13 = (bf16[448,768]{1,0:T(8,128)(2,1)S(1)}, bf16[448,768]{1,0:T(8,128)(2,1)S(1)}, u32[]{:S(2)}, u32[]{:S(2)}) collective-permute-start(bf16[448,768]{1,0:T(8,128)(2,1)S(1)} %collective-permute-done.9.rest_7_.rest_5_), channel_id=1, source_target_pairs={{0,4},{1,5},{2,6},{3,7},{4,0},{5,1},{6,2},{7,3},{8,12},{9,13},{10,... | collective-permute-start | bytes 2064392 | tf_op jit(solution)/shard_map/ppermute | solution.py:503
  83.3 23.4 %collective-permute-start.17 = (bf16[256,768]{1,0:T(8,128)(2,1)S(1)}, bf16[256,768]{1,0:T(8,128)(2,1)S(1)}, u32[]{:S(2)}, u32[]{:S(2)}) collective-permute-start(bf16[256,768]{1,0:T(8,128)(2,1)S(1)} %get-tuple-element.177), channel_id=1, source_target_pairs={{0,1},{1,0},{2,3},{3,2},{4,5},{5,4},{6,7},{7,6},{8,9},{9,8},{10,11... | collective-permute-start | bytes 1179656 | tf_op jit(solution)/shard_map/ppermute | solution.py:503
  87.2 19.5 %collective-permute-start.18 = (bf16[256,768]{1,0:T(8,128)(2,1)S(1)}, bf16[256,768]{1,0:T(8,128)(2,1)S(1)}, u32[]{:S(2)}, u32[]{:S(2)}) collective-permute-start(bf16[256,768]{1,0:T(8,128)(2,1)S(1)} %get-tuple-element.178), channel_id=1, source_target_pairs={{0,2},{1,3},{2,0},{3,1},{4,6},{5,7},{6,4},{7,5},{8,10},{9,11},{10,... | collective-permute-start | bytes 1179656 | tf_op jit(solution)/shard_map/ppermute | solution.py:503
  106.8 22.2 %collective-permute-start.21 = (bf16[864,768]{1,0:T(8,128)(2,1)}, bf16[864,768]{1,0:T(8,128)(2,1)}, u32[]{:S(2)}, u32[]{:S(2)}) collective-permute-start(bf16[864,768]{1,0:T(8,128)(2,1)} %collective-permute-done.14.rest_5_), channel_id=1, source_target_pairs={{0,4},{1,5},{2,6},{3,7},{4,0},{5,1},{6,2},{7,3},{8,12},{9,13},{10,... | collective-permute-start | bytes 3981320 | tf_op jit(solution)/shard_map/ppermute | solution.py:503
  106.8 22.1 %collective-permute-start.22 = (bf16[864,768]{1,0:T(8,128)(2,1)}, bf16[864,768]{1,0:T(8,128)(2,1)}, u32[]{:S(2)}, u32[]{:S(2)}) collective-permute-start(bf16[864,768]{1,0:T(8,128)(2,1)} %collective-permute-done.15.rest_6_), channel_id=1, source_target_pairs={{0,4},{1,5},{2,6},{3,7},{4,0},{5,1},{6,2},{7,3},{8,12},{9,13},{10,... | collective-permute-start | bytes 3981320 | tf_op jit(solution)/shard_map/ppermute | solution.py:503
  108.5 20.4 %collective-permute-start.19 = (bf16[480,768]{1,0:T(8,128)(2,1)S(1)}, bf16[480,768]{1,0:T(8,128)(2,1)}, u32[]{:S(2)}, u32[]{:S(2)}) collective-permute-start(bf16[480,768]{1,0:T(8,128)(2,1)S(1)} %slice.108), channel_id=1, source_target_pairs={{0,8},{1,9},{2,10},{3,11},{4,12},{5,13},{6,14},{7,15},{8,0},{9,1},... | collective-permute-start | bytes 2211848 | tf_op jit(solution)/shard_map/ppermute | solution.py:503
  110.2 18.7 %collective-permute-start.20 = (bf16[384,768]{1,0:T(8,128)(2,1)S(1)}, bf16[384,768]{1,0:T(8,128)(2,1)}, u32[]{:S(2)}, u32[]{:S(2)}) collective-permute-start(bf16[384,768]{1,0:T(8,128)(2,1)S(1)} %slice.109), channel_id=1, source_target_pairs={{0,16},{1,17},{2,18},{3,19},{4,20},{5,21},{6,22},{7,23},{8,24},{9,... | collective-permute-start | bytes 1769480 | tf_op jit(solution)/shard_map/ppermute | solution.py:503
  111.1 17.8 %collective-permute-start.23 = (bf16[256,768]{1,0:T(8,128)(2,1)S(1)}, bf16[256,768]{1,0:T(8,128)(2,1)S(1)}, u32[]{:S(2)}, u32[]{:S(2)}) collective-permute-start(bf16[256,768]{1,0:T(8,128)(2,1)S(1)} %get-tuple-element.193), channel_id=1, source_target_pairs={{0,3},{1,2},{2,1},{3,0},{4,7},{5,6},{6,5},{7,4},{8,11},{9,10},{10,... | collective-permute-start | bytes 1179656 | tf_op jit(solution)/shard_map/ppermute | solution.py:503
  128.9 3.3 collective-permute-start.24
  129.0 3.3 collective-permute-start.25
  188.1 20.1 %collective-permute-start.26 = (bf16[4,864,768]{2,1,0:T(8,128)(2,1)}, bf16[4,864,768]{2,1,0:T(8,128)(2,1)}, u32[]{:S(2)}, u32[]{:S(2)}) collective-permute-start(bf16[4,864,768]{2,1,0:T(8,128)(2,1)} %get-tuple-element.210), channel_id=1, source_target_pairs={{0,4},{1,5},{2,6},{3,7},{4,0},{5,1},{6,2},{7,3},{8,12},{9,13},{10,... | collective-permute-start | bytes 15925256 | tf_op jit(solution)/shard_map/ppermute | solution.py:503
  189.4 18.8 %collective-permute-start.27 = (bf16[256,768]{1,0:T(8,128)(2,1)S(1)}, bf16[256,768]{1,0:T(8,128)(2,1)S(1)}, u32[]{:S(2)}, u32[]{:S(2)}) collective-permute-start(bf16[256,768]{1,0:T(8,128)(2,1)S(1)} %get-tuple-element.295), channel_id=1, source_target_pairs={{0,1},{1,0},{2,3},{3,2},{4,5},{5,4},{6,7},{7,6},{8,9},{9,8},{10,11... | collective-permute-start | bytes 1179656 | tf_op jit(solution)/shard_map/ppermute | solution.py:503
  213.3 60.1 %collective-permute-start.30 = (bf16[864,768]{1,0:T(8,128)(2,1)}, bf16[864,768]{1,0:T(8,128)(2,1)}, u32[]{:S(2)}, u32[]{:S(2)}) collective-permute-start(bf16[864,768]{1,0:T(8,128)(2,1)} %get-tuple-element.239), channel_id=1, source_target_pairs={{0,8},{1,9},{2,10},{3,11},{4,12},{5,13},{6,14},{7,15},{8,0},{9,1},... | collective-permute-start | bytes 3981320 | tf_op jit(solution)/shard_map/ppermute | solution.py:503
  214.8 59.6 %collective-permute-start.31 = (bf16[864,768]{1,0:T(8,128)(2,1)}, bf16[864,768]{1,0:T(8,128)(2,1)}, u32[]{:S(2)}, u32[]{:S(2)}) collective-permute-start(bf16[864,768]{1,0:T(8,128)(2,1)} %get-tuple-element.240), channel_id=1, source_target_pairs={{0,16},{1,17},{2,18},{3,19},{4,20},{5,21},{6,22},{7,23},{8,24},{9,... | collective-permute-start | bytes 3981320 | tf_op jit(solution)/shard_map/ppermute | solution.py:503
  215.4 59.0 %collective-permute-start.32 = (bf16[864,768]{1,0:T(8,128)(2,1)}, bf16[864,768]{1,0:T(8,128)(2,1)}, u32[]{:S(2)}, u32[]{:S(2)}) collective-permute-start(bf16[864,768]{1,0:T(8,128)(2,1)} %get-tuple-element.241), channel_id=1, source_target_pairs={{0,24},{1,25},{2,26},{3,27},{4,28},{5,29},{6,30},{7,31},{8,16},{9,... | collective-permute-start | bytes 3981320 | tf_op jit(solution)/shard_map/ppermute | solution.py:503
  216.9 41.5 %collective-permute-start.28 = (bf16[256,768]{1,0:T(8,128)(2,1)S(1)}, bf16[256,768]{1,0:T(8,128)(2,1)S(1)}, u32[]{:S(2)}, u32[]{:S(2)}) collective-permute-start(bf16[256,768]{1,0:T(8,128)(2,1)S(1)} %get-tuple-element.294), channel_id=1, source_target_pairs={{0,2},{1,3},{2,0},{3,1},{4,6},{5,7},{6,4},{7,5},{8,10},{9,11},{10,... | collective-permute-start | bytes 1179656 | tf_op jit(solution)/shard_map/ppermute | solution.py:503
  217.8 40.6 %collective-permute-start.29 = (bf16[256,768]{1,0:T(8,128)(2,1)S(1)}, bf16[256,768]{1,0:T(8,128)(2,1)S(1)}, u32[]{:S(2)}, u32[]{:S(2)}) collective-permute-start(bf16[256,768]{1,0:T(8,128)(2,1)S(1)} %get-tuple-element.293), channel_id=1, source_target_pairs={{0,3},{1,2},{2,1},{3,0},{4,7},{5,6},{6,5},{7,4},{8,11},{9,10},{10,... | collective-permute-start | bytes 1179656 | tf_op jit(solution)/shard_map/ppermute | solution.py:503
  259.1 20.0 %collective-permute-start.33 = (bf16[256,768]{1,0:T(8,128)(2,1)}, bf16[256,768]{1,0:T(8,128)(2,1)S(1)}, u32[]{:S(2)}, u32[]{:S(2)}) collective-permute-start(bf16[256,768]{1,0:T(8,128)(2,1)} %get-tuple-element.249), channel_id=1, source_target_pairs={{0,1},{1,0},{2,3},{3,2},{4,5},{5,4},{6,7},{7,6},{8,9},{9,8},{10,11... | collective-permute-start | bytes 1179656 | tf_op jit(solution)/shard_map/ppermute | solution.py:503
  260.2 19.0 %collective-permute-start.34 = (bf16[256,768]{1,0:T(8,128)(2,1)}, bf16[256,768]{1,0:T(8,128)(2,1)S(1)}, u32[]{:S(2)}, u32[]{:S(2)}) collective-permute-start(bf16[256,768]{1,0:T(8,128)(2,1)} %get-tuple-element.250), channel_id=1, source_target_pairs={{0,2},{1,3},{2,0},{3,1},{4,6},{5,7},{6,4},{7,5},{8,10},{9,11},{10,... | collective-permute-start | bytes 1179656 | tf_op jit(solution)/shard_map/ppermute | solution.py:503
  280.0 5.3 %collective-permute-start.35 = (bf16[4,448,768]{2,1,0:T(8,128)(2,1)}, bf16[4,448,768]{2,1,0:T(8,128)(2,1)S(1)}, u32[]{:S(2)}, u32[]{:S(2)}) collective-permute-start(bf16[4,448,768]{2,1,0:T(8,128)(2,1)} %get-tuple-element.253), channel_id=1, source_target_pairs={{0,4},{1,5},{2,6},{3,7},{4,0},{5,1},{6,2},{7,3},{8,12},{9,13},{10,... | collective-permute-start | bytes 8257544 | tf_op jit(solution)/shard_map/ppermute | solution.py:503
  280.0 17.6 %collective-permute-start.39 = (bf16[2,216,768]{2,1,0:T(8,128)(2,1)}, bf16[2,216,768]{2,1,0:T(8,128)(2,1)}, u32[]{:S(2)}, u32[]{:S(2)}) collective-permute-start(bf16[2,216,768]{2,1,0:T(8,128)(2,1)} %get-tuple-element.258), channel_id=1, source_target_pairs={{0,1},{1,0},{2,3},{3,2},{4,5},{5,4},{6,7},{7,6},{8,9},{9,8},{10,11... | collective-permute-start | bytes 1990664 | tf_op jit(solution)/shard_map/ppermute | solution.py:503
  281.7 15.9 %copy-start.5 = (f32[2,216,768]{2,1,0:T(8,128)S(1)}, f32[2,216,768]{2,1,0:T(8,128)}, u32[]{:S(2)}) copy-start(f32[2,216,768]{2,1,0:T(8,128)} %get-tuple-element.257) | copy-start | bytes 3981316
  281.7 25.4 %collective-permute-start.41 = (bf16[256,768]{1,0:T(8,128)(2,1)}, bf16[256,768]{1,0:T(8,128)(2,1)}, u32[]{:S(2)}, u32[]{:S(2)}) collective-permute-start(bf16[256,768]{1,0:T(8,128)(2,1)} %get-tuple-element.262), channel_id=1, source_target_pairs={{0,3},{1,2},{2,1},{3,0},{4,7},{5,6},{6,5},{7,4},{8,11},{9,10},{10,... | collective-permute-start | bytes 1179656 | tf_op jit(solution)/shard_map/ppermute | solution.py:503
  290.0 30.7 %collective-permute-start.36 = (bf16[448,768]{1,0:T(8,128)(2,1)}, bf16[448,768]{1,0:T(8,128)(2,1)S(1)}, u32[]{:S(2)}, u32[]{:S(2)}) collective-permute-start(bf16[448,768]{1,0:T(8,128)(2,1)} %get-tuple-element.254), channel_id=1, source_target_pairs={{0,8},{1,9},{2,10},{3,11},{4,12},{5,13},{6,14},{7,15},{8,0},{9,1},... | collective-permute-start | bytes 2064392 | tf_op jit(solution)/shard_map/ppermute | solution.py:503
  291.5 32.2 %collective-permute-start.37 = (bf16[448,768]{1,0:T(8,128)(2,1)}, bf16[448,768]{1,0:T(8,128)(2,1)S(1)}, u32[]{:S(2)}, u32[]{:S(2)}) collective-permute-start(bf16[448,768]{1,0:T(8,128)(2,1)} %get-tuple-element.255), channel_id=1, source_target_pairs={{0,16},{1,17},{2,18},{3,19},{4,20},{5,21},{6,22},{7,23},{8,24},{9,... | collective-permute-start | bytes 2064392 | tf_op jit(solution)/shard_map/ppermute | solution.py:503
  292.2 31.4 %collective-permute-start.38 = (bf16[448,768]{1,0:T(8,128)(2,1)}, bf16[448,768]{1,0:T(8,128)(2,1)S(1)}, u32[]{:S(2)}, u32[]{:S(2)}) collective-permute-start(bf16[448,768]{1,0:T(8,128)(2,1)} %get-tuple-element.256), channel_id=1, source_target_pairs={{0,24},{1,25},{2,26},{3,27},{4,28},{5,29},{6,30},{7,31},{8,16},{9,... | collective-permute-start | bytes 2064392 | tf_op jit(solution)/shard_map/ppermute | solution.py:503
  298.9 21.8 %collective-permute-start.40 = (bf16[1,216,768]{2,1,0:T(8,128)(2,1)S(1)}, bf16[1,216,768]{2,1,0:T(8,128)(2,1)S(1)}, u32[]{:S(2)}, u32[]{:S(2)}) collective-permute-start(bf16[1,216,768]{2,1,0:T(8,128)(2,1)S(1)} %slice.141), channel_id=1, source_target_pairs={{0,2},{1,3},{2,0},{3,1},{4,6},{5,7},{6,4},{7,5},{8,10},{9,11},{10,... | collective-permute-start | bytes 995336 | tf_op jit(solution)/shard_map/ppermute | solution.py:503
  327.8 8.4 %collective-permute-start.42 = (bf16[2,112,768]{2,1,0:T(8,128)(2,1)}, bf16[2,112,768]{2,1,0:T(8,128)(2,1)}, u32[]{:S(2)}, u32[]{:S(2)}) collective-permute-start(bf16[2,112,768]{2,1,0:T(8,128)(2,1)} %get-tuple-element.271), channel_id=1, source_target_pairs={{0,1},{1,0},{2,3},{3,2},{4,5},{5,4},{6,7},{7,6},{8,9},{9,8},{10,11... | collective-permute-start | bytes 1032200 | tf_op jit(solution)/shard_map/ppermute | solution.py:503
  333.2 15.3 %copy-start.1 = (f32[4,256,768]{2,1,0:T(8,128)}, f32[4,256,768]{2,1,0:T(8,128)S(1)}, u32[]{:S(2)}) copy-start(f32[4,256,768]{2,1,0:T(8,128)S(1)} %convert_dynamic-update-slice_fusion) | copy-start | bytes 9437188
  337.3 8.8 %collective-permute-start.43 = (bf16[1,112,768]{2,1,0:T(8,128)(2,1)S(1)}, bf16[1,112,768]{2,1,0:T(8,128)(2,1)S(1)}, u32[]{:S(2)}, u32[]{:S(2)}) collective-permute-start(bf16[1,112,768]{2,1,0:T(8,128)(2,1)S(1)} %slice.142), channel_id=1, source_target_pairs={{0,2},{1,3},{2,0},{3,1},{4,6},{5,7},{6,4},{7,5},{8,10},{9,11},{10,... | collective-permute-start | bytes 516104 | tf_op jit(solution)/shard_map/ppermute | solution.py:503
  (30 other events, 113.2 us)

commit v2 on v1

--- a/solution.py
+++ b/solution.py
@@ -56,7 +56,7 @@
       compiler_params=pltpu.CompilerParams(vmem_limit_bytes=60*2**20),
       cost_estimate=pl.CostEstimate(flops=np_*2*L*L*64*4,bytes_accessed=np_*L*128*2*5,transcendentals=np_*2*L*L),
       name="attn_fwd")(q,k,v,auxk)
-def bwd_kernel(p0,q_ref,k_ref,v_ref,do_ref,auxk_ref,auxq_ref,auxd_ref,out_ref,kaug,vaug,qa,doa,qm,dom,dk_acc,dv_acc):
+def bwd_pair(p0,q_ref,k_ref,v_ref,do_ref,auxk_ref,auxq_ref,auxd_ref,out_ref,kaug,vaug,qa,doa,qm,dom,dk_acc,dv_acc):
     pair=p0+pl.program_id(0)
     L=q_ref.shape[0]
     k=k_ref[...]; v=v_ref[...]; q=q_ref[...]; do=do_ref[...]
@@ -89,18 +89,22 @@
         out_ref[0,r,:]=(dq*0.125).astype(BF)
     out_ref[1]=dk_acc[...].astype(BF)
     out_ref[2]=dv_acc[...].astype(BF)
-def attn_bwd(q,k,v,do,auxk,auxq,auxd,p0,np_,a0):
+def bwd_specs(q,k,v,do,auxk,auxq,auxd,p0,a0):
     L=q.shape[0]
     col=lambda: pl.BlockSpec((L,128),lambda p:(0,p0+p))
     con=lambda: pl.BlockSpec((L,128),lambda p:(0,0))
-    return pl.pallas_call(functools.partial(bwd_kernel,p0),grid=(np_,),
-      in_specs=[col(),col(),col(),col(),con(),pl.BlockSpec((1,L,128),lambda p:(a0+p,0,0)),con()],
+    return ([col(),col(),col(),col(),con(),pl.BlockSpec((1,L,128),lambda p:(a0+p,0,0)),con()],
+      [pltpu.VMEM((2,L,256),BF),pltpu.VMEM((2,L,256),BF),pltpu.VMEM((L,256),BF),pltpu.VMEM((L,256),BF),
+        pltpu.VMEM((2,L,128),BF),pltpu.VMEM((2,L,128),BF),pltpu.VMEM((L,128),F32),pltpu.VMEM((L,128),F32)])
+def bwd_cost(L,np_): return pl.CostEstimate(flops=np_*2*L*L*64*10,bytes_accessed=np_*L*128*2*9,transcendentals=np_*2*L*L)
+def attn_bwd(q,k,v,do,auxk,auxq,auxd,p0,np_,a0):
+    L=q.shape[0]
+    ins,scratch=bwd_specs(q,k,v,do,auxk,auxq,auxd,p0,a0)
+    return pl.pallas_call(functools.partial(bwd_pair,p0),grid=(np_,),in_specs=ins,
       out_specs=pl.BlockSpec((3,L,128),lambda p:(0,0,p)),
-      out_shape=jax.ShapeDtypeStruct((3,L,128*np_),BF),
-      scratch_shapes=[pltpu.VMEM((2,L,256),BF),pltpu.VMEM((2,L,256),BF),pltpu.VMEM((L,256),BF),pltpu.VMEM((L,256),BF),
-        pltpu.VMEM((2,L,128),BF),pltpu.VMEM((2,L,128),BF),pltpu.VMEM((L,128),F32),pltpu.VMEM((L,128),F32)],
+      out_shape=jax.ShapeDtypeStruct((3,L,128*np_),BF),scratch_shapes=scratch,
       compiler_params=pltpu.CompilerParams(vmem_limit_bytes=60*2**20),
-      cost_estimate=pl.CostEstimate(flops=np_*2*L*L*64*10,bytes_accessed=np_*L*128*2*9,transcendentals=np_*2*L*L),
+      cost_estimate=bwd_cost(L,np_),
       name="attn_bwd")(q,k,v,do,auxk,auxq,auxd)
 
 SMALL=16; Q_B,V_B,OUT_B,ATT_G,ATT_S,DOWN_B,FFN_G,FFN_S,STAMP_B,EMBED_B=range(4,14); UP_B=14
@@ -213,50 +217,47 @@
 def three(rows):
     r=lax.broadcasted_iota(jnp.int32,rows.shape,0)
     return jnp.where(r<3,jnp.broadcast_to(rows[0:1,:].astype(F32),rows.shape),0.0).astype(BF)
-def token_kernel(nc,me_ref,info_ref,ga_ref,pre_ref,*rest):
-    grads=rest[:nc]; pieces=rest[nc:nc+8]
-    *tg_refs,rows_ref,wq,wk,wv,we,sems=rest[nc+8:]
+def finish_kernel(p0,nt,me_ref,info_ref,*rest):
+    att=rest[:7]; ga_hbm,pre_ref,first=rest[7:10]; pieces=rest[10:18]
+    out_ref=rest[18]; tg_refs=rest[19:19+nt]; rows_ref=rest[19+nt]
+    *work,ga,all_grads,wq,wk,wv,we,sems=rest[20+nt:]
     i=pl.program_id(0); me=me_ref[0]
-    D=wq.shape[0]; n=D//8
-    wcp=[load_weights(me,pieces,w*n,n,dst,sems.at[w]) for w,dst in enumerate((wq,wk,wv,we))]
+    L,D=ga.shape; n=D//8; F=first.shape[2]
+    cps=[pltpu.make_async_copy(first,all_grads.at[:,:,pl.ds(0,F)],sems.at[0]),pltpu.make_async_copy(ga_hbm,ga,sems.at[0])]
+    for w,dst in enumerate((wq,wk,wv,we)): cps+=load_weights(me,pieces,w*n,n,dst,sems.at[0])
     @pl.when(i==0)
     def _():
-        for w in wcp:
-            for c in w: c.start()
+        for c in cps: c.start()
+    bwd_pair(p0,*att,out_ref,*work)
+    all_grads[:,:,pl.ds(pl.multiple_of(F+i*128,128),128)]=out_ref[...]
+    @pl.when(i==pl.num_programs(0)-1)
+    def _():
+        for c in cps: c.wait()
         rows_ref[...]=jnp.zeros_like(rows_ref)
-    g=ga_ref[...]
-    for w,dst in enumerate((wq,wk,wv)):
-        y=jnp.concatenate([s[w] for s in grads],axis=1)
-        if w!=1: rows_ref[pl.ds(w//2,1),:]+=jnp.sum(y.astype(F32),axis=0,keepdims=True)
-        @pl.when(i==0)
-        def _():
-            for c in wcp[w]: c.wait()
-        g=g+mm(y,dst[...],NT)
-    R=tg_refs[0].shape[0]; per=g.shape[0]//R
-    for c in range(per):
-        rows_ref[pl.ds(3,1),:]+=info_ref[i*per+c,0].astype(F32)*jnp.sum(g[c*R:(c+1)*R],axis=0,keepdims=True)
-    for c,ref in enumerate(tg_refs):
-        @pl.when(i==c//per)
-        def _(): ref[...]=g[c%per*R:(c%per+1)*R].astype(BF)
-    @pl.when(i==pl.num_programs(0)-1)
-    def _():
-        for c in wcp[3]: c.wait()
+        R=L//nt
+        for c in range(nt):
+            r=pl.ds(c*R,R)
+            y=[all_grads[w,r,:] for w in range(3)]
+            for w in (0,2): rows_ref[pl.ds(w//2,1),:]+=jnp.sum(y[w].astype(F32),axis=0,keepdims=True)
+            g=ga[r,:]+(mm(y[0],wq[...],NT)+mm(y[1],wk[...],NT)+mm(y[2],wv[...],NT))
+            rows_ref[pl.ds(3,1),:]+=info_ref[c,0].astype(F32)*jnp.sum(g,axis=0,keepdims=True)
+            tg_refs[c][...]=g.astype(BF)
         gh=jnp.sum(mm(spread3(rows_ref[pl.ds(3,1),:]),we[...],NT),axis=0,keepdims=True)
         pre=pre_ref[0:1,:]
         sg=1.0/(1.0+jnp.exp(-pre))
         rows_ref[pl.ds(2,1),:]=gh*(sg*(1.0+pre*(1.0-sg)))
-STEP=512
-def token_grads(me,info,ga,pre,grads,pieces,C):
-    L,D=ga.shape; R=max(STEP,C); nt=L//R; nc=len(grads)
-    outs=[sds((C,D),BF)]*(L//C)+[sds((8,D),F32)]
-    return pl.pallas_call(functools.partial(token_kernel,nc),grid=(nt,),
-      in_specs=[smem(),smem(),pl.BlockSpec((R,D),lambda i:(i,0)),pl.BlockSpec((8,D),lambda i:(0,0))]+[pl.BlockSpec((3,R,a.shape[2]),lambda i:(0,i,0)) for a in grads]+[anyw()]*8,
-      out_specs=[once(o) for o in outs],
-      out_shape=outs,
-      scratch_shapes=[pltpu.VMEM((D,D),BF)]*4+[pltpu.SemaphoreType.DMA((4,))],
+def attn_finish(me,info,att,ga,pre,first,pieces,p0,np_,C):
+    L,D=ga.shape; nt=L//C
+    ins,scratch=bwd_specs(*att,p0,0)
+    outs=[sds((3,L,128*np_),BF)]+[sds((C,D),BF)]*nt+[sds((8,D),F32)]
+    return pl.pallas_call(functools.partial(finish_kernel,p0,nt),grid=(np_,),
+      in_specs=[smem(),smem()]+ins+[anyw(),pl.BlockSpec((8,D),lambda i:(0,0)),anyw()]+[anyw()]*8,
+      out_specs=[pl.BlockSpec((3,L,128),lambda p:(0,0,p))]+[once(o) for o in outs[1:]],out_shape=outs,
+      scratch_shapes=scratch+[pltpu.VMEM((L,D),F32),pltpu.VMEM((3,L,D),BF)]+[pltpu.VMEM((D,D),BF)]*4+[pltpu.SemaphoreType.DMA((1,))],
       compiler_params=pltpu.CompilerParams(vmem_limit_bytes=60*2**20),
-      cost_estimate=pl.CostEstimate(flops=2*L*D*D*3,bytes_accessed=15_000_000,transcendentals=0),
-      name="token_grads")(me,info,ga,pre,*grads,*pieces)
+      cost_estimate=bwd_cost(L,np_),
+      name="attn_finish")(me,info,*att,ga,pre,first,*pieces)
+STEP=1024
 def weight_kernel(nc,unit,me_ref,inp_ref,rows_ref,hid_ref,feat_ref,dvec_ref,dupb_ref,*rest):
     grads=rest[:nc]
     mine_ref,theirs_ref,acc=rest[nc:]
@@ -294,7 +295,7 @@
         for t in range(8):
             for w in range(4): to(t)[t%4,w*n:(w+1)*n,:]=acc[rows_at(me,t,n),w*D:(w+1)*D].astype(BF)
 def weight_grads(me,inp,rows,hid,feat,dvec,dupb,grads,unit):
-    L,D=inp.shape; R=STEP; n=D//8; nc=len(grads)
+    L,D=inp.shape; R=min(STEP,L); n=D//8; nc=len(grads)
     outs=[sds((4,4*n+feat.shape[1]//8,D),BF)]*2
     full=lambda a: pl.BlockSpec(a.shape,lambda i:(0,)*a.ndim)
     return pl.pallas_call(functools.partial(weight_kernel,nc,unit),grid=(L//R,),
@@ -305,6 +306,7 @@
       cost_estimate=pl.CostEstimate(flops=2*L*D*D*3,bytes_accessed=12_000_000,transcendentals=0),
       name="weight_grads")(me,inp,rows,hid,feat,dvec,dupb,*grads)
 LB=384
+def room(rows): return (60 if rows>512 else 20)*2**20
 def take(k,R): return pl.BlockSpec((1,R,LB),lambda i:(k,0,i))
 def flat(R): return pl.BlockSpec((R,LB),lambda i:(0,i))
 def total_of(refs):
@@ -316,7 +318,7 @@
 def sum_three(mine,got):
     _,R,D=mine.shape
     return pl.pallas_call(three_kernel,grid=(D//LB,),in_specs=[take(1,R)]*2+[take(2,R)]*2+[take(3,R)]*2,
-      out_specs=[flat(R)]*3,out_shape=[sds((R,D),BF)]*3,compiler_params=pltpu.CompilerParams(vmem_limit_bytes=60*2**20),name="sum_three")(mine,got,mine,got,mine,got)
+      out_specs=[flat(R)]*3,out_shape=[sds((R,D),BF)]*3,compiler_params=pltpu.CompilerParams(vmem_limit_bytes=room(R)),name="sum_three")(mine,got,mine,got,mine,got)
 def own_kernel(sizes,unit,nx,inner_ref,a,b,*rest):
     more=rest[:nx]; keep,send,scr=rest[nx:]
     inner=inner_ref[0]
@@ -341,23 +343,47 @@
     blk=pl.BlockSpec((unit//2,rows,LB),lambda i:(0,0,i))
     keep,send=pl.pallas_call(functools.partial(own_kernel,sizes,unit,len(more)),grid=(D//LB,),
       in_specs=[smem()]+[take(0,R)]*2+[flat(R)]*len(more),out_specs=[blk]*2,
-      out_shape=[sds((unit//2,rows,D),F32),sds((unit//2,rows,D),BF)],scratch_shapes=[pltpu.VMEM((R,LB),F32)],compiler_params=pltpu.CompilerParams(vmem_limit_bytes=60*2**20),name="sum_own")(inner.reshape(1).astype(jnp.int32),mine,got,*more)
+      out_shape=[sds((unit//2,rows,D),F32),sds((unit//2,rows,D),BF)],scratch_shapes=[pltpu.VMEM((R,LB),F32)],compiler_params=pltpu.CompilerParams(vmem_limit_bytes=room(R)),name="sum_own")(inner.reshape(1).astype(jnp.int32),mine,got,*more)
     return keep,send
-def last1_kernel(keep_ref,got_ref,*outs):
-    x=keep_ref[...]+got_ref[...].astype(F32)
+def direct_kernel(sizes,unit,nx,inner_ref,a,b,*rest):
+    more=rest[:nx]; outs=rest[nx:nx+unit]; scr=rest[nx+unit]
+    inner=inner_ref[0]
+    scr[...]=total_of((a[0],b[0])+tuple(x[...] for x in more))
+    for j,dst in enumerate(outs):
+        k=jnp.bitwise_xor(inner,j); at=0; out=0
+        for count,size in sizes:
+            for c in range(count):
+                dst[out:out+size,:]=scr[pl.ds(pl.multiple_of(at+k*size,8),size),:].astype(dst.dtype)
+                at+=unit*size; out+=size
+def sum_direct(inner,mine,got,more,sizes,unit):
+    _,R,D=mine.shape; rows=R//unit
+    if any(size%8 for _,size in sizes):
+        x=mine[0].astype(F32)+got[0].astype(F32)+sum(m.astype(F32) for m in more); at=0; parts=[]
+        for count,size in sizes:
+            for c in range(count):
+                parts.append(x[at:at+unit*size].reshape(unit,size,D)); at+=unit*size
+        x=in_order(jnp.concatenate(parts,1),inner)
+        return [x[0]]+[x[j].astype(BF) for j in range(1,unit)]
+    return pl.pallas_call(functools.partial(direct_kernel,sizes,unit,len(more)),grid=(D//LB,),
+      in_specs=[smem()]+[take(0,R)]*2+[flat(R)]*len(more),out_specs=[flat(rows)]*unit,
+      out_shape=[sds((rows,D),F32)]+[sds((rows,D),BF)]*(unit-1),scratch_shapes=[pltpu.VMEM((R,LB),F32)],
+      compiler_params=pltpu.CompilerParams(vmem_limit_bytes=room(R)),name="sum_direct")(inner.reshape(1).astype(jnp.int32),mine,got,*more)
+def last1_kernel(ng,*refs):
+    x=total_of([r[...] for r in refs[:ng]]); outs=refs[ng:]
     *mats,st=outs[:5]; n=mats[0].shape[0]
     for w,o in enumerate(mats): o[...]=x[w*n:(w+1)*n]
     st[...]=x[4*n:4*n+st.shape[0]]
     for r,o in enumerate(outs[5:]):
         o[...]=x[4*n+4+r:4*n+5+r,:o.shape[0]].reshape(o.shape)
-def last1(keep,got,n,stamp_rows,sizes):
-    D=keep.shape[1]
+def last1(given,n,stamp_rows,sizes):
+    D=given[0].shape[1]
     vm=pl.BlockSpec(memory_space=pltpu.VMEM)
     outs=[sds((n,D),F32)]*4+[sds((stamp_rows,D),F32)]+[sds((k,),F32) for k in sizes]
     if n%8:
-        x=keep+got.astype(F32)
+        x=sum(g.astype(F32) for g in given)
         return [x[w*n:(w+1)*n] for w in range(4)]+[x[4*n:4*n+stamp_rows]]+[x[4*n+4+r,:k] for r,k in enumerate(sizes)]
-    return pl.pallas_call(last1_kernel,in_specs=[vm]*2,out_specs=[vm]*len(outs),out_shape=outs,compiler_params=pltpu.CompilerParams(vmem_limit_bytes=60*2**20),name="last_attn")(keep,got)
+    return pl.pallas_call(functools.partial(last1_kernel,len(given)),in_specs=[vm]*len(given),out_specs=[vm]*len(outs),out_shape=outs,
+      compiler_params=pltpu.CompilerParams(vmem_limit_bytes=12*2**20),name="last_attn")(*given)
 def last2_kernel(keep_ref,got_ref,wo,wd,wu):
     x=keep_ref[...]+got_ref[...].astype(F32); n,D=wo.shape; m=wd.shape[0]
     wo[...]=x[:n]; wd[...]=x[n:n+m]
@@ -369,7 +395,7 @@
     if n%8:
         x=keep+got.astype(F32)
         return x[:n],x[n:n+m],jnp.concatenate([x[n+m+c*n:n+m+(c+1)*n] for c in range(FF//D)],1)
-    return pl.pallas_call(last2_kernel,in_specs=[vm]*2,out_specs=[vm]*3,out_shape=outs,compiler_params=pltpu.CompilerParams(vmem_limit_bytes=60*2**20),name="last_ffn")(keep,got)
+    return pl.pallas_call(last2_kernel,in_specs=[vm]*2,out_specs=[vm]*3,out_shape=outs,compiler_params=pltpu.CompilerParams(vmem_limit_bytes=12*2**20),name="last_ffn")(keep,got)
 
 INV_SQRT2=0.7071067811865476; INV_SQRT2PI=0.3989422804014327
 HEAD=64
@@ -381,9 +407,9 @@
 def norm_back(e,n,r):
     return r*(e-jnp.mean(e,axis=1,keepdims=True)-n*jnp.mean(e*n,axis=1,keepdims=True))
 def colsum(x): return jnp.sum(x,axis=0,keepdims=True)
-def mid_kernel(nblk,me_ref,info_ref,mix_ref,cot_ref,att_refs,vec_ref,upb_ref,pieces,
-        out_ref,gas_ref,gatt_ref,auxd_ref,mine_ref,theirs_ref,dvec_ref,dupb_ref,
-        wo,wd,wu,awo,awd,awu,gel,dgel,sems):
+def mid_kernel(nblk,me_ref,info_ref,mix_ref,cot_refs,att_refs,vec_ref,upb_ref,pieces,
+        out_refs,gas_ref,gatt_ref,auxd_ref,mine_ref,theirs_ref,dvec_ref,dupb_ref,
+        wo,wd,wu,cot,res,atta,hida,gda,gba,gel,gup,dgel,sems):
     i=pl.program_id(0); nb=pl.num_programs(0)
     D=wo.shape[0]; FF=wd.shape[0]; ro=D//nblk; rd=FF//nblk
     me=me_ref[0]
@@ -393,6 +419,7 @@
         [pltpu.make_async_copy(p.at[pl.ds(at+b*ro,ro),:],wu.at[rows_at(me,t,ro),pl.ds(b*D,D)],sems.at[1])
             for b in range(FF//D) for t,(p,at) in enumerate(upper)],
         load_weights(me,lower,ro,rd,wd,sems.at[2])]
+    cps[0]+=[pltpu.make_async_copy(src,cot.at[c],sems.at[0]) for c,src in enumerate(cot_refs)]
     def wait(which):
         @pl.when(i==0)
         def _():
@@ -401,7 +428,6 @@
     def _():
         for w in cps:
             for c in w: c.start()
-        awo[...]=jnp.zeros_like(awo); awd[...]=jnp.zeros_like(awd); awu[...]=jnp.zeros_like(awu)
         dvec_ref[...]=jnp.zeros_like(dvec_ref); dupb_ref[...]=jnp.zeros_like(dupb_ref)
     vec=lambda r: vec_ref[pl.ds(r,1),:].astype(F32)
     nlive=info_ref[i,1]
@@ -409,10 +435,13 @@
     live=(lax.broadcasted_iota(jnp.int32,(RB,1),0)<nlive).astype(F32)
     wait(0)
     att=jnp.concatenate([a[...] for a in att_refs],axis=1)
+    rows=pl.ds(pl.multiple_of(i*RB,RB),RB)
+    atta[rows,:]=att
     asum=x0+(mm(att,wo[...],NN)+vec(OUT_B))
     n1,r1=norm_stats(asum)
     normed=n1*vec(ATT_G)+vec(ATT_S)
     hid=normed.astype(BF)
+    hida[rows,:]=hid
     wait(1); wait(2)
     down=None
     for f in range(FF//FC):
@@ -421,27 +450,27 @@
         ph=0.5+0.5*lax.erf(u*INV_SQRT2)
         pd=jnp.exp(u*u*-0.5)*INV_SQRT2PI
         g=(u*ph).astype(BF)
-        gel[:,c]=g
+        gel[rows,c]=g
         dgel[:,c]=ph+u*pd
         t=mm(g,wd[c,:],NN)
         down=t if down is None else down+t
     fsum=normed+(down+vec(DOWN_B))
     n2,r2=norm_stats(fsum)
     g2=vec(FFN_G)
-    out_ref[0]=((n2*g2+vec(FFN_S))*live).astype(BF)
-    og=cot_ref[0].astype(F32)*live
+    res[i]=((n2*g2+vec(FFN_S))*live).astype(BF)
+    og=cot[i].astype(F32)*live
     dvec_ref[pl.ds(FFN_G,1),:]+=colsum(og*n2)
     dvec_ref[pl.ds(FFN_S,1),:]+=colsum(og)
     gf=norm_back(og*g2,n2,r2)
     gd=gf.astype(BF)
+    gda[rows,:]=gd
     dvec_ref[pl.ds(DOWN_B,1),:]+=colsum(gd.astype(F32))
     gn=gf
     for f in range(FF//FC):
         c=slice(f*FC,(f+1)*FC)
         gu=(mm(gd,wd[c,:],NT)*dgel[:,c]).astype(BF)
         dupb_ref[:,c]+=colsum(gu.astype(F32))
-        awd[c,:]+=mm(gel[:,c],gd,TN)
-        awu[:,c]+=mm(hid,gu,TN)
+        gup[rows,c]=gu
         gn=gn+mm(gu,wu[:,c],NT)
     dvec_ref[pl.ds(ATT_G,1),:]+=colsum(gn*n1)
     dvec_ref[pl.ds(ATT_S,1),:]+=colsum(gn)
@@ -449,7 +478,7 @@
     gas_ref[...]=ga
     gb=ga.astype(BF)
     dvec_ref[pl.ds(OUT_B,1),:]+=colsum(gb.astype(F32))
-    awo[...]+=mm(att,gb,TN)
+    gba[rows,:]=gb
     gatt=mm(gb,wo[...],NT).astype(BF)
     gatt_ref[...]=gatt
     pr=-(gatt.astype(F32)*att.astype(F32))
@@ -467,35 +496,42 @@
             cps=[pltpu.make_async_copy(src.at[rows_at(me,t,n),:],(mine_ref if t<4 else theirs_ref).at[t%4,pl.ds(at,n),:],sems.at[3]) for t in range(8)]
             for c in cps: c.start()
             return cps
-        wo[...]=awo[...].astype(BF)
-        out=send(wo,0,ro)
-        wd[...]=awd[...].astype(BF)
+        out=[pltpu.make_async_copy(res.at[c],dst,sems.at[3]) for c,dst in enumerate(out_refs)]
+        for c in out: c.start()
+        for b in range(FF//D):
+            c=slice(b*D,(b+1)*D)
+            wd[c,:]=mm(gel[:,c],gda[...],TN).astype(BF)
         out+=send(wd,ro,rd)
-        wu[...]=awu[...].astype(BF)
-        for b in range(FF//D): out+=send(wu.at[:,pl.ds(b*D,D)],ro+rd+b*ro,ro)
+        wo[...]=mm(atta[...],gba[...],TN).astype(BF)
+        out+=send(wo,0,ro)
+        for b in range(FF//D):
+            c=slice(b*D,(b+1)*D)
+            wu[:,c]=mm(hida[...],gup[:,c],TN).astype(BF)
+            out+=send(wu.at[:,pl.ds(b*D,D)],ro+rd+b*ro,ro)
         for c in out: c.wait()
-def middle(me,info,mixed,cot,atts,vec,upb,pieces):
+def middle(me,info,mixed,cots,atts,vec,upb,pieces):
     nblk=8; L,D=mixed.shape; FF=upb.shape[1]; ro=D//8; rd=FF//8
-    nb=L//RB; na=len(atts)
+    nb=L//RB; na=len(atts); nt=len(cots)
     flat_pieces=jax.tree.leaves(pieces)
-    def kern(me_ref,info_ref,mix_ref,cot_ref,*rest):
-        att=rest[:na]; rest=rest[na:]
+    def kern(me_ref,info_ref,mix_ref,*rest):
+        cot=rest[:nt]; att=rest[nt:nt+na]; rest=rest[nt+na:]
         given=iter(rest[2:2+len(flat_pieces)])
         blocks=[(next(given),next(given)) if isinstance(p,tuple) else next(given) for p in pieces]
-        mid_kernel(nblk,me_ref,info_ref,mix_ref,cot_ref,att,rest[0],rest[1],blocks,*rest[2+len(flat_pieces):])
+        rest_out=rest[2+len(flat_pieces):]
+        mid_kernel(nblk,me_ref,info_ref,mix_ref,cot,att,rest[0],rest[1],blocks,rest_out[:nt],*rest_out[nt:])
     full=lambda a: pl.BlockSpec(a.shape,lambda i:(0,)*a.ndim)
-    blk=pl.BlockSpec((1,RB,D),lambda i:(i,0,0)); row=pl.BlockSpec((RB,D),lambda i:(i,0))
-    outs=[sds((nb,RB,D),BF),sds((L,D),F32),sds((L,D),BF),sds((L,128),BF)]+[sds((4,)+pieces[0].shape,BF)]*2+[sds((16,D),F32),sds((1,FF),F32)]
+    row=pl.BlockSpec((RB,D),lambda i:(i,0))
+    outs=[sds((RB,D),BF)]*nt+[sds((L,D),F32),sds((L,D),BF),sds((L,128),BF)]+[sds((4,)+pieces[0].shape,BF)]*2+[sds((16,D),F32),sds((1,FF),F32)]
     return pl.pallas_call(kern,grid=(nb,),
-      in_specs=[smem(),smem(),row,blk]+[pl.BlockSpec((RB,a.shape[1]),lambda i:(i,0)) for a in atts]+[full(vec),full(upb)]+[anyw()]*len(flat_pieces),
-      out_specs=[blk,row,row,pl.BlockSpec((RB,128),lambda i:(i,0)),anyw(),anyw()]+[once(s) for s in outs[6:]],
+      in_specs=[smem(),smem(),row]+[anyw()]*nt+[pl.BlockSpec((RB,a.shape[1]),lambda i:(i,0)) for a in atts]+[full(vec),full(upb)]+[anyw()]*len(flat_pieces),
+      out_specs=[anyw()]*nt+[row,row,pl.BlockSpec((RB,128),lambda i:(i,0)),anyw(),anyw()]+[once(s) for s in outs[nt+5:]],
       out_shape=outs,
       scratch_shapes=[pltpu.VMEM((D,D),BF),pltpu.VMEM((FF,D),BF),pltpu.VMEM((D,FF),BF),
-        pltpu.VMEM((D,D),F32),pltpu.VMEM((FF,D),F32),pltpu.VMEM((D,FF),F32),
-        pltpu.VMEM((RB,FF),BF),pltpu.VMEM((RB,FF),F32),pltpu.SemaphoreType.DMA((4,))],
+        pltpu.VMEM((nt,RB,D),BF),pltpu.VMEM((nt,RB,D),BF)]+[pltpu.VMEM((L,D),BF)]*4+[pltpu.VMEM((L,FF),BF)]*2+[
+        pltpu.VMEM((RB,FF),F32),pltpu.SemaphoreType.DMA((4,))],
       compiler_params=pltpu.CompilerParams(vmem_limit_bytes=61*2**20),
       cost_estimate=pl.CostEstimate(flops=2*L*D*(3*D+6*FF),bytes_accessed=60_000_000,transcendentals=2*L*FF),
-      name="middle")(me,info,mixed,cot,*atts,vec,upb,*flat_pieces)
+      name="middle")(me,info,mixed,*cots,*atts,vec,upb,*flat_pieces)
 
 GROUPS=8
 AXES=("seq","stream")
@@ -603,8 +639,7 @@
     low,high,far,atts,cots=sync(low,high,far,atts,cots)
     diag=(low,high)
     p2=n2+[diag]+far+[tuple(flip(x,unit,total) for x in diag)]
-    cot=jnp.stack(cots)
-    output,ga,gatt,auxd,mine2,theirs2,dvec,dupb=sync(*middle(me,info,mixed,cot,atts,vec,upb,p2))
+    *output,ga,gatt,auxd,mine2,theirs2,dvec,dupb=sync(*middle(me,info,mixed,cots,atts,vec,upb,p2))
     grads=[]
     def backward(c,q):
         grads.append(attn_bwd(q,k,v,gatt,auxk,auxq[c],auxd,sum(parts[:c]),parts[c],0))
@@ -614,21 +649,21 @@
     got,q,output,backs,grads=sync(got,q,output,backs,grads)
     fx,fy,fd=(flip(x,g*unit,total) for x,g in zip(sum_three(mine2,got),(2,4,6)))
     backs+=[flip(output[c],c,total) for c in range(2,streams)]
-    backward(1,q)
+    out,*tg,rows4=attn_finish(me,info,(q,k,v,gatt,auxk,auxq[1],auxd),ga,pre,grads[0],p1,parts[0],parts[1],R)
+    grads.append(out)
     def place(chunks,dtype):
         out=jnp.zeros((seqs,R,D),dtype)
         for c,part in enumerate(chunks):
             out=lax.dynamic_update_index_in_dim(out,part.astype(dtype),s0^c,0)
         return out
-    *tg,rows4=token_grads(me,info,ga,pre,grads,p1,R)
     tg,rows4,backs=sync(tg,rows4,backs)
     held=[flip(tg[c],c,total) for c in range(1,streams-1)]
     mine1,theirs1=weight_grads(me,inputs,rows4,hid,feat,dvec,dupb,grads,unit)
-    mine1,theirs1,fx,fy,fd=sync(mine1,theirs1,fx,fy,fd)
+    mine1,theirs1,fx,fy,fd,held=sync(mine1,theirs1,fx,fy,fd,held)
     keep2,send2=sum_own(inner,mine2,got,(fx,fy,fd),((1,shard),(1,ff_shard),(FF//D,shard)),unit)
-    keep2,send2,theirs1,held,tg=sync(keep2,send2,theirs1,held,tg)
+    got1=flip(theirs1,unit,total)
+    keep2,send2,tg=sync(keep2,send2,tg)
     got2=flip(send2,1,total)
-    got1=flip(theirs1,unit,total)
     tgs=[tg[0]]+held+[flip(tg[streams-1],streams-1,total)]
     blocks=sum_three(mine1,got1)
     fx,fy,fd=(flip(x,g*unit,total) for x,g in zip(blocks,(2,4,6)))
@@ -636,9 +671,9 @@
     fx,fy,fd,keep2,got2,tgs=sync(fx,fy,fd,keep2,got2,tgs)
     output=place(backs,BF)
     dwo,dwd,dwu=last2(keep2,got2,shard,ff_shard,FF)
-    keep1,send1=sum_own(inner,mine1,got1,(fx,fy,fd),((4,shard),(1,SMALL)),unit)
-    keep1,got1=finish2(keep1,flip(send1,1,total),total)
-    dwq,dwk,dwv,dwe,dws,bq,bv,bo,ag,as_,bd,fg,fs,bs,be,bu=last1(keep1,got1,shard,stamp_rows,[shard]*10+[ff_shard])
+    keep1,*sends=sum_direct(inner,mine1,got1,(fx,fy,fd),((4,shard),(1,SMALL)),unit)
+    given=[keep1]+[flip(x,c+1,total) for c,x in enumerate(sends)]
+    dwq,dwk,dwv,dwe,dws,bq,bv,bo,ag,as_,bd,fg,fs,bs,be,bu=last1(given,shard,stamp_rows,[shard]*10+[ff_shard])
     token_grad=place(tgs,F32)
     return (output,token_grad,dwq,bq,dwk,dwv,bv,dwo,bo,ag,as_,dwu,bu,dwd,bd,fg,fs,dws,bs,dwe,be)
 

time: 352 us -> 338 us (0.960)
  Pallas kernels: 175 us -> 159 us
  waiting for transfers between devices: 82.1 us -> 89.9 us
  local copies, waits for them, and re-layouts: 23 us -> 16.4 us
    pallas_call x5, Pallas kernels: 110 us -> 101 us  [the longest x1 51.8 us: middle(): pl.pallas_call(kern, grid=(nb,), in_specs=[smem(), smem(), row] + [anyw()...]
    ppermute x44 -> x45, waiting for transfers between devices: 82.1 us -> 89.9 us  [flip(): return lax.ppermute(x, AXES, [(i, i ^ mask) for i in range(total)])]
    unnamed x68 -> x62, local copies, waits for them, and re-layouts: 9.21 us -> 4.42 us
    pallas_call x2 -> x1, Pallas kernels: 7.78 us -> 4.71 us  [sum_own(): pl.pallas_call(functools.partial(own_kernel, sizes, unit, len(more)), gri...]
    ppermute x44 -> x45, starting transfers between devices: 56.4 us -> 59 us  [flip(): return lax.ppermute(x, AXES, [(i, i ^ mask) for i in range(total)])]
  transfers between devices with their start and end apart: 44 -> 45, of which waited for: 17 -> 15; matrix products, arithmetic and copies ran while one was open for 6% -> 5% of each run, Pallas kernels for 31% -> 29%
where the time goes in v2:
time: 338 us; the launch traced here: 334 us
  Pallas kernels  159 us (47%)
  waiting for transfers between devices  89.9 us (27%)
  starting transfers between devices  59 us (17%)
  local copies, waits for them, and re-layouts  16.4 us (5%)
  other arithmetic  7.3 us (2%)
    ppermute x45, waiting for transfers between devices, flip(): return lax.ppermute(x, AXES, [(i, i ^ mask) for i in range(total)])  89.9 us
    ppermute x45, starting transfers between devices, flip(): return lax.ppermute(x, AXES, [(i, i ^ mask) for i in range(total)])  59 us
    pallas_call x1, Pallas kernels, middle(): pl.pallas_call(kern, grid=(nb,), in_specs=[smem(), smem(), row] + [anyw()...  51.8 us
    pallas_call x1, Pallas kernels, attn_finish(): pl.pallas_call(functools.partial(finish_kernel, p0, nt), grid=(np_,), in_...  33 us
    pallas_call x2, Pallas kernels, attn_fwd(): pl.pallas_call(fwd_kernel, grid=(np_,), in_specs=[col(), col(), col(), pl...  23.8 us
    pallas_call x1, Pallas kernels, attn_bwd(): pl.pallas_call(functools.partial(bwd_pair, p0), grid=(np_,), in_specs=ins...  14.6 us
    pallas_call x1, Pallas kernels, weight_grads(): pl.pallas_call(functools.partial(weight_kernel, nc, unit), grid=(L // R,)...  10.5 us
    pallas_call x1, Pallas kernels, project(): pl.pallas_call(functools.partial(in_kernel, nt, unit), grid=(nt,), in_spe...  9.57 us
  transfers between devices with their start and end apart: 45, of which 15 were waited for; matrix products, arithmetic and copies ran while one was open for 5% of the time, Pallas kernels for 29%

profile of v2, /device:TPU:0, one launch (start us, length us, event | category | flops | bytes accessed | tf_op | source)
XLA Modules:
  0.0 334.3 jit_solution(5963206767079993241)
XLA Ops:
  0.7 2.1 pack.1
  2.8 4.0 %collective-permute-start = (bf16[1,112,768]{2,1,0:T(8,128)(2,1)}, bf16[1,112,768]{2,1,0:T(8,128)(2,1)S(1)}, u32[]{:S(2)}, u32[]{:S(2)}) collective-permute-start(bf16[1,112,768]{2,1,0:T(8,128)(2,1)} %bitcast.67), channel_id=1, source_target_pairs={{0,2},{1,3},{2,0},{3,1},{4,6},{5,7},{6,4},{7,5},{8,10},{9,11},{10,... | collective-permute-start | bytes 516104 | tf_op jit(solution)/shard_map/ppermute | solution.py:539
  12.3 1.3 select_clamp_fusion
  13.7 2.3 dynamic-slice_bitcast_fusion.4
  16.7 3.2 collective-permute-start.1
  20.0 13.4 %collective-permute-done.2 = bf16[1,216,768]{2,1,0:T(8,128)(2,1)S(1)} collective-permute-done((bf16[1,216,768]{2,1,0:T(8,128)(2,1)S(1)}, bf16[1,216,768]{2,1,0:T(8,128)(2,1)S(1)}, u32[]{:S(2)}, u32[]{:S(2)}) %collective-permute-start.2) | collective-permute-done | bytes 331808 | tf_op jit(solution)/shard_map/ppermute | solution.py:539
  35.2 1.5 collective-permute-start.3
  36.7 1.5 collective-permute-start.4
  38.2 3.6 %collective-permute-start.5 = (bf16[256,768]{1,0:T(8,128)(2,1)S(1)}, bf16[256,768]{1,0:T(8,128)(2,1)S(1)}, u32[]{:S(2)}, u32[]{:S(2)}) collective-permute-start(bf16[256,768]{1,0:T(8,128)(2,1)S(1)} %get-tuple-element.172), channel_id=1, source_target_pairs={{0,2},{1,3},{2,0},{3,1},{4,6},{5,7},{6,4},{7,5},{8,10},{9,11},{10,... | collective-permute-start | bytes 1179656 | tf_op jit(solution)/shard_map/ppermute | solution.py:539
  42.3 16.6 %collective-permute-done.6 = bf16[2,216,768]{2,1,0:T(8,128)(2,1)S(1)} collective-permute-done((bf16[2,216,768]{2,1,0:T(8,128)(2,1)S(1)}, bf16[2,216,768]{2,1,0:T(8,128)(2,1)S(1)}, u32[]{:S(2)}, u32[]{:S(2)}) %collective-permute-start.6) | collective-permute-done | bytes 663584 | tf_op jit(solution)/shard_map/ppermute | solution.py:539
  59.1 3.1 collective-permute-start.8
  62.1 4.8 %collective-permute-done.4.rest_6_.rest_12_ = bf16[448,768]{1,0:T(8,128)(2,1)S(1)} collective-permute-done((bf16[448,768]{1,0:T(8,128)(2,1)S(1)}, bf16[448,768]{1,0:T(8,128)(2,1)S(1)}, u32[]{:S(2)}, u32[]{:S(2)}) %collective-permute-start.4) | collective-permute-done | bytes 688160 | tf_op jit(solution)/shard_map/ppermute | solution.py:539
  68.8 1.8 collective-permute-start.7
  70.6 2.0 collective-permute-done.8.rest_3_
  72.6 1.5 collective-permute-start.14
  74.1 1.5 collective-permute-start.15
  75.7 5.3 %collective-permute-done.7.rest_1_ = bf16[256,768]{1,0:T(8,128)(2,1)S(1)} collective-permute-done((bf16[256,768]{1,0:T(8,128)(2,1)S(1)}, bf16[256,768]{1,0:T(8,128)(2,1)S(1)}, u32[]{:S(2)}, u32[]{:S(2)}) %collective-permute-start.7) | collective-permute-done | bytes 393248 | tf_op jit(solution)/shard_map/ppermute | solution.py:539
  83.1 2.9 collective-permute-start.17
  86.1 2.2 collective-permute-start.18
  88.2 9.6 %project.1 = (f32[1024,768]{1,0:T(8,128)}, bf16[1024,768]{1,0:T(8,128)(2,1)}, bf16[1024,768]{1,0:T(8,128)(2,1)}, bf16[1024,768]{1,0:T(8,128)(2,1)}, bf16[1024,76...) custom-call(s32[1]{0:T(128)} %bitcast.me_ref, ...), custom_call_target="tpu_custom_call" | custom-call | flops 3623878656 | bytes 20000000 | tf_op jit(solution)/shard_map/project/pallas_call | solution.py:204
  97.8 8.7 %attn_fwd.2 = (bf16[1024,256]{1,0:T(8,128)(2,1)}, bf16[2,1024,128]{2,1,0:T(8,128)(2,1)}) custom-call(bf16[1024,768]{1,0:T(8,128)(2,1)} %get-tuple-element.222.q_ref.rest_0_, bf16[1024,768]{1,0:T(8,128)(2,1)} %get-tuple-element.186.k_ref.rest_1_, bf16[1024,768]{1,0:T(8,128)(2,1)} %get-tuple-element.187.v_ref.rest_2_, ...), custom_call_target="tpu_custom_call" | custom-call | flops 1073741824 | bytes 2621440 | tf_op jit(solution)/shard_map/attn_fwd/pallas_call | solution.py:51
  109.9 2.8 collective-permute-start.23
  112.7 15.2 %attn_fwd.3 = (bf16[1024,512]{1,0:T(8,128)(2,1)}, bf16[4,1024,128]{2,1,0:T(8,128)(2,1)}) custom-call(bf16[1024,768]{1,0:T(8,128)(2,1)} %get-tuple-element.222.q_ref.rest_0_, bf16[1024,768]{1,0:T(8,128)(2,1)} %get-tuple-element.186.k_ref.rest_1_, bf16[1024,768]{1,0:T(8,128)(2,1)} %get-tuple-element.187.v_ref.rest_2_, ...), custom_call_target="tpu_custom_call" | custom-call | flops 2147483648 | bytes 5242880 | tf_op jit(solution)/shard_map/attn_fwd/pallas_call | solution.py:51
  128.5 2.8 collective-permute-done.25.rest_17_
  132.4 51.8 %middle.1 = (bf16[256,768]{1,0:T(8,128)(2,1)}, bf16[256,768]{1,0:T(8,128)(2,1)}, bf16[256,768]{1,0:T(8,128)(2,1)}, bf16[256,768]{1,0:T(8,128)(2,1)}, f32[1024,76...) custom-call(s32[1]{0:T(128)} %bitcast.me_ref, ...), custom_call_target="tpu_custom_call" | custom-call | flops 32614907904 | bytes 60000000 | tf_op jit(solution)/shard_map/middle/pallas_call | solution.py:525
  184.4 3.9 %collective-permute-start.27 = (bf16[256,768]{1,0:T(8,128)(2,1)}, bf16[256,768]{1,0:T(8,128)(2,1)S(1)}, u32[]{:S(2)}, u32[]{:S(2)}) collective-permute-start(bf16[256,768]{1,0:T(8,128)(2,1)} %get-tuple-element.215), channel_id=1, source_target_pairs={{0,1},{1,0},{2,3},{3,2},{4,5},{5,4},{6,7},{7,6},{8,9},{9,8},{10,11... | collective-permute-start | bytes 1179656 | tf_op jit(solution)/shard_map/ppermute | solution.py:539
  188.3 14.6 %attn_bwd.1.rest_9_.rest_0_ = bf16[3,1024,256]{2,1,0:T(8,128)(2,1)} custom-call(bf16[1024,768]{1,0:T(8,128)(2,1)} %get-tuple-element.222.q_ref.rest_0_, bf16[1024,768]{1,0:T(8,128)(2,1)} %get-tuple-element.186.k_ref.rest_1_, bf16[1024,768]{1,0:T(8,128)(2,1)} %get-tuple-element.187.v_ref.rest_2_, bf16[1024,768]{1,0:T(8,128)(2,1)} %get-tuple-element.219.do_ref.rest_3_, ...), custom_call_target="tpu_custom_call" | custom-call | flops 2684354560 | bytes 4718592 | tf_op jit(solution)/shard_map/attn_bwd/pallas_call | solution.py:103
  202.9 5.2 %sum_three.2 = (bf16[864,768]{1,0:T(8,128)(2,1)}, bf16[864,768]{1,0:T(8,128)(2,1)}, bf16[864,768]{1,0:T(8,128)(2,1)}) custom-call(bf16[4,864,768]{2,1,0:T(8,128)(2,1)} %get-tuple-element.248.a1.a2.a3.a, bf16[4,864,768]{2,1,0:T(8,128)(2,1)} %collective-permute-done.26.b1.b2.b3.b, bf16[4,864,768]{2,1,0:T(8,128)(2,1)} %get-tuple-element.248.a1.a2.a3.a, ...), custom_call_target="tpu_custom_call" | custom-call | tf_op jit(solution)/shard_map/sum_three/pallas_call | solution.py:320
  208.1 1.6 collective-permute-start.30
  210.3 1.4 collective-permute-start.32
  212.6 1.5 collective-permute-start.29
  214.0 33.0 %attn_finish.1 = (bf16[3,1024,512]{2,1,0:T(8,128)(2,1)}, bf16[256,768]{1,0:T(8,128)(2,1)}, bf16[256,768]{1,0:T(8,128)(2,1)}, bf16[256,768]{1,0:T(8,128)(2,1)}, b...) custom-call(s32[1]{0:T(128)} %bitcast.me_ref, s32[4,2]{1,0:T(4,128)} %pad_add_fusion.info_ref, ...), custom_call_target="tpu_custom_call" | custom-call | flops 5368709120 | bytes 9437184 | tf_op jit(solution)/shard_map/attn_finish/pallas_call | solution.py:253
  247.0 1.6 collective-permute-start.33
  248.7 1.4 collective-permute-start.34
  250.0 10.5 %weight_grads.1 = (bf16[4,448,768]{2,1,0:T(8,128)(2,1)}, bf16[4,448,768]{2,1,0:T(8,128)(2,1)}) custom-call(s32[1]{0:T(128)} %bitcast.me_ref, bf16[1024,768]{1,0:T(8,128)(2,1)} %get-tuple-element.240.inp_ref, f32[8,768]{1,0:T(8,128)} %get-tuple-element.241.rows_ref, bf16[8,768]{1,0:T(8,128)(2,1)} %get-tuple-element.242.hid_ref, ...), custom_call_target="tpu_custom_call" | custom-call | flops 3623878656 | bytes 12000000 | tf_op jit(solution)/shard_map/weight_grads/pallas_call | solution.py:301
  260.5 6.0 %collective-permute-done.33 = bf16[256,768]{1,0:T(8,128)(2,1)} collective-permute-done((bf16[256,768]{1,0:T(8,128)(2,1)}, bf16[256,768]{1,0:T(8,128)(2,1)}, u32[]{:S(2)}, u32[]{:S(2)}) %collective-permute-start.33) | collective-permute-done | bytes 393248 | tf_op jit(solution)/shard_map/ppermute | solution.py:539
  266.5 2.6 collective-permute-done.34
  271.1 4.7 %sum_own.1 = (f32[2,216,768]{2,1,0:T(8,128)}, bf16[2,216,768]{2,1,0:T(8,128)(2,1)}) custom-call(s32[1]{0:T(128)} %bitcast.27.inner_ref, bf16[4,864,768]{2,1,0:T(8,128)(2,1)} %get-tuple-element.248.a1.a2.a3.a, bf16[4,864,768]{2,1,0:T(8,128)(2,1)} %collective-permute-done.26.b1.b2.b3.b, bf16[864,768]{1,0:T(8,128)(2,1)} %copy-done.4, ...), custom_call_target="tpu_custom_call" | custom-call | tf_op jit(solution)/shard_map/sum_own/pallas_call | solution.py:344
  278.2 2.3 collective-permute-start.41
  282.5 1.5 collective-permute-start.37
  285.2 7.8 %collective-permute-done.39 = bf16[2,216,768]{2,1,0:T(8,128)(2,1)S(1)} collective-permute-done((bf16[2,216,768]{2,1,0:T(8,128)(2,1)}, bf16[2,216,768]{2,1,0:T(8,128)(2,1)S(1)}, u32[]{:S(2)}, u32[]{:S(2)}) %collective-permute-start.39) | collective-permute-done | bytes 663584 | tf_op jit(solution)/shard_map/ppermute | solution.py:539
  293.3 1.7 collective-permute-start.40
  296.1 6.6 %collective-permute-done.41 = bf16[256,768]{1,0:T(8,128)(2,1)S(1)} collective-permute-done((bf16[256,768]{1,0:T(8,128)(2,1)S(1)}, bf16[256,768]{1,0:T(8,128)(2,1)S(1)}, u32[]{:S(2)}, u32[]{:S(2)}) %collective-permute-start.41) | collective-permute-done | bytes 393248 | tf_op jit(solution)/shard_map/ppermute | solution.py:539
  302.6 13.7 %collective-permute-done.40 = bf16[1,216,768]{2,1,0:T(8,128)(2,1)S(1)} collective-permute-done((bf16[1,216,768]{2,1,0:T(8,128)(2,1)S(1)}, bf16[1,216,768]{2,1,0:T(8,128)(2,1)S(1)}, u32[]{:S(2)}, u32[]{:S(2)}) %collective-permute-start.40) | collective-permute-done | bytes 331808 | tf_op jit(solution)/shard_map/ppermute | solution.py:539
  316.3 1.3 sum_direct.1
  317.7 2.1 collective-permute-start.43
  319.8 2.3 collective-permute-start.44
  326.5 6.8 %collective-permute-done.43.refs_2_ = bf16[112,768]{1,0:T(8,128)(2,1)S(1)} collective-permute-done((bf16[112,768]{1,0:T(8,128)(2,1)S(1)}, bf16[112,768]{1,0:T(8,128)(2,1)S(1)}, u32[]{:S(2)}, u32[]{:S(2)}) %collective-permute-start.43) | collective-permute-done | bytes 172064 | tf_op jit(solution)/shard_map/ppermute | solution.py:539
  (170 shorter events, 32.9 us)
Async XLA Ops:
  2.8 13.1 %collective-permute-start = (bf16[1,112,768]{2,1,0:T(8,128)(2,1)}, bf16[1,112,768]{2,1,0:T(8,128)(2,1)S(1)}, u32[]{:S(2)}, u32[]{:S(2)}) collective-permute-start(bf16[1,112,768]{2,1,0:T(8,128)(2,1)} %bitcast.67), channel_id=1, source_target_pairs={{0,2},{1,3},{2,0},{3,1},{4,6},{5,7},{6,4},{7,5},{8,10},{9,11},{10,... | collective-permute-start | bytes 516104 | tf_op jit(solution)/shard_map/ppermute | solution.py:539
  16.0 17.4 %collective-permute-start.2 = (bf16[1,216,768]{2,1,0:T(8,128)(2,1)S(1)}, bf16[1,216,768]{2,1,0:T(8,128)(2,1)S(1)}, u32[]{:S(2)}, u32[]{:S(2)}) collective-permute-start(bf16[1,216,768]{2,1,0:T(8,128)(2,1)S(1)} %bitcast.65), channel_id=1, source_target_pairs={{0,2},{1,3},{2,0},{3,1},{4,6},{5,7},{6,4},{7,5},{8,10},{9,11},{10,... | collective-permute-start | bytes 995336 | tf_op jit(solution)/shard_map/ppermute | solution.py:539
  16.7 17.2 %collective-permute-start.1 = (bf16[2,112,768]{2,1,0:T(8,128)(2,1)S(1)}, bf16[2,112,768]{2,1,0:T(8,128)(2,1)S(1)}, u32[]{:S(2)}, u32[]{:S(2)}) collective-permute-start(bf16[2,112,768]{2,1,0:T(8,128)(2,1)S(1)} %pad_maximum_fusion.4), channel_id=1, source_target_pairs={{0,1},{1,0},{2,3},{3,2},{4,5},{5,4},{6,7},{7,6},{8,9},{9,8},{10,11... | collective-permute-start | bytes 1032200 | tf_op jit(solution)/shard_map/ppermute | solution.py:539
  34.6 24.5 %copy-start.9 = (bf16[448,768]{1,0:T(8,128)(2,1)}, bf16[448,768]{1,0:T(8,128)(2,1)S(1)}, u32[]{:S(2)}) copy-start(bf16[448,768]{1,0:T(8,128)(2,1)S(1)} %pad_maximum_fusion.2.rest_4_.rest_10_) | copy-start | bytes 2064388
  35.2 23.7 %collective-permute-start.6 = (bf16[2,216,768]{2,1,0:T(8,128)(2,1)S(1)}, bf16[2,216,768]{2,1,0:T(8,128)(2,1)S(1)}, u32[]{:S(2)}, u32[]{:S(2)}) collective-permute-start(bf16[2,216,768]{2,1,0:T(8,128)(2,1)S(1)} %pad_maximum_fusion.3), channel_id=1, source_target_pairs={{0,1},{1,0},{2,3},{3,2},{4,5},{5,4},{6,7},{7,6},{8,9},{9,8},{10,11... | collective-permute-start | bytes 1990664 | tf_op jit(solution)/shard_map/ppermute | solution.py:539
  35.2 26.9 %collective-permute-start.3 = (bf16[448,768]{1,0:T(8,128)(2,1)S(1)}, bf16[448,768]{1,0:T(8,128)(2,1)S(1)}, u32[]{:S(2)}, u32[]{:S(2)}) collective-permute-start(bf16[448,768]{1,0:T(8,128)(2,1)S(1)} %pad_maximum_fusion.2.rest_4_.rest_10_), channel_id=1, source_target_pairs={{0,8},{1,9},{2,10},{3,11},{4,12},{5,13},{6,14},{7,15},{8,0},{9,1},... | collective-permute-start | bytes 2064392 | tf_op jit(solution)/shard_map/ppermute | solution.py:539
  36.7 30.3 %collective-permute-start.4 = (bf16[448,768]{1,0:T(8,128)(2,1)S(1)}, bf16[448,768]{1,0:T(8,128)(2,1)S(1)}, u32[]{:S(2)}, u32[]{:S(2)}) collective-permute-start(bf16[448,768]{1,0:T(8,128)(2,1)S(1)} %pad_maximum_fusion.2.rest_4_.rest_10_), channel_id=1, source_target_pairs={{0,16},{1,17},{2,18},{3,19},{4,20},{5,21},{6,22},{7,23},{8,24},{9,... | collective-permute-start | bytes 2064392 | tf_op jit(solution)/shard_map/ppermute | solution.py:539
  38.2 20.8 %collective-permute-start.5 = (bf16[256,768]{1,0:T(8,128)(2,1)S(1)}, bf16[256,768]{1,0:T(8,128)(2,1)S(1)}, u32[]{:S(2)}, u32[]{:S(2)}) collective-permute-start(bf16[256,768]{1,0:T(8,128)(2,1)S(1)} %get-tuple-element.172), channel_id=1, source_target_pairs={{0,2},{1,3},{2,0},{3,1},{4,6},{5,7},{6,4},{7,5},{8,10},{9,11},{10,... | collective-permute-start | bytes 1179656 | tf_op jit(solution)/shard_map/ppermute | solution.py:539
  41.8 32.3 %collective-permute-start.9 = (bf16[448,768]{1,0:T(8,128)(2,1)S(1)}, bf16[448,768]{1,0:T(8,128)(2,1)S(1)}, u32[]{:S(2)}, u32[]{:S(2)}) collective-permute-start(bf16[448,768]{1,0:T(8,128)(2,1)S(1)} %pad_maximum_fusion.2.rest_4_.rest_10_), channel_id=1, source_target_pairs={{0,24},{1,25},{2,26},{3,27},{4,28},{5,29},{6,30},{7,31},{8,16},{9,... | collective-permute-start | bytes 2064392 | tf_op jit(solution)/shard_map/ppermute | solution.py:539
  58.9 16.8 %collective-permute-start.10 = (bf16[448,768]{1,0:T(8,128)(2,1)S(1)}, bf16[448,768]{1,0:T(8,128)(2,1)S(1)}, u32[]{:S(2)}, u32[]{:S(2)}) collective-permute-start(bf16[448,768]{1,0:T(8,128)(2,1)S(1)} %pad_maximum_fusion.2.rest_4_.rest_10_), channel_id=1, source_target_pairs={{0,4},{1,5},{2,6},{3,7},{4,0},{5,1},{6,2},{7,3},{8,12},{9,13},{10,... | collective-permute-start | bytes 2064392 | tf_op jit(solution)/shard_map/ppermute | solution.py:539
  59.1 13.6 %collective-permute-start.8 = (bf16[256,768]{1,0:T(8,128)(2,1)S(1)}, bf16[256,768]{1,0:T(8,128)(2,1)S(1)}, u32[]{:S(2)}, u32[]{:S(2)}) collective-permute-start(bf16[256,768]{1,0:T(8,128)(2,1)S(1)} %get-tuple-element.177), channel_id=1, source_target_pairs={{0,3},{1,2},{2,1},{3,0},{4,7},{5,6},{6,5},{7,4},{8,11},{9,10},{10,... | collective-permute-start | bytes 1179656 | tf_op jit(solution)/shard_map/ppermute | solution.py:539
  67.5 13.7 %collective-permute-start.11 = (bf16[448,768]{1,0:T(8,128)(2,1)S(1)}, bf16[448,768]{1,0:T(8,128)(2,1)S(1)}, u32[]{:S(2)}, u32[]{:S(2)}) collective-permute-start(bf16[448,768]{1,0:T(8,128)(2,1)S(1)} %collective-permute-done.3.rest_5_.rest_11_), channel_id=1, source_target_pairs={{0,4},{1,5},{2,6},{3,7},{4,0},{5,1},{6,2},{7,3},{8,12},{9,13},{10,... | collective-permute-start | bytes 2064392 | tf_op jit(solution)/shard_map/ppermute | solution.py:539
  68.8 12.1 %collective-permute-start.7 = (bf16[256,768]{1,0:T(8,128)(2,1)S(1)}, bf16[256,768]{1,0:T(8,128)(2,1)S(1)}, u32[]{:S(2)}, u32[]{:S(2)}) collective-permute-start(bf16[256,768]{1,0:T(8,128)(2,1)S(1)} %get-tuple-element.175), channel_id=1, source_target_pairs={{0,1},{1,0},{2,3},{3,2},{4,5},{5,4},{6,7},{7,6},{8,9},{9,8},{10,11... | collective-permute-start | bytes 1179656 | tf_op jit(solution)/shard_map/ppermute | solution.py:539
  72.6 33.9 %collective-permute-start.14 = (bf16[864,768]{1,0:T(8,128)(2,1)S(1)}, bf16[864,768]{1,0:T(8,128)(2,1)}, u32[]{:S(2)}, u32[]{:S(2)}) collective-permute-start(bf16[864,768]{1,0:T(8,128)(2,1)S(1)} %pad_maximum_fusion.1.rest_8_), channel_id=1, source_target_pairs={{0,8},{1,9},{2,10},{3,11},{4,12},{5,13},{6,14},{7,15},{8,0},{9,1},... | collective-permute-start | bytes 3981320 | tf_op jit(solution)/shard_map/ppermute | solution.py:539
  74.1 32.4 %collective-permute-start.15 = (bf16[864,768]{1,0:T(8,128)(2,1)S(1)}, bf16[864,768]{1,0:T(8,128)(2,1)S(1)}, u32[]{:S(2)}, u32[]{:S(2)}) collective-permute-start(bf16[864,768]{1,0:T(8,128)(2,1)S(1)} %pad_maximum_fusion.1.rest_8_), channel_id=1, source_target_pairs={{0,16},{1,17},{2,18},{3,19},{4,20},{5,21},{6,22},{7,23},{8,24},{9,... | collective-permute-start | bytes 3981320 | tf_op jit(solution)/shard_map/ppermute | solution.py:539
  75.7 30.8 %collective-permute-start.16 = (bf16[864,768]{1,0:T(8,128)(2,1)S(1)}, bf16[864,768]{1,0:T(8,128)(2,1)}, u32[]{:S(2)}, u32[]{:S(2)}) collective-permute-start(bf16[864,768]{1,0:T(8,128)(2,1)S(1)} %pad_maximum_fusion.1.rest_8_), channel_id=1, source_target_pairs={{0,4},{1,5},{2,6},{3,7},{4,0},{5,1},{6,2},{7,3},{8,12},{9,13},{10,... | collective-permute-start | bytes 3981320 | tf_op jit(solution)/shard_map/ppermute | solution.py:539
  81.0 2.1 collective-permute-start.12
  81.2 4.9 %collective-permute-start.13 = (bf16[448,768]{1,0:T(8,128)(2,1)S(1)}, bf16[448,768]{1,0:T(8,128)(2,1)S(1)}, u32[]{:S(2)}, u32[]{:S(2)}) collective-permute-start(bf16[448,768]{1,0:T(8,128)(2,1)S(1)} %collective-permute-done.9.rest_7_.rest_13_), channel_id=1, source_target_pairs={{0,4},{1,5},{2,6},{3,7},{4,0},{5,1},{6,2},{7,3},{8,12},{9,13},{10,... | collective-permute-start | bytes 2064392 | tf_op jit(solution)/shard_map/ppermute | solution.py:539
  83.1 23.4 %collective-permute-start.17 = (bf16[256,768]{1,0:T(8,128)(2,1)S(1)}, bf16[256,768]{1,0:T(8,128)(2,1)}, u32[]{:S(2)}, u32[]{:S(2)}) collective-permute-start(bf16[256,768]{1,0:T(8,128)(2,1)S(1)} %get-tuple-element.183), channel_id=1, source_target_pairs={{0,1},{1,0},{2,3},{3,2},{4,5},{5,4},{6,7},{7,6},{8,9},{9,8},{10,11... | collective-permute-start | bytes 1179656 | tf_op jit(solution)/shard_map/ppermute | solution.py:539
  86.1 20.4 %collective-permute-start.18 = (bf16[256,768]{1,0:T(8,128)(2,1)S(1)}, bf16[256,768]{1,0:T(8,128)(2,1)}, u32[]{:S(2)}, u32[]{:S(2)}) collective-permute-start(bf16[256,768]{1,0:T(8,128)(2,1)S(1)} %get-tuple-element.184), channel_id=1, source_target_pairs={{0,2},{1,3},{2,0},{3,1},{4,6},{5,7},{6,4},{7,5},{8,10},{9,11},{10,... | collective-permute-start | bytes 1179656 | tf_op jit(solution)/shard_map/ppermute | solution.py:539
  106.5 21.4 %collective-permute-start.21 = (bf16[864,768]{1,0:T(8,128)(2,1)}, bf16[864,768]{1,0:T(8,128)(2,1)}, u32[]{:S(2)}, u32[]{:S(2)}) collective-permute-start(bf16[864,768]{1,0:T(8,128)(2,1)} %collective-permute-done.14.rest_9_), channel_id=1, source_target_pairs={{0,4},{1,5},{2,6},{3,7},{4,0},{5,1},{6,2},{7,3},{8,12},{9,13},{10,... | collective-permute-start | bytes 3981320 | tf_op jit(solution)/shard_map/ppermute | solution.py:539
  106.6 21.3 %collective-permute-start.22 = (bf16[864,768]{1,0:T(8,128)(2,1)S(1)}, bf16[864,768]{1,0:T(8,128)(2,1)}, u32[]{:S(2)}, u32[]{:S(2)}) collective-permute-start(bf16[864,768]{1,0:T(8,128)(2,1)S(1)} %collective-permute-done.15.rest_10_), channel_id=1, source_target_pairs={{0,4},{1,5},{2,6},{3,7},{4,0},{5,1},{6,2},{7,3},{8,12},{9,13},{10,... | collective-permute-start | bytes 3981320 | tf_op jit(solution)/shard_map/ppermute | solution.py:539
  107.2 20.7 %collective-permute-start.19 = (bf16[480,768]{1,0:T(8,128)(2,1)S(1)}, bf16[480,768]{1,0:T(8,128)(2,1)S(1)}, u32[]{:S(2)}, u32[]{:S(2)}) collective-permute-start(bf16[480,768]{1,0:T(8,128)(2,1)S(1)} %slice.89), channel_id=1, source_target_pairs={{0,8},{1,9},{2,10},{3,11},{4,12},{5,13},{6,14},{7,15},{8,0},{9,1},... | collective-permute-start | bytes 2211848 | tf_op jit(solution)/shard_map/ppermute | solution.py:539
  108.9 19.0 %collective-permute-start.20 = (bf16[384,768]{1,0:T(8,128)(2,1)S(1)}, bf16[384,768]{1,0:T(8,128)(2,1)}, u32[]{:S(2)}, u32[]{:S(2)}) collective-permute-start(bf16[384,768]{1,0:T(8,128)(2,1)S(1)} %slice.90), channel_id=1, source_target_pairs={{0,16},{1,17},{2,18},{3,19},{4,20},{5,21},{6,22},{7,23},{8,24},{9,... | collective-permute-start | bytes 1769480 | tf_op jit(solution)/shard_map/ppermute | solution.py:539
  109.9 18.0 %collective-permute-start.23 = (bf16[256,768]{1,0:T(8,128)(2,1)S(1)}, bf16[256,768]{1,0:T(8,128)(2,1)}, u32[]{:S(2)}, u32[]{:S(2)}) collective-permute-start(bf16[256,768]{1,0:T(8,128)(2,1)S(1)} %get-tuple-element.199), channel_id=1, source_target_pairs={{0,3},{1,2},{2,1},{3,0},{4,7},{5,6},{6,5},{7,4},{8,11},{9,10},{10,... | collective-permute-start | bytes 1179656 | tf_op jit(solution)/shard_map/ppermute | solution.py:539
  127.9 3.3 collective-permute-start.24
  128.0 3.3 collective-permute-start.25
  184.2 18.7 %collective-permute-start.26 = (bf16[4,864,768]{2,1,0:T(8,128)(2,1)}, bf16[4,864,768]{2,1,0:T(8,128)(2,1)}, u32[]{:S(2)}, u32[]{:S(2)}) collective-permute-start(bf16[4,864,768]{2,1,0:T(8,128)(2,1)} %get-tuple-element.214), channel_id=1, source_target_pairs={{0,4},{1,5},{2,6},{3,7},{4,0},{5,1},{6,2},{7,3},{8,12},{9,13},{10,... | collective-permute-start | bytes 15925256 | tf_op jit(solution)/shard_map/ppermute | solution.py:539
  184.4 18.5 %collective-permute-start.27 = (bf16[256,768]{1,0:T(8,128)(2,1)}, bf16[256,768]{1,0:T(8,128)(2,1)S(1)}, u32[]{:S(2)}, u32[]{:S(2)}) collective-permute-start(bf16[256,768]{1,0:T(8,128)(2,1)} %get-tuple-element.215), channel_id=1, source_target_pairs={{0,1},{1,0},{2,3},{3,2},{4,5},{5,4},{6,7},{7,6},{8,9},{9,8},{10,11... | collective-permute-start | bytes 1179656 | tf_op jit(solution)/shard_map/ppermute | solution.py:539
  208.1 61.0 %collective-permute-start.30 = (bf16[864,768]{1,0:T(8,128)(2,1)}, bf16[864,768]{1,0:T(8,128)(2,1)S(1)}, u32[]{:S(2)}, u32[]{:S(2)}) collective-permute-start(bf16[864,768]{1,0:T(8,128)(2,1)} %get-tuple-element.250), channel_id=1, source_target_pairs={{0,8},{1,9},{2,10},{3,11},{4,12},{5,13},{6,14},{7,15},{8,0},{9,1},... | collective-permute-start | bytes 3981320 | tf_op jit(solution)/shard_map/ppermute | solution.py:539
  209.7 59.5 %collective-permute-start.31 = (bf16[864,768]{1,0:T(8,128)(2,1)}, bf16[864,768]{1,0:T(8,128)(2,1)S(1)}, u32[]{:S(2)}, u32[]{:S(2)}) collective-permute-start(bf16[864,768]{1,0:T(8,128)(2,1)} %get-tuple-element.251), channel_id=1, source_target_pairs={{0,16},{1,17},{2,18},{3,19},{4,20},{5,21},{6,22},{7,23},{8,24},{9,... | collective-permute-start | bytes 3981320 | tf_op jit(solution)/shard_map/ppermute | solution.py:539
  210.3 58.9 %collective-permute-start.32 = (bf16[864,768]{1,0:T(8,128)(2,1)}, bf16[864,768]{1,0:T(8,128)(2,1)S(1)}, u32[]{:S(2)}, u32[]{:S(2)}) collective-permute-start(bf16[864,768]{1,0:T(8,128)(2,1)} %get-tuple-element.252), channel_id=1, source_target_pairs={{0,24},{1,25},{2,26},{3,27},{4,28},{5,29},{6,30},{7,31},{8,16},{9,... | collective-permute-start | bytes 3981320 | tf_op jit(solution)/shard_map/ppermute | solution.py:539
  211.6 35.4 %collective-permute-start.28 = (bf16[256,768]{1,0:T(8,128)(2,1)}, bf16[256,768]{1,0:T(8,128)(2,1)}, u32[]{:S(2)}, u32[]{:S(2)}) collective-permute-start(bf16[256,768]{1,0:T(8,128)(2,1)} %get-tuple-element.234), channel_id=1, source_target_pairs={{0,2},{1,3},{2,0},{3,1},{4,6},{5,7},{6,4},{7,5},{8,10},{9,11},{10,... | collective-permute-start | bytes 1179656 | tf_op jit(solution)/shard_map/ppermute | solution.py:539
  212.6 34.5 %collective-permute-start.29 = (bf16[256,768]{1,0:T(8,128)(2,1)}, bf16[256,768]{1,0:T(8,128)(2,1)}, u32[]{:S(2)}, u32[]{:S(2)}) collective-permute-start(bf16[256,768]{1,0:T(8,128)(2,1)} %get-tuple-element.235), channel_id=1, source_target_pairs={{0,3},{1,2},{2,1},{3,0},{4,7},{5,6},{6,5},{7,4},{8,11},{9,10},{10,... | collective-permute-start | bytes 1179656 | tf_op jit(solution)/shard_map/ppermute | solution.py:539
  247.0 19.5 %collective-permute-start.33 = (bf16[256,768]{1,0:T(8,128)(2,1)}, bf16[256,768]{1,0:T(8,128)(2,1)}, u32[]{:S(2)}, u32[]{:S(2)}) collective-permute-start(bf16[256,768]{1,0:T(8,128)(2,1)} %get-tuple-element.253), channel_id=1, source_target_pairs={{0,1},{1,0},{2,3},{3,2},{4,5},{5,4},{6,7},{7,6},{8,9},{9,8},{10,11... | collective-permute-start | bytes 1179656 | tf_op jit(solution)/shard_map/ppermute | solution.py:539
  248.7 20.4 %collective-permute-start.34 = (bf16[256,768]{1,0:T(8,128)(2,1)}, bf16[256,768]{1,0:T(8,128)(2,1)}, u32[]{:S(2)}, u32[]{:S(2)}) collective-permute-start(bf16[256,768]{1,0:T(8,128)(2,1)} %get-tuple-element.254), channel_id=1, source_target_pairs={{0,2},{1,3},{2,0},{3,1},{4,6},{5,7},{6,4},{7,5},{8,10},{9,11},{10,... | collective-permute-start | bytes 1179656 | tf_op jit(solution)/shard_map/ppermute | solution.py:539
  270.7 9.7 %collective-permute-start.35 = (bf16[4,448,768]{2,1,0:T(8,128)(2,1)}, bf16[4,448,768]{2,1,0:T(8,128)(2,1)S(1)}, u32[]{:S(2)}, u32[]{:S(2)}) collective-permute-start(bf16[4,448,768]{2,1,0:T(8,128)(2,1)} %get-tuple-element.256), channel_id=1, source_target_pairs={{0,4},{1,5},{2,6},{3,7},{4,0},{5,1},{6,2},{7,3},{8,12},{9,13},{10,... | collective-permute-start | bytes 8257544 | tf_op jit(solution)/shard_map/ppermute | solution.py:539
  275.8 17.2 %collective-permute-start.39 = (bf16[2,216,768]{2,1,0:T(8,128)(2,1)}, bf16[2,216,768]{2,1,0:T(8,128)(2,1)S(1)}, u32[]{:S(2)}, u32[]{:S(2)}) collective-permute-start(bf16[2,216,768]{2,1,0:T(8,128)(2,1)} %get-tuple-element.268), channel_id=1, source_target_pairs={{0,1},{1,0},{2,3},{3,2},{4,5},{5,4},{6,7},{7,6},{8,9},{9,8},{10,11... | collective-permute-start | bytes 1990664 | tf_op jit(solution)/shard_map/ppermute | solution.py:539
  278.2 14.9 %copy-start.7 = (f32[2,216,768]{2,1,0:T(8,128)S(1)}, f32[2,216,768]{2,1,0:T(8,128)}, u32[]{:S(2)}) copy-start(f32[2,216,768]{2,1,0:T(8,128)} %get-tuple-element.267) | copy-start | bytes 3981316
  278.2 24.5 %collective-permute-start.41 = (bf16[256,768]{1,0:T(8,128)(2,1)S(1)}, bf16[256,768]{1,0:T(8,128)(2,1)S(1)}, u32[]{:S(2)}, u32[]{:S(2)}) collective-permute-start(bf16[256,768]{1,0:T(8,128)(2,1)S(1)} %copy-done.27), channel_id=1, source_target_pairs={{0,3},{1,2},{2,1},{3,0},{4,7},{5,6},{6,5},{7,4},{8,11},{9,10},{10,... | collective-permute-start | bytes 1179656 | tf_op jit(solution)/shard_map/ppermute | solution.py:539
  281.6 34.7 %collective-permute-start.36 = (bf16[448,768]{1,0:T(8,128)(2,1)S(1)}, bf16[448,768]{1,0:T(8,128)(2,1)S(1)}, u32[]{:S(2)}, u32[]{:S(2)}) collective-permute-start(bf16[448,768]{1,0:T(8,128)(2,1)S(1)} %get-tuple-element.257), channel_id=1, source_target_pairs={{0,8},{1,9},{2,10},{3,11},{4,12},{5,13},{6,14},{7,15},{8,0},{9,1},... | collective-permute-start | bytes 2064392 | tf_op jit(solution)/shard_map/ppermute | solution.py:539
  282.5 33.8 %collective-permute-start.37 = (bf16[448,768]{1,0:T(8,128)(2,1)S(1)}, bf16[448,768]{1,0:T(8,128)(2,1)S(1)}, u32[]{:S(2)}, u32[]{:S(2)}) collective-permute-start(bf16[448,768]{1,0:T(8,128)(2,1)S(1)} %get-tuple-element.258), channel_id=1, source_target_pairs={{0,16},{1,17},{2,18},{3,19},{4,20},{5,21},{6,22},{7,23},{8,24},{9,... | collective-permute-start | bytes 2064392 | tf_op jit(solution)/shard_map/ppermute | solution.py:539
  284.0 32.3 %collective-permute-start.38 = (bf16[448,768]{1,0:T(8,128)(2,1)S(1)}, bf16[448,768]{1,0:T(8,128)(2,1)S(1)}, u32[]{:S(2)}, u32[]{:S(2)}) collective-permute-start(bf16[448,768]{1,0:T(8,128)(2,1)S(1)} %get-tuple-element.259), channel_id=1, source_target_pairs={{0,24},{1,25},{2,26},{3,27},{4,28},{5,29},{6,30},{7,31},{8,16},{9,... | collective-permute-start | bytes 2064392 | tf_op jit(solution)/shard_map/ppermute | solution.py:539
  293.3 23.0 %collective-permute-start.40 = (bf16[1,216,768]{2,1,0:T(8,128)(2,1)S(1)}, bf16[1,216,768]{2,1,0:T(8,128)(2,1)S(1)}, u32[]{:S(2)}, u32[]{:S(2)}) collective-permute-start(bf16[1,216,768]{2,1,0:T(8,128)(2,1)S(1)} %slice.108), channel_id=1, source_target_pairs={{0,2},{1,3},{2,0},{3,1},{4,6},{5,7},{6,4},{7,5},{8,10},{9,11},{10,... | collective-permute-start | bytes 995336 | tf_op jit(solution)/shard_map/ppermute | solution.py:539
  296.0 21.6 %copy-start.2 = (bf16[4,256,768]{2,1,0:T(8,128)(2,1)}, bf16[4,256,768]{2,1,0:T(8,128)(2,1)S(1)}, u32[]{:S(2)}) copy-start(bf16[4,256,768]{2,1,0:T(8,128)(2,1)S(1)} %bitcast_dynamic-update-slice_fusion) | copy-start | bytes 4718596
  317.6 8.9 %collective-permute-start.42 = (bf16[112,768]{1,0:T(8,128)(2,1)S(1)}, bf16[112,768]{1,0:T(8,128)(2,1)S(1)}, u32[]{:S(2)}, u32[]{:S(2)}) collective-permute-start(bf16[112,768]{1,0:T(8,128)(2,1)S(1)} %get-tuple-element.281), channel_id=1, source_target_pairs={{0,1},{1,0},{2,3},{3,2},{4,5},{5,4},{6,7},{7,6},{8,9},{9,8},{10,11... | collective-permute-start | bytes 516104 | tf_op jit(solution)/shard_map/ppermute | solution.py:539
  317.7 15.6 %collective-permute-start.43 = (bf16[112,768]{1,0:T(8,128)(2,1)S(1)}, bf16[112,768]{1,0:T(8,128)(2,1)S(1)}, u32[]{:S(2)}, u32[]{:S(2)}) collective-permute-start(bf16[112,768]{1,0:T(8,128)(2,1)S(1)} %get-tuple-element.282), channel_id=1, source_target_pairs={{0,2},{1,3},{2,0},{3,1},{4,6},{5,7},{6,4},{7,5},{8,10},{9,11},{10,... | collective-permute-start | bytes 516104 | tf_op jit(solution)/shard_map/ppermute | solution.py:539
  319.8 13.5 %collective-permute-start.44 = (bf16[112,768]{1,0:T(8,128)(2,1)S(1)}, bf16[112,768]{1,0:T(8,128)(2,1)S(1)}, u32[]{:S(2)}, u32[]{:S(2)}) collective-permute-start(bf16[112,768]{1,0:T(8,128)(2,1)S(1)} %get-tuple-element.283), channel_id=1, source_target_pairs={{0,3},{1,2},{2,1},{3,0},{4,7},{5,6},{6,5},{7,4},{8,11},{9,10},{10,... | collective-permute-start | bytes 516104 | tf_op jit(solution)/shard_map/ppermute | solution.py:539
  (28 other events, 138.6 us)

commit v3 on v2

--- a/solution.py
+++ b/solution.py
@@ -216,32 +216,37 @@
     return jnp.where(r==0,hi,jnp.where(r==1,mid,jnp.where(r==2,lo,0.0))).astype(BF)
 def three(rows):
     r=lax.broadcasted_iota(jnp.int32,rows.shape,0)
-    return jnp.where(r<3,jnp.broadcast_to(rows[0:1,:].astype(F32),rows.shape),0.0).astype(BF)
+    return jnp.where(r<3,jnp.broadcast_to(rows.astype(F32)[0:1,:],rows.shape),0.0).astype(BF)
 def finish_kernel(p0,nt,me_ref,info_ref,*rest):
     att=rest[:7]; ga_hbm,pre_ref,first=rest[7:10]; pieces=rest[10:18]
     out_ref=rest[18]; tg_refs=rest[19:19+nt]; rows_ref=rest[19+nt]
-    *work,ga,all_grads,wq,wk,wv,we,sems=rest[20+nt:]
+    *work,ga,all_grads,wqkv,we,sems=rest[20+nt:]
     i=pl.program_id(0); me=me_ref[0]
     L,D=ga.shape; n=D//8; F=first.shape[2]
-    cps=[pltpu.make_async_copy(first,all_grads.at[:,:,pl.ds(0,F)],sems.at[0]),pltpu.make_async_copy(ga_hbm,ga,sems.at[0])]
-    for w,dst in enumerate((wq,wk,wv,we)): cps+=load_weights(me,pieces,w*n,n,dst,sems.at[0])
+    cps=[pltpu.make_async_copy(ga_hbm,ga,sems.at[0])]
+    for w in range(3):
+        cps.append(pltpu.make_async_copy(first.at[w],all_grads.at[:,pl.ds(w*D,F)],sems.at[0]))
+        cps+=load_weights(me,pieces,w*n,n,wqkv.at[:,pl.ds(w*D,D)],sems.at[0])
+    cps+=load_weights(me,pieces,3*n,n,we,sems.at[0])
     @pl.when(i==0)
     def _():
         for c in cps: c.start()
     bwd_pair(p0,*att,out_ref,*work)
-    all_grads[:,:,pl.ds(pl.multiple_of(F+i*128,128),128)]=out_ref[...]
+    for w in range(3): all_grads[:,pl.ds(pl.multiple_of(w*D+F+i*128,128),128)]=out_ref[w]
     @pl.when(i==pl.num_programs(0)-1)
     def _():
         for c in cps: c.wait()
         rows_ref[...]=jnp.zeros_like(rows_ref)
-        R=L//nt
-        for c in range(nt):
-            r=pl.ds(c*R,R)
-            y=[all_grads[w,r,:] for w in range(3)]
-            for w in (0,2): rows_ref[pl.ds(w//2,1),:]+=jnp.sum(y[w].astype(F32),axis=0,keepdims=True)
-            g=ga[r,:]+(mm(y[0],wq[...],NT)+mm(y[1],wk[...],NT)+mm(y[2],wv[...],NT))
-            rows_ref[pl.ds(3,1),:]+=info_ref[c,0].astype(F32)*jnp.sum(g,axis=0,keepdims=True)
-            tg_refs[c][...]=g.astype(BF)
+        R=L//nt; per=max(1,MROWS//R)
+        for c in range(0,nt,per):
+            r=pl.ds(c*R,per*R)
+            y=all_grads[r,:]
+            for w in (0,2): rows_ref[pl.ds(w//2,1),:]+=jnp.sum(y[:,w*D:(w+1)*D].astype(F32),axis=0,keepdims=True)
+            g=ga[r,:]+mm(y,wqkv[...],NT)
+            for p in range(per):
+                part=g[p*R:(p+1)*R]
+                rows_ref[pl.ds(3,1),:]+=info_ref[c+p,0].astype(F32)*jnp.sum(part,axis=0,keepdims=True)
+                tg_refs[c+p][...]=part.astype(BF)
         gh=jnp.sum(mm(spread3(rows_ref[pl.ds(3,1),:]),we[...],NT),axis=0,keepdims=True)
         pre=pre_ref[0:1,:]
         sg=1.0/(1.0+jnp.exp(-pre))
@@ -253,11 +258,12 @@
     return pl.pallas_call(functools.partial(finish_kernel,p0,nt),grid=(np_,),
       in_specs=[smem(),smem()]+ins+[anyw(),pl.BlockSpec((8,D),lambda i:(0,0)),anyw()]+[anyw()]*8,
       out_specs=[pl.BlockSpec((3,L,128),lambda p:(0,0,p))]+[once(o) for o in outs[1:]],out_shape=outs,
-      scratch_shapes=scratch+[pltpu.VMEM((L,D),F32),pltpu.VMEM((3,L,D),BF)]+[pltpu.VMEM((D,D),BF)]*4+[pltpu.SemaphoreType.DMA((1,))],
+      scratch_shapes=scratch+[pltpu.VMEM((L,D),F32),pltpu.VMEM((L,3*D),BF),pltpu.VMEM((D,3*D),BF),pltpu.VMEM((D,D),BF)]+[pltpu.SemaphoreType.DMA((1,))],
       compiler_params=pltpu.CompilerParams(vmem_limit_bytes=60*2**20),
       cost_estimate=bwd_cost(L,np_),
       name="attn_finish")(me,info,*att,ga,pre,first,*pieces)
 STEP=1024
+MROWS=512
 def weight_kernel(nc,unit,me_ref,inp_ref,rows_ref,hid_ref,feat_ref,dvec_ref,dupb_ref,*rest):
     grads=rest[:nc]
     mine_ref,theirs_ref,acc=rest[nc:]
@@ -319,18 +325,19 @@
     _,R,D=mine.shape
     return pl.pallas_call(three_kernel,grid=(D//LB,),in_specs=[take(1,R)]*2+[take(2,R)]*2+[take(3,R)]*2,
       out_specs=[flat(R)]*3,out_shape=[sds((R,D),BF)]*3,compiler_params=pltpu.CompilerParams(vmem_limit_bytes=room(R)),name="sum_three")(mine,got,mine,got,mine,got)
+def inner_rows(scr,tmp,sizes,unit,k):
+    at=0; out=0
+    for count,size in sizes:
+        for c in range(count):
+            tmp[out:out+size,:]=scr[pl.ds(pl.multiple_of(at+k*size,8),size),:]
+            at+=unit*size; out+=size
+    return tmp[...]
 def own_kernel(sizes,unit,nx,inner_ref,a,b,*rest):
-    more=rest[:nx]; keep,send,scr=rest[nx:]
-    inner=inner_ref[0]
+    more=rest[:nx]; keep,send,scr,tmp=rest[nx:]
     scr[...]=total_of((a[0],b[0])+tuple(x[...] for x in more))
     for j in range(unit):
-        k=jnp.bitwise_xor(inner,j); at=0; out=0
-        for count,size in sizes:
-            for c in range(count):
-                x=scr[pl.ds(pl.multiple_of(at+k*size,8),size),:]
-                if j%2: send[j//2,out:out+size,:]=x.astype(BF)
-                else: keep[j//2,out:out+size,:]=x
-                at+=unit*size; out+=size
+        dst=send if j%2 else keep
+        dst[j//2]=inner_rows(scr,tmp,sizes,unit,jnp.bitwise_xor(inner_ref[0],j)).astype(dst.dtype)
 def sum_own(inner,mine,got,more,sizes,unit):
     _,R,D=mine.shape; rows=R//unit
     if any(size%8 for _,size in sizes):
@@ -343,18 +350,13 @@
     blk=pl.BlockSpec((unit//2,rows,LB),lambda i:(0,0,i))
     keep,send=pl.pallas_call(functools.partial(own_kernel,sizes,unit,len(more)),grid=(D//LB,),
       in_specs=[smem()]+[take(0,R)]*2+[flat(R)]*len(more),out_specs=[blk]*2,
-      out_shape=[sds((unit//2,rows,D),F32),sds((unit//2,rows,D),BF)],scratch_shapes=[pltpu.VMEM((R,LB),F32)],compiler_params=pltpu.CompilerParams(vmem_limit_bytes=room(R)),name="sum_own")(inner.reshape(1).astype(jnp.int32),mine,got,*more)
+      out_shape=[sds((unit//2,rows,D),F32),sds((unit//2,rows,D),BF)],scratch_shapes=[pltpu.VMEM((R,LB),F32),pltpu.VMEM((rows,LB),F32)],compiler_params=pltpu.CompilerParams(vmem_limit_bytes=room(R)),name="sum_own")(inner.reshape(1).astype(jnp.int32),mine,got,*more)
     return keep,send
 def direct_kernel(sizes,unit,nx,inner_ref,a,b,*rest):
-    more=rest[:nx]; outs=rest[nx:nx+unit]; scr=rest[nx+unit]
-    inner=inner_ref[0]
+    more=rest[:nx]; outs=rest[nx:nx+unit]; scr,tmp=rest[nx+unit:]
     scr[...]=total_of((a[0],b[0])+tuple(x[...] for x in more))
     for j,dst in enumerate(outs):
-        k=jnp.bitwise_xor(inner,j); at=0; out=0
-        for count,size in sizes:
-            for c in range(count):
-                dst[out:out+size,:]=scr[pl.ds(pl.multiple_of(at+k*size,8),size),:].astype(dst.dtype)
-                at+=unit*size; out+=size
+        dst[...]=inner_rows(scr,tmp,sizes,unit,jnp.bitwise_xor(inner_ref[0],j)).astype(dst.dtype)
 def sum_direct(inner,mine,got,more,sizes,unit):
     _,R,D=mine.shape; rows=R//unit
     if any(size%8 for _,size in sizes):
@@ -366,7 +368,7 @@
         return [x[0]]+[x[j].astype(BF) for j in range(1,unit)]
     return pl.pallas_call(functools.partial(direct_kernel,sizes,unit,len(more)),grid=(D//LB,),
       in_specs=[smem()]+[take(0,R)]*2+[flat(R)]*len(more),out_specs=[flat(rows)]*unit,
-      out_shape=[sds((rows,D),F32)]+[sds((rows,D),BF)]*(unit-1),scratch_shapes=[pltpu.VMEM((R,LB),F32)],
+      out_shape=[sds((rows,D),F32)]+[sds((rows,D),BF)]*(unit-1),scratch_shapes=[pltpu.VMEM((R,LB),F32),pltpu.VMEM((rows,LB),F32)],
       compiler_params=pltpu.CompilerParams(vmem_limit_bytes=room(R)),name="sum_direct")(inner.reshape(1).astype(jnp.int32),mine,got,*more)
 def last1_kernel(ng,*refs):
     x=total_of([r[...] for r in refs[:ng]]); outs=refs[ng:]

time: 338 us -> 338 us (level)
  no operation moved by 1% of the time
where the time goes in v3:
time: 338 us; the launch traced here: 334 us
  Pallas kernels  159 us (47%)
  waiting for transfers between devices  90.2 us (27%)
  starting transfers between devices  59 us (17%)
  local copies, waits for them, and re-layouts  16.4 us (5%)
  other arithmetic  7.3 us (2%)
    ppermute x45, waiting for transfers between devices, flip(): return lax.ppermute(x, AXES, [(i, i ^ mask) for i in range(total)])  90.2 us
    ppermute x45, starting transfers between devices, flip(): return lax.ppermute(x, AXES, [(i, i ^ mask) for i in range(total)])  59 us
    pallas_call x1, Pallas kernels, middle(): pl.pallas_call(kern, grid=(nb,), in_specs=[smem(), smem(), row] + [anyw()...  51.8 us
    pallas_call x1, Pallas kernels, attn_finish(): pl.pallas_call(functools.partial(finish_kernel, p0, nt), grid=(np_,), in_...  32.7 us
    pallas_call x2, Pallas kernels, attn_fwd(): pl.pallas_call(fwd_kernel, grid=(np_,), in_specs=[col(), col(), col(), pl...  23.8 us
    pallas_call x1, Pallas kernels, attn_bwd(): pl.pallas_call(functools.partial(bwd_pair, p0), grid=(np_,), in_specs=ins...  14.6 us
    pallas_call x1, Pallas kernels, weight_grads(): pl.pallas_call(functools.partial(weight_kernel, nc, unit), grid=(L // R,)...  10.5 us
    pallas_call x1, Pallas kernels, project(): pl.pallas_call(functools.partial(in_kernel, nt, unit), grid=(nt,), in_spe...  9.57 us
  transfers between devices with their start and end apart: 45, of which 15 were waited for; matrix products, arithmetic and copies ran while one was open for 5% of the time, Pallas kernels for 29%

profile of v3, /device:TPU:0, one launch (start us, length us, event | category | flops | bytes accessed | tf_op | source)
XLA Modules:
  0.0 334.3 jit_solution(16001734951765457542)
XLA Ops:
  0.7 2.1 pack.1
  2.8 4.0 %collective-permute-start = (bf16[1,112,768]{2,1,0:T(8,128)(2,1)}, bf16[1,112,768]{2,1,0:T(8,128)(2,1)S(1)}, u32[]{:S(2)}, u32[]{:S(2)}) collective-permute-start(bf16[1,112,768]{2,1,0:T(8,128)(2,1)} %bitcast.67), channel_id=1, source_target_pairs={{0,2},{1,3},{2,0},{3,1},{4,6},{5,7},{6,4},{7,5},{8,10},{9,11},{10,... | collective-permute-start | bytes 516104 | tf_op jit(solution)/shard_map/ppermute | solution.py:541
  12.3 1.3 select_clamp_fusion
  13.7 2.3 dynamic-slice_bitcast_fusion.4
  16.7 3.2 collective-permute-start.1
  20.0 13.4 %collective-permute-done.2 = bf16[1,216,768]{2,1,0:T(8,128)(2,1)S(1)} collective-permute-done((bf16[1,216,768]{2,1,0:T(8,128)(2,1)S(1)}, bf16[1,216,768]{2,1,0:T(8,128)(2,1)S(1)}, u32[]{:S(2)}, u32[]{:S(2)}) %collective-permute-start.2) | collective-permute-done | bytes 331808 | tf_op jit(solution)/shard_map/ppermute | solution.py:541
  35.2 1.5 collective-permute-start.3
  36.7 1.5 collective-permute-start.4
  38.2 3.6 %collective-permute-start.5 = (bf16[256,768]{1,0:T(8,128)(2,1)S(1)}, bf16[256,768]{1,0:T(8,128)(2,1)S(1)}, u32[]{:S(2)}, u32[]{:S(2)}) collective-permute-start(bf16[256,768]{1,0:T(8,128)(2,1)S(1)} %get-tuple-element.172), channel_id=1, source_target_pairs={{0,2},{1,3},{2,0},{3,1},{4,6},{5,7},{6,4},{7,5},{8,10},{9,11},{10,... | collective-permute-start | bytes 1179656 | tf_op jit(solution)/shard_map/ppermute | solution.py:541
  42.3 16.6 %collective-permute-done.6 = bf16[2,216,768]{2,1,0:T(8,128)(2,1)S(1)} collective-permute-done((bf16[2,216,768]{2,1,0:T(8,128)(2,1)S(1)}, bf16[2,216,768]{2,1,0:T(8,128)(2,1)S(1)}, u32[]{:S(2)}, u32[]{:S(2)}) %collective-permute-start.6) | collective-permute-done | bytes 663584 | tf_op jit(solution)/shard_map/ppermute | solution.py:541
  59.1 3.1 collective-permute-start.8
  62.1 4.8 %collective-permute-done.4.rest_6_.rest_12_ = bf16[448,768]{1,0:T(8,128)(2,1)S(1)} collective-permute-done((bf16[448,768]{1,0:T(8,128)(2,1)S(1)}, bf16[448,768]{1,0:T(8,128)(2,1)S(1)}, u32[]{:S(2)}, u32[]{:S(2)}) %collective-permute-start.4) | collective-permute-done | bytes 688160 | tf_op jit(solution)/shard_map/ppermute | solution.py:541
  68.8 1.8 collective-permute-start.7
  70.6 2.0 collective-permute-done.8.rest_3_
  72.6 1.5 collective-permute-start.14
  74.1 1.5 collective-permute-start.15
  75.7 5.3 %collective-permute-done.7.rest_1_ = bf16[256,768]{1,0:T(8,128)(2,1)S(1)} collective-permute-done((bf16[256,768]{1,0:T(8,128)(2,1)S(1)}, bf16[256,768]{1,0:T(8,128)(2,1)S(1)}, u32[]{:S(2)}, u32[]{:S(2)}) %collective-permute-start.7) | collective-permute-done | bytes 393248 | tf_op jit(solution)/shard_map/ppermute | solution.py:541
  83.1 2.9 collective-permute-start.17
  86.1 2.2 collective-permute-start.18
  88.2 9.6 %project.1 = (f32[1024,768]{1,0:T(8,128)}, bf16[1024,768]{1,0:T(8,128)(2,1)}, bf16[1024,768]{1,0:T(8,128)(2,1)}, bf16[1024,768]{1,0:T(8,128)(2,1)}, bf16[1024,76...) custom-call(s32[1]{0:T(128)} %bitcast.me_ref, ...), custom_call_target="tpu_custom_call" | custom-call | flops 3623878656 | bytes 20000000 | tf_op jit(solution)/shard_map/project/pallas_call | solution.py:204
  97.8 8.7 %attn_fwd.2 = (bf16[1024,256]{1,0:T(8,128)(2,1)}, bf16[2,1024,128]{2,1,0:T(8,128)(2,1)}) custom-call(bf16[1024,768]{1,0:T(8,128)(2,1)} %get-tuple-element.222.q_ref.rest_0_, bf16[1024,768]{1,0:T(8,128)(2,1)} %get-tuple-element.186.k_ref.rest_1_, bf16[1024,768]{1,0:T(8,128)(2,1)} %get-tuple-element.187.v_ref.rest_2_, ...), custom_call_target="tpu_custom_call" | custom-call | flops 1073741824 | bytes 2621440 | tf_op jit(solution)/shard_map/attn_fwd/pallas_call | solution.py:51
  109.9 2.8 collective-permute-start.23
  112.7 15.2 %attn_fwd.3 = (bf16[1024,512]{1,0:T(8,128)(2,1)}, bf16[4,1024,128]{2,1,0:T(8,128)(2,1)}) custom-call(bf16[1024,768]{1,0:T(8,128)(2,1)} %get-tuple-element.222.q_ref.rest_0_, bf16[1024,768]{1,0:T(8,128)(2,1)} %get-tuple-element.186.k_ref.rest_1_, bf16[1024,768]{1,0:T(8,128)(2,1)} %get-tuple-element.187.v_ref.rest_2_, ...), custom_call_target="tpu_custom_call" | custom-call | flops 2147483648 | bytes 5242880 | tf_op jit(solution)/shard_map/attn_fwd/pallas_call | solution.py:51
  128.5 2.8 collective-permute-done.25.rest_17_
  132.4 51.8 %middle.1 = (bf16[256,768]{1,0:T(8,128)(2,1)}, bf16[256,768]{1,0:T(8,128)(2,1)}, bf16[256,768]{1,0:T(8,128)(2,1)}, bf16[256,768]{1,0:T(8,128)(2,1)}, f32[1024,76...) custom-call(s32[1]{0:T(128)} %bitcast.me_ref, ...), custom_call_target="tpu_custom_call" | custom-call | flops 32614907904 | bytes 60000000 | tf_op jit(solution)/shard_map/middle/pallas_call | solution.py:527
  184.4 3.9 %collective-permute-start.27 = (bf16[256,768]{1,0:T(8,128)(2,1)}, bf16[256,768]{1,0:T(8,128)(2,1)S(1)}, u32[]{:S(2)}, u32[]{:S(2)}) collective-permute-start(bf16[256,768]{1,0:T(8,128)(2,1)} %get-tuple-element.215), channel_id=1, source_target_pairs={{0,1},{1,0},{2,3},{3,2},{4,5},{5,4},{6,7},{7,6},{8,9},{9,8},{10,11... | collective-permute-start | bytes 1179656 | tf_op jit(solution)/shard_map/ppermute | solution.py:541
  188.3 14.6 %attn_bwd.1.rest_9_.rest_0_ = bf16[3,1024,256]{2,1,0:T(8,128)(2,1)} custom-call(bf16[1024,768]{1,0:T(8,128)(2,1)} %get-tuple-element.222.q_ref.rest_0_, bf16[1024,768]{1,0:T(8,128)(2,1)} %get-tuple-element.186.k_ref.rest_1_, bf16[1024,768]{1,0:T(8,128)(2,1)} %get-tuple-element.187.v_ref.rest_2_, bf16[1024,768]{1,0:T(8,128)(2,1)} %get-tuple-element.219.do_ref.rest_3_, ...), custom_call_target="tpu_custom_call" | custom-call | flops 2684354560 | bytes 4718592 | tf_op jit(solution)/shard_map/attn_bwd/pallas_call | solution.py:103
  202.9 5.2 %sum_three.2 = (bf16[864,768]{1,0:T(8,128)(2,1)}, bf16[864,768]{1,0:T(8,128)(2,1)}, bf16[864,768]{1,0:T(8,128)(2,1)}) custom-call(bf16[4,864,768]{2,1,0:T(8,128)(2,1)} %get-tuple-element.248.a1.a2.a3.a, bf16[4,864,768]{2,1,0:T(8,128)(2,1)} %collective-permute-done.26.b1.b2.b3.b, bf16[4,864,768]{2,1,0:T(8,128)(2,1)} %get-tuple-element.248.a1.a2.a3.a, ...), custom_call_target="tpu_custom_call" | custom-call | tf_op jit(solution)/shard_map/sum_three/pallas_call | solution.py:326
  208.1 1.6 collective-permute-start.30
  210.3 1.4 collective-permute-start.32
  212.6 1.5 collective-permute-start.29
  214.0 32.7 %attn_finish.1 = (bf16[3,1024,512]{2,1,0:T(8,128)(2,1)}, bf16[256,768]{1,0:T(8,128)(2,1)}, bf16[256,768]{1,0:T(8,128)(2,1)}, bf16[256,768]{1,0:T(8,128)(2,1)}, b...) custom-call(s32[1]{0:T(128)} %bitcast.me_ref, s32[4,2]{1,0:T(4,128)} %pad_add_fusion.info_ref, ...), custom_call_target="tpu_custom_call" | custom-call | flops 5368709120 | bytes 9437184 | tf_op jit(solution)/shard_map/attn_finish/pallas_call | solution.py:258
  246.7 1.9 collective-permute-start.33
  249.7 10.5 %weight_grads.1 = (bf16[4,448,768]{2,1,0:T(8,128)(2,1)}, bf16[4,448,768]{2,1,0:T(8,128)(2,1)}) custom-call(s32[1]{0:T(128)} %bitcast.me_ref, bf16[1024,768]{1,0:T(8,128)(2,1)} %get-tuple-element.240.inp_ref, f32[8,768]{1,0:T(8,128)} %get-tuple-element.241.rows_ref, bf16[8,768]{1,0:T(8,128)(2,1)} %get-tuple-element.242.hid_ref, ...), custom_call_target="tpu_custom_call" | custom-call | flops 3623878656 | bytes 12000000 | tf_op jit(solution)/shard_map/weight_grads/pallas_call | solution.py:307
  260.2 6.3 %collective-permute-done.33 = bf16[256,768]{1,0:T(8,128)(2,1)} collective-permute-done((bf16[256,768]{1,0:T(8,128)(2,1)}, bf16[256,768]{1,0:T(8,128)(2,1)}, u32[]{:S(2)}, u32[]{:S(2)}) %collective-permute-start.33) | collective-permute-done | bytes 393248 | tf_op jit(solution)/shard_map/ppermute | solution.py:541
  266.5 2.6 collective-permute-done.34
  271.1 4.7 %sum_own.1 = (f32[2,216,768]{2,1,0:T(8,128)}, bf16[2,216,768]{2,1,0:T(8,128)(2,1)}) custom-call(s32[1]{0:T(128)} %bitcast.27.inner_ref, bf16[4,864,768]{2,1,0:T(8,128)(2,1)} %get-tuple-element.248.a1.a2.a3.a, bf16[4,864,768]{2,1,0:T(8,128)(2,1)} %collective-permute-done.26.b1.b2.b3.b, bf16[864,768]{1,0:T(8,128)(2,1)} %copy-done.4, ...), custom_call_target="tpu_custom_call" | custom-call | tf_op jit(solution)/shard_map/sum_own/pallas_call | solution.py:351
  276.9 1.2 bitcast_dynamic-update-slice_fusion.1
  278.2 2.3 collective-permute-start.41
  282.5 1.5 collective-permute-start.37
  285.2 7.8 %collective-permute-done.39 = bf16[2,216,768]{2,1,0:T(8,128)(2,1)S(1)} collective-permute-done((bf16[2,216,768]{2,1,0:T(8,128)(2,1)}, bf16[2,216,768]{2,1,0:T(8,128)(2,1)S(1)}, u32[]{:S(2)}, u32[]{:S(2)}) %collective-permute-start.39) | collective-permute-done | bytes 663584 | tf_op jit(solution)/shard_map/ppermute | solution.py:541
  293.3 1.7 collective-permute-start.40
  296.1 6.6 %collective-permute-done.41 = bf16[256,768]{1,0:T(8,128)(2,1)S(1)} collective-permute-done((bf16[256,768]{1,0:T(8,128)(2,1)S(1)}, bf16[256,768]{1,0:T(8,128)(2,1)S(1)}, u32[]{:S(2)}, u32[]{:S(2)}) %collective-permute-start.41) | collective-permute-done | bytes 393248 | tf_op jit(solution)/shard_map/ppermute | solution.py:541
  302.6 13.7 %collective-permute-done.40 = bf16[1,216,768]{2,1,0:T(8,128)(2,1)S(1)} collective-permute-done((bf16[1,216,768]{2,1,0:T(8,128)(2,1)S(1)}, bf16[1,216,768]{2,1,0:T(8,128)(2,1)S(1)}, u32[]{:S(2)}, u32[]{:S(2)}) %collective-permute-start.40) | collective-permute-done | bytes 331808 | tf_op jit(solution)/shard_map/ppermute | solution.py:541
  316.3 1.3 sum_direct.1
  317.7 2.1 collective-permute-start.43
  319.8 2.3 collective-permute-start.44
  326.5 6.8 %collective-permute-done.43.refs_2_ = bf16[112,768]{1,0:T(8,128)(2,1)S(1)} collective-permute-done((bf16[112,768]{1,0:T(8,128)(2,1)S(1)}, bf16[112,768]{1,0:T(8,128)(2,1)S(1)}, u32[]{:S(2)}, u32[]{:S(2)}) %collective-permute-start.43) | collective-permute-done | bytes 172064 | tf_op jit(solution)/shard_map/ppermute | solution.py:541
  (170 shorter events, 32.7 us)
Async XLA Ops:
  2.8 13.1 %collective-permute-start = (bf16[1,112,768]{2,1,0:T(8,128)(2,1)}, bf16[1,112,768]{2,1,0:T(8,128)(2,1)S(1)}, u32[]{:S(2)}, u32[]{:S(2)}) collective-permute-start(bf16[1,112,768]{2,1,0:T(8,128)(2,1)} %bitcast.67), channel_id=1, source_target_pairs={{0,2},{1,3},{2,0},{3,1},{4,6},{5,7},{6,4},{7,5},{8,10},{9,11},{10,... | collective-permute-start | bytes 516104 | tf_op jit(solution)/shard_map/ppermute | solution.py:541
  16.0 17.4 %collective-permute-start.2 = (bf16[1,216,768]{2,1,0:T(8,128)(2,1)S(1)}, bf16[1,216,768]{2,1,0:T(8,128)(2,1)S(1)}, u32[]{:S(2)}, u32[]{:S(2)}) collective-permute-start(bf16[1,216,768]{2,1,0:T(8,128)(2,1)S(1)} %bitcast.65), channel_id=1, source_target_pairs={{0,2},{1,3},{2,0},{3,1},{4,6},{5,7},{6,4},{7,5},{8,10},{9,11},{10,... | collective-permute-start | bytes 995336 | tf_op jit(solution)/shard_map/ppermute | solution.py:541
  16.7 17.2 %collective-permute-start.1 = (bf16[2,112,768]{2,1,0:T(8,128)(2,1)S(1)}, bf16[2,112,768]{2,1,0:T(8,128)(2,1)S(1)}, u32[]{:S(2)}, u32[]{:S(2)}) collective-permute-start(bf16[2,112,768]{2,1,0:T(8,128)(2,1)S(1)} %pad_maximum_fusion.4), channel_id=1, source_target_pairs={{0,1},{1,0},{2,3},{3,2},{4,5},{5,4},{6,7},{7,6},{8,9},{9,8},{10,11... | collective-permute-start | bytes 1032200 | tf_op jit(solution)/shard_map/ppermute | solution.py:541
  34.6 24.5 %copy-start.9 = (bf16[448,768]{1,0:T(8,128)(2,1)}, bf16[448,768]{1,0:T(8,128)(2,1)S(1)}, u32[]{:S(2)}) copy-start(bf16[448,768]{1,0:T(8,128)(2,1)S(1)} %pad_maximum_fusion.2.rest_4_.rest_10_) | copy-start | bytes 2064388
  35.2 23.7 %collective-permute-start.6 = (bf16[2,216,768]{2,1,0:T(8,128)(2,1)S(1)}, bf16[2,216,768]{2,1,0:T(8,128)(2,1)S(1)}, u32[]{:S(2)}, u32[]{:S(2)}) collective-permute-start(bf16[2,216,768]{2,1,0:T(8,128)(2,1)S(1)} %pad_maximum_fusion.3), channel_id=1, source_target_pairs={{0,1},{1,0},{2,3},{3,2},{4,5},{5,4},{6,7},{7,6},{8,9},{9,8},{10,11... | collective-permute-start | bytes 1990664 | tf_op jit(solution)/shard_map/ppermute | solution.py:541
  35.2 26.9 %collective-permute-start.3 = (bf16[448,768]{1,0:T(8,128)(2,1)S(1)}, bf16[448,768]{1,0:T(8,128)(2,1)S(1)}, u32[]{:S(2)}, u32[]{:S(2)}) collective-permute-start(bf16[448,768]{1,0:T(8,128)(2,1)S(1)} %pad_maximum_fusion.2.rest_4_.rest_10_), channel_id=1, source_target_pairs={{0,8},{1,9},{2,10},{3,11},{4,12},{5,13},{6,14},{7,15},{8,0},{9,1},... | collective-permute-start | bytes 2064392 | tf_op jit(solution)/shard_map/ppermute | solution.py:541
  36.7 30.3 %collective-permute-start.4 = (bf16[448,768]{1,0:T(8,128)(2,1)S(1)}, bf16[448,768]{1,0:T(8,128)(2,1)S(1)}, u32[]{:S(2)}, u32[]{:S(2)}) collective-permute-start(bf16[448,768]{1,0:T(8,128)(2,1)S(1)} %pad_maximum_fusion.2.rest_4_.rest_10_), channel_id=1, source_target_pairs={{0,16},{1,17},{2,18},{3,19},{4,20},{5,21},{6,22},{7,23},{8,24},{9,... | collective-permute-start | bytes 2064392 | tf_op jit(solution)/shard_map/ppermute | solution.py:541
  38.2 20.8 %collective-permute-start.5 = (bf16[256,768]{1,0:T(8,128)(2,1)S(1)}, bf16[256,768]{1,0:T(8,128)(2,1)S(1)}, u32[]{:S(2)}, u32[]{:S(2)}) collective-permute-start(bf16[256,768]{1,0:T(8,128)(2,1)S(1)} %get-tuple-element.172), channel_id=1, source_target_pairs={{0,2},{1,3},{2,0},{3,1},{4,6},{5,7},{6,4},{7,5},{8,10},{9,11},{10,... | collective-permute-start | bytes 1179656 | tf_op jit(solution)/shard_map/ppermute | solution.py:541
  41.8 32.3 %collective-permute-start.9 = (bf16[448,768]{1,0:T(8,128)(2,1)S(1)}, bf16[448,768]{1,0:T(8,128)(2,1)S(1)}, u32[]{:S(2)}, u32[]{:S(2)}) collective-permute-start(bf16[448,768]{1,0:T(8,128)(2,1)S(1)} %pad_maximum_fusion.2.rest_4_.rest_10_), channel_id=1, source_target_pairs={{0,24},{1,25},{2,26},{3,27},{4,28},{5,29},{6,30},{7,31},{8,16},{9,... | collective-permute-start | bytes 2064392 | tf_op jit(solution)/shard_map/ppermute | solution.py:541
  58.9 16.8 %collective-permute-start.10 = (bf16[448,768]{1,0:T(8,128)(2,1)S(1)}, bf16[448,768]{1,0:T(8,128)(2,1)S(1)}, u32[]{:S(2)}, u32[]{:S(2)}) collective-permute-start(bf16[448,768]{1,0:T(8,128)(2,1)S(1)} %pad_maximum_fusion.2.rest_4_.rest_10_), channel_id=1, source_target_pairs={{0,4},{1,5},{2,6},{3,7},{4,0},{5,1},{6,2},{7,3},{8,12},{9,13},{10,... | collective-permute-start | bytes 2064392 | tf_op jit(solution)/shard_map/ppermute | solution.py:541
  59.1 13.6 %collective-permute-start.8 = (bf16[256,768]{1,0:T(8,128)(2,1)S(1)}, bf16[256,768]{1,0:T(8,128)(2,1)S(1)}, u32[]{:S(2)}, u32[]{:S(2)}) collective-permute-start(bf16[256,768]{1,0:T(8,128)(2,1)S(1)} %get-tuple-element.177), channel_id=1, source_target_pairs={{0,3},{1,2},{2,1},{3,0},{4,7},{5,6},{6,5},{7,4},{8,11},{9,10},{10,... | collective-permute-start | bytes 1179656 | tf_op jit(solution)/shard_map/ppermute | solution.py:541
  67.5 13.7 %collective-permute-start.11 = (bf16[448,768]{1,0:T(8,128)(2,1)S(1)}, bf16[448,768]{1,0:T(8,128)(2,1)S(1)}, u32[]{:S(2)}, u32[]{:S(2)}) collective-permute-start(bf16[448,768]{1,0:T(8,128)(2,1)S(1)} %collective-permute-done.3.rest_5_.rest_11_), channel_id=1, source_target_pairs={{0,4},{1,5},{2,6},{3,7},{4,0},{5,1},{6,2},{7,3},{8,12},{9,13},{10,... | collective-permute-start | bytes 2064392 | tf_op jit(solution)/shard_map/ppermute | solution.py:541
  68.8 12.1 %collective-permute-start.7 = (bf16[256,768]{1,0:T(8,128)(2,1)S(1)}, bf16[256,768]{1,0:T(8,128)(2,1)S(1)}, u32[]{:S(2)}, u32[]{:S(2)}) collective-permute-start(bf16[256,768]{1,0:T(8,128)(2,1)S(1)} %get-tuple-element.175), channel_id=1, source_target_pairs={{0,1},{1,0},{2,3},{3,2},{4,5},{5,4},{6,7},{7,6},{8,9},{9,8},{10,11... | collective-permute-start | bytes 1179656 | tf_op jit(solution)/shard_map/ppermute | solution.py:541
  72.6 33.9 %collective-permute-start.14 = (bf16[864,768]{1,0:T(8,128)(2,1)S(1)}, bf16[864,768]{1,0:T(8,128)(2,1)}, u32[]{:S(2)}, u32[]{:S(2)}) collective-permute-start(bf16[864,768]{1,0:T(8,128)(2,1)S(1)} %pad_maximum_fusion.1.rest_8_), channel_id=1, source_target_pairs={{0,8},{1,9},{2,10},{3,11},{4,12},{5,13},{6,14},{7,15},{8,0},{9,1},... | collective-permute-start | bytes 3981320 | tf_op jit(solution)/shard_map/ppermute | solution.py:541
  74.1 32.4 %collective-permute-start.15 = (bf16[864,768]{1,0:T(8,128)(2,1)S(1)}, bf16[864,768]{1,0:T(8,128)(2,1)S(1)}, u32[]{:S(2)}, u32[]{:S(2)}) collective-permute-start(bf16[864,768]{1,0:T(8,128)(2,1)S(1)} %pad_maximum_fusion.1.rest_8_), channel_id=1, source_target_pairs={{0,16},{1,17},{2,18},{3,19},{4,20},{5,21},{6,22},{7,23},{8,24},{9,... | collective-permute-start | bytes 3981320 | tf_op jit(solution)/shard_map/ppermute | solution.py:541
  75.7 30.8 %collective-permute-start.16 = (bf16[864,768]{1,0:T(8,128)(2,1)S(1)}, bf16[864,768]{1,0:T(8,128)(2,1)}, u32[]{:S(2)}, u32[]{:S(2)}) collective-permute-start(bf16[864,768]{1,0:T(8,128)(2,1)S(1)} %pad_maximum_fusion.1.rest_8_), channel_id=1, source_target_pairs={{0,4},{1,5},{2,6},{3,7},{4,0},{5,1},{6,2},{7,3},{8,12},{9,13},{10,... | collective-permute-start | bytes 3981320 | tf_op jit(solution)/shard_map/ppermute | solution.py:541
  81.0 2.1 collective-permute-start.12
  81.2 4.9 %collective-permute-start.13 = (bf16[448,768]{1,0:T(8,128)(2,1)S(1)}, bf16[448,768]{1,0:T(8,128)(2,1)S(1)}, u32[]{:S(2)}, u32[]{:S(2)}) collective-permute-start(bf16[448,768]{1,0:T(8,128)(2,1)S(1)} %collective-permute-done.9.rest_7_.rest_13_), channel_id=1, source_target_pairs={{0,4},{1,5},{2,6},{3,7},{4,0},{5,1},{6,2},{7,3},{8,12},{9,13},{10,... | collective-permute-start | bytes 2064392 | tf_op jit(solution)/shard_map/ppermute | solution.py:541
  83.1 23.4 %collective-permute-start.17 = (bf16[256,768]{1,0:T(8,128)(2,1)S(1)}, bf16[256,768]{1,0:T(8,128)(2,1)}, u32[]{:S(2)}, u32[]{:S(2)}) collective-permute-start(bf16[256,768]{1,0:T(8,128)(2,1)S(1)} %get-tuple-element.183), channel_id=1, source_target_pairs={{0,1},{1,0},{2,3},{3,2},{4,5},{5,4},{6,7},{7,6},{8,9},{9,8},{10,11... | collective-permute-start | bytes 1179656 | tf_op jit(solution)/shard_map/ppermute | solution.py:541
  86.1 20.4 %collective-permute-start.18 = (bf16[256,768]{1,0:T(8,128)(2,1)S(1)}, bf16[256,768]{1,0:T(8,128)(2,1)}, u32[]{:S(2)}, u32[]{:S(2)}) collective-permute-start(bf16[256,768]{1,0:T(8,128)(2,1)S(1)} %get-tuple-element.184), channel_id=1, source_target_pairs={{0,2},{1,3},{2,0},{3,1},{4,6},{5,7},{6,4},{7,5},{8,10},{9,11},{10,... | collective-permute-start | bytes 1179656 | tf_op jit(solution)/shard_map/ppermute | solution.py:541
  106.5 21.4 %collective-permute-start.21 = (bf16[864,768]{1,0:T(8,128)(2,1)}, bf16[864,768]{1,0:T(8,128)(2,1)}, u32[]{:S(2)}, u32[]{:S(2)}) collective-permute-start(bf16[864,768]{1,0:T(8,128)(2,1)} %collective-permute-done.14.rest_9_), channel_id=1, source_target_pairs={{0,4},{1,5},{2,6},{3,7},{4,0},{5,1},{6,2},{7,3},{8,12},{9,13},{10,... | collective-permute-start | bytes 3981320 | tf_op jit(solution)/shard_map/ppermute | solution.py:541
  106.6 21.3 %collective-permute-start.22 = (bf16[864,768]{1,0:T(8,128)(2,1)S(1)}, bf16[864,768]{1,0:T(8,128)(2,1)}, u32[]{:S(2)}, u32[]{:S(2)}) collective-permute-start(bf16[864,768]{1,0:T(8,128)(2,1)S(1)} %collective-permute-done.15.rest_10_), channel_id=1, source_target_pairs={{0,4},{1,5},{2,6},{3,7},{4,0},{5,1},{6,2},{7,3},{8,12},{9,13},{10,... | collective-permute-start | bytes 3981320 | tf_op jit(solution)/shard_map/ppermute | solution.py:541
  107.2 20.7 %collective-permute-start.19 = (bf16[480,768]{1,0:T(8,128)(2,1)S(1)}, bf16[480,768]{1,0:T(8,128)(2,1)S(1)}, u32[]{:S(2)}, u32[]{:S(2)}) collective-permute-start(bf16[480,768]{1,0:T(8,128)(2,1)S(1)} %slice.89), channel_id=1, source_target_pairs={{0,8},{1,9},{2,10},{3,11},{4,12},{5,13},{6,14},{7,15},{8,0},{9,1},... | collective-permute-start | bytes 2211848 | tf_op jit(solution)/shard_map/ppermute | solution.py:541
  108.9 19.0 %collective-permute-start.20 = (bf16[384,768]{1,0:T(8,128)(2,1)S(1)}, bf16[384,768]{1,0:T(8,128)(2,1)}, u32[]{:S(2)}, u32[]{:S(2)}) collective-permute-start(bf16[384,768]{1,0:T(8,128)(2,1)S(1)} %slice.90), channel_id=1, source_target_pairs={{0,16},{1,17},{2,18},{3,19},{4,20},{5,21},{6,22},{7,23},{8,24},{9,... | collective-permute-start | bytes 1769480 | tf_op jit(solution)/shard_map/ppermute | solution.py:541
  109.9 18.0 %collective-permute-start.23 = (bf16[256,768]{1,0:T(8,128)(2,1)S(1)}, bf16[256,768]{1,0:T(8,128)(2,1)}, u32[]{:S(2)}, u32[]{:S(2)}) collective-permute-start(bf16[256,768]{1,0:T(8,128)(2,1)S(1)} %get-tuple-element.199), channel_id=1, source_target_pairs={{0,3},{1,2},{2,1},{3,0},{4,7},{5,6},{6,5},{7,4},{8,11},{9,10},{10,... | collective-permute-start | bytes 1179656 | tf_op jit(solution)/shard_map/ppermute | solution.py:541
  127.9 3.3 collective-permute-start.24
  128.0 3.3 collective-permute-start.25
  184.2 18.7 %collective-permute-start.26 = (bf16[4,864,768]{2,1,0:T(8,128)(2,1)}, bf16[4,864,768]{2,1,0:T(8,128)(2,1)}, u32[]{:S(2)}, u32[]{:S(2)}) collective-permute-start(bf16[4,864,768]{2,1,0:T(8,128)(2,1)} %get-tuple-element.214), channel_id=1, source_target_pairs={{0,4},{1,5},{2,6},{3,7},{4,0},{5,1},{6,2},{7,3},{8,12},{9,13},{10,... | collective-permute-start | bytes 15925256 | tf_op jit(solution)/shard_map/ppermute | solution.py:541
  184.4 18.5 %collective-permute-start.27 = (bf16[256,768]{1,0:T(8,128)(2,1)}, bf16[256,768]{1,0:T(8,128)(2,1)S(1)}, u32[]{:S(2)}, u32[]{:S(2)}) collective-permute-start(bf16[256,768]{1,0:T(8,128)(2,1)} %get-tuple-element.215), channel_id=1, source_target_pairs={{0,1},{1,0},{2,3},{3,2},{4,5},{5,4},{6,7},{7,6},{8,9},{9,8},{10,11... | collective-permute-start | bytes 1179656 | tf_op jit(solution)/shard_map/ppermute | solution.py:541
  208.1 61.0 %collective-permute-start.30 = (bf16[864,768]{1,0:T(8,128)(2,1)}, bf16[864,768]{1,0:T(8,128)(2,1)S(1)}, u32[]{:S(2)}, u32[]{:S(2)}) collective-permute-start(bf16[864,768]{1,0:T(8,128)(2,1)} %get-tuple-element.250), channel_id=1, source_target_pairs={{0,8},{1,9},{2,10},{3,11},{4,12},{5,13},{6,14},{7,15},{8,0},{9,1},... | collective-permute-start | bytes 3981320 | tf_op jit(solution)/shard_map/ppermute | solution.py:541
  209.7 59.5 %collective-permute-start.31 = (bf16[864,768]{1,0:T(8,128)(2,1)}, bf16[864,768]{1,0:T(8,128)(2,1)S(1)}, u32[]{:S(2)}, u32[]{:S(2)}) collective-permute-start(bf16[864,768]{1,0:T(8,128)(2,1)} %get-tuple-element.251), channel_id=1, source_target_pairs={{0,16},{1,17},{2,18},{3,19},{4,20},{5,21},{6,22},{7,23},{8,24},{9,... | collective-permute-start | bytes 3981320 | tf_op jit(solution)/shard_map/ppermute | solution.py:541
  210.3 58.9 %collective-permute-start.32 = (bf16[864,768]{1,0:T(8,128)(2,1)}, bf16[864,768]{1,0:T(8,128)(2,1)S(1)}, u32[]{:S(2)}, u32[]{:S(2)}) collective-permute-start(bf16[864,768]{1,0:T(8,128)(2,1)} %get-tuple-element.252), channel_id=1, source_target_pairs={{0,24},{1,25},{2,26},{3,27},{4,28},{5,29},{6,30},{7,31},{8,16},{9,... | collective-permute-start | bytes 3981320 | tf_op jit(solution)/shard_map/ppermute | solution.py:541
  211.6 35.1 %collective-permute-start.28 = (bf16[256,768]{1,0:T(8,128)(2,1)}, bf16[256,768]{1,0:T(8,128)(2,1)}, u32[]{:S(2)}, u32[]{:S(2)}) collective-permute-start(bf16[256,768]{1,0:T(8,128)(2,1)} %get-tuple-element.234), channel_id=1, source_target_pairs={{0,2},{1,3},{2,0},{3,1},{4,6},{5,7},{6,4},{7,5},{8,10},{9,11},{10,... | collective-permute-start | bytes 1179656 | tf_op jit(solution)/shard_map/ppermute | solution.py:541
  212.6 34.2 %collective-permute-start.29 = (bf16[256,768]{1,0:T(8,128)(2,1)}, bf16[256,768]{1,0:T(8,128)(2,1)}, u32[]{:S(2)}, u32[]{:S(2)}) collective-permute-start(bf16[256,768]{1,0:T(8,128)(2,1)} %get-tuple-element.235), channel_id=1, source_target_pairs={{0,3},{1,2},{2,1},{3,0},{4,7},{5,6},{6,5},{7,4},{8,11},{9,10},{10,... | collective-permute-start | bytes 1179656 | tf_op jit(solution)/shard_map/ppermute | solution.py:541
  246.7 19.8 %collective-permute-start.33 = (bf16[256,768]{1,0:T(8,128)(2,1)}, bf16[256,768]{1,0:T(8,128)(2,1)}, u32[]{:S(2)}, u32[]{:S(2)}) collective-permute-start(bf16[256,768]{1,0:T(8,128)(2,1)} %get-tuple-element.253), channel_id=1, source_target_pairs={{0,1},{1,0},{2,3},{3,2},{4,5},{5,4},{6,7},{7,6},{8,9},{9,8},{10,11... | collective-permute-start | bytes 1179656 | tf_op jit(solution)/shard_map/ppermute | solution.py:541
  248.7 20.4 %collective-permute-start.34 = (bf16[256,768]{1,0:T(8,128)(2,1)}, bf16[256,768]{1,0:T(8,128)(2,1)}, u32[]{:S(2)}, u32[]{:S(2)}) collective-permute-start(bf16[256,768]{1,0:T(8,128)(2,1)} %get-tuple-element.254), channel_id=1, source_target_pairs={{0,2},{1,3},{2,0},{3,1},{4,6},{5,7},{6,4},{7,5},{8,10},{9,11},{10,... | collective-permute-start | bytes 1179656 | tf_op jit(solution)/shard_map/ppermute | solution.py:541
  270.7 9.7 %collective-permute-start.35 = (bf16[4,448,768]{2,1,0:T(8,128)(2,1)}, bf16[4,448,768]{2,1,0:T(8,128)(2,1)S(1)}, u32[]{:S(2)}, u32[]{:S(2)}) collective-permute-start(bf16[4,448,768]{2,1,0:T(8,128)(2,1)} %get-tuple-element.256), channel_id=1, source_target_pairs={{0,4},{1,5},{2,6},{3,7},{4,0},{5,1},{6,2},{7,3},{8,12},{9,13},{10,... | collective-permute-start | bytes 8257544 | tf_op jit(solution)/shard_map/ppermute | solution.py:541
  275.8 17.2 %collective-permute-start.39 = (bf16[2,216,768]{2,1,0:T(8,128)(2,1)}, bf16[2,216,768]{2,1,0:T(8,128)(2,1)S(1)}, u32[]{:S(2)}, u32[]{:S(2)}) collective-permute-start(bf16[2,216,768]{2,1,0:T(8,128)(2,1)} %get-tuple-element.268), channel_id=1, source_target_pairs={{0,1},{1,0},{2,3},{3,2},{4,5},{5,4},{6,7},{7,6},{8,9},{9,8},{10,11... | collective-permute-start | bytes 1990664 | tf_op jit(solution)/shard_map/ppermute | solution.py:541
  278.2 14.9 %copy-start.7 = (f32[2,216,768]{2,1,0:T(8,128)S(1)}, f32[2,216,768]{2,1,0:T(8,128)}, u32[]{:S(2)}) copy-start(f32[2,216,768]{2,1,0:T(8,128)} %get-tuple-element.267) | copy-start | bytes 3981316
  278.2 24.5 %collective-permute-start.41 = (bf16[256,768]{1,0:T(8,128)(2,1)S(1)}, bf16[256,768]{1,0:T(8,128)(2,1)S(1)}, u32[]{:S(2)}, u32[]{:S(2)}) collective-permute-start(bf16[256,768]{1,0:T(8,128)(2,1)S(1)} %copy-done.27), channel_id=1, source_target_pairs={{0,3},{1,2},{2,1},{3,0},{4,7},{5,6},{6,5},{7,4},{8,11},{9,10},{10,... | collective-permute-start | bytes 1179656 | tf_op jit(solution)/shard_map/ppermute | solution.py:541
  281.6 34.7 %collective-permute-start.36 = (bf16[448,768]{1,0:T(8,128)(2,1)S(1)}, bf16[448,768]{1,0:T(8,128)(2,1)S(1)}, u32[]{:S(2)}, u32[]{:S(2)}) collective-permute-start(bf16[448,768]{1,0:T(8,128)(2,1)S(1)} %get-tuple-element.257), channel_id=1, source_target_pairs={{0,8},{1,9},{2,10},{3,11},{4,12},{5,13},{6,14},{7,15},{8,0},{9,1},... | collective-permute-start | bytes 2064392 | tf_op jit(solution)/shard_map/ppermute | solution.py:541
  282.5 33.8 %collective-permute-start.37 = (bf16[448,768]{1,0:T(8,128)(2,1)S(1)}, bf16[448,768]{1,0:T(8,128)(2,1)S(1)}, u32[]{:S(2)}, u32[]{:S(2)}) collective-permute-start(bf16[448,768]{1,0:T(8,128)(2,1)S(1)} %get-tuple-element.258), channel_id=1, source_target_pairs={{0,16},{1,17},{2,18},{3,19},{4,20},{5,21},{6,22},{7,23},{8,24},{9,... | collective-permute-start | bytes 2064392 | tf_op jit(solution)/shard_map/ppermute | solution.py:541
  284.0 32.3 %collective-permute-start.38 = (bf16[448,768]{1,0:T(8,128)(2,1)S(1)}, bf16[448,768]{1,0:T(8,128)(2,1)S(1)}, u32[]{:S(2)}, u32[]{:S(2)}) collective-permute-start(bf16[448,768]{1,0:T(8,128)(2,1)S(1)} %get-tuple-element.259), channel_id=1, source_target_pairs={{0,24},{1,25},{2,26},{3,27},{4,28},{5,29},{6,30},{7,31},{8,16},{9,... | collective-permute-start | bytes 2064392 | tf_op jit(solution)/shard_map/ppermute | solution.py:541
  293.3 23.0 %collective-permute-start.40 = (bf16[1,216,768]{2,1,0:T(8,128)(2,1)S(1)}, bf16[1,216,768]{2,1,0:T(8,128)(2,1)S(1)}, u32[]{:S(2)}, u32[]{:S(2)}) collective-permute-start(bf16[1,216,768]{2,1,0:T(8,128)(2,1)S(1)} %slice.108), channel_id=1, source_target_pairs={{0,2},{1,3},{2,0},{3,1},{4,6},{5,7},{6,4},{7,5},{8,10},{9,11},{10,... | collective-permute-start | bytes 995336 | tf_op jit(solution)/shard_map/ppermute | solution.py:541
  296.0 21.6 %copy-start.2 = (bf16[4,256,768]{2,1,0:T(8,128)(2,1)}, bf16[4,256,768]{2,1,0:T(8,128)(2,1)S(1)}, u32[]{:S(2)}) copy-start(bf16[4,256,768]{2,1,0:T(8,128)(2,1)S(1)} %bitcast_dynamic-update-slice_fusion) | copy-start | bytes 4718596
  317.6 8.9 %collective-permute-start.42 = (bf16[112,768]{1,0:T(8,128)(2,1)S(1)}, bf16[112,768]{1,0:T(8,128)(2,1)S(1)}, u32[]{:S(2)}, u32[]{:S(2)}) collective-permute-start(bf16[112,768]{1,0:T(8,128)(2,1)S(1)} %get-tuple-element.281), channel_id=1, source_target_pairs={{0,1},{1,0},{2,3},{3,2},{4,5},{5,4},{6,7},{7,6},{8,9},{9,8},{10,11... | collective-permute-start | bytes 516104 | tf_op jit(solution)/shard_map/ppermute | solution.py:541
  317.7 15.6 %collective-permute-start.43 = (bf16[112,768]{1,0:T(8,128)(2,1)S(1)}, bf16[112,768]{1,0:T(8,128)(2,1)S(1)}, u32[]{:S(2)}, u32[]{:S(2)}) collective-permute-start(bf16[112,768]{1,0:T(8,128)(2,1)S(1)} %get-tuple-element.282), channel_id=1, source_target_pairs={{0,2},{1,3},{2,0},{3,1},{4,6},{5,7},{6,4},{7,5},{8,10},{9,11},{10,... | collective-permute-start | bytes 516104 | tf_op jit(solution)/shard_map/ppermute | solution.py:541
  319.8 13.5 %collective-permute-start.44 = (bf16[112,768]{1,0:T(8,128)(2,1)S(1)}, bf16[112,768]{1,0:T(8,128)(2,1)S(1)}, u32[]{:S(2)}, u32[]{:S(2)}) collective-permute-start(bf16[112,768]{1,0:T(8,128)(2,1)S(1)} %get-tuple-element.283), channel_id=1, source_target_pairs={{0,3},{1,2},{2,1},{3,0},{4,7},{5,6},{6,5},{7,4},{8,11},{9,10},{10,... | collective-permute-start | bytes 516104 | tf_op jit(solution)/shard_map/ppermute | solution.py:541
  (28 other events, 138.6 us)

commit v4 on v3

--- a/solution.py
+++ b/solution.py
@@ -263,7 +263,7 @@
       cost_estimate=bwd_cost(L,np_),
       name="attn_finish")(me,info,*att,ga,pre,first,*pieces)
 STEP=1024
-MROWS=512
+MROWS=1024
 def weight_kernel(nc,unit,me_ref,inp_ref,rows_ref,hid_ref,feat_ref,dvec_ref,dupb_ref,*rest):
     grads=rest[:nc]
     mine_ref,theirs_ref,acc=rest[nc:]
@@ -659,7 +659,7 @@
             out=lax.dynamic_update_index_in_dim(out,part.astype(dtype),s0^c,0)
         return out
     tg,rows4,backs=sync(tg,rows4,backs)
-    held=[flip(tg[c],c,total) for c in range(1,streams-1)]
+    held=[flip(tg[c],c,total) for c in range(streams-2,0,-1)][::-1]
     mine1,theirs1=weight_grads(me,inputs,rows4,hid,feat,dvec,dupb,grads,unit)
     mine1,theirs1,fx,fy,fd,held=sync(mine1,theirs1,fx,fy,fd,held)
     keep2,send2=sum_own(inner,mine2,got,(fx,fy,fd),((1,shard),(1,ff_shard),(FF//D,shard)),unit)
@@ -674,7 +674,7 @@
     output=place(backs,BF)
     dwo,dwd,dwu=last2(keep2,got2,shard,ff_shard,FF)
     keep1,*sends=sum_direct(inner,mine1,got1,(fx,fy,fd),((4,shard),(1,SMALL)),unit)
-    given=[keep1]+[flip(x,c+1,total) for c,x in enumerate(sends)]
+    given=[keep1]+[flip(x,c+1,total) for c,x in reversed(list(enumerate(sends)))]
     dwq,dwk,dwv,dwe,dws,bq,bv,bo,ag,as_,bd,fg,fs,bs,be,bu=last1(given,shard,stamp_rows,[shard]*10+[ff_shard])
     token_grad=place(tgs,F32)
     return (output,token_grad,dwq,bq,dwk,dwv,bv,dwo,bo,ag,as_,dwu,bu,dwd,bd,fg,fs,dws,bs,dwe,be)

time: 338 us -> 338 us (level)
  no operation moved by 1% of the time
where the time goes in v4:
time: 338 us; the launch traced here: 334 us
  Pallas kernels  159 us (47%)
  waiting for transfers between devices  89.8 us (27%)
  starting transfers between devices  59 us (17%)
  local copies, waits for them, and re-layouts  16.4 us (5%)
  other arithmetic  7.3 us (2%)
    ppermute x45, waiting for transfers between devices, flip(): return lax.ppermute(x, AXES, [(i, i ^ mask) for i in range(total)])  89.8 us
    ppermute x45, starting transfers between devices, flip(): return lax.ppermute(x, AXES, [(i, i ^ mask) for i in range(total)])  59 us
    pallas_call x1, Pallas kernels, middle(): pl.pallas_call(kern, grid=(nb,), in_specs=[smem(), smem(), row] + [anyw()...  51.8 us
    pallas_call x1, Pallas kernels, attn_finish(): pl.pallas_call(functools.partial(finish_kernel, p0, nt), grid=(np_,), in_...  33 us
    pallas_call x2, Pallas kernels, attn_fwd(): pl.pallas_call(fwd_kernel, grid=(np_,), in_specs=[col(), col(), col(), pl...  23.8 us
    pallas_call x1, Pallas kernels, attn_bwd(): pl.pallas_call(functools.partial(bwd_pair, p0), grid=(np_,), in_specs=ins...  14.6 us
    pallas_call x1, Pallas kernels, weight_grads(): pl.pallas_call(functools.partial(weight_kernel, nc, unit), grid=(L // R,)...  10.5 us
    pallas_call x1, Pallas kernels, project(): pl.pallas_call(functools.partial(in_kernel, nt, unit), grid=(nt,), in_spe...  9.57 us
  transfers between devices with their start and end apart: 45, of which 15 were waited for; matrix products, arithmetic and copies ran while one was open for 5% of the time, Pallas kernels for 29%

profile of v4, /device:TPU:0, one launch (start us, length us, event | category | flops | bytes accessed | tf_op | source)
XLA Modules:
  0.0 334.3 jit_solution(17349745269211390040)
XLA Ops:
  0.7 2.1 pack.1
  2.8 4.0 %collective-permute-start = (bf16[1,112,768]{2,1,0:T(8,128)(2,1)}, bf16[1,112,768]{2,1,0:T(8,128)(2,1)S(1)}, u32[]{:S(2)}, u32[]{:S(2)}) collective-permute-start(bf16[1,112,768]{2,1,0:T(8,128)(2,1)} %bitcast.67), channel_id=1, source_target_pairs={{0,2},{1,3},{2,0},{3,1},{4,6},{5,7},{6,4},{7,5},{8,10},{9,11},{10,... | collective-permute-start | bytes 516104 | tf_op jit(solution)/shard_map/ppermute | solution.py:541
  12.3 1.3 select_clamp_fusion
  13.7 2.3 dynamic-slice_bitcast_fusion.4
  16.7 3.2 collective-permute-start.1
  20.0 13.4 %collective-permute-done.2 = bf16[1,216,768]{2,1,0:T(8,128)(2,1)S(1)} collective-permute-done((bf16[1,216,768]{2,1,0:T(8,128)(2,1)S(1)}, bf16[1,216,768]{2,1,0:T(8,128)(2,1)S(1)}, u32[]{:S(2)}, u32[]{:S(2)}) %collective-permute-start.2) | collective-permute-done | bytes 331808 | tf_op jit(solution)/shard_map/ppermute | solution.py:541
  35.2 1.5 collective-permute-start.3
  36.7 1.5 collective-permute-start.4
  38.2 3.6 %collective-permute-start.5 = (bf16[256,768]{1,0:T(8,128)(2,1)S(1)}, bf16[256,768]{1,0:T(8,128)(2,1)S(1)}, u32[]{:S(2)}, u32[]{:S(2)}) collective-permute-start(bf16[256,768]{1,0:T(8,128)(2,1)S(1)} %get-tuple-element.172), channel_id=1, source_target_pairs={{0,2},{1,3},{2,0},{3,1},{4,6},{5,7},{6,4},{7,5},{8,10},{9,11},{10,... | collective-permute-start | bytes 1179656 | tf_op jit(solution)/shard_map/ppermute | solution.py:541
  42.3 16.6 %collective-permute-done.6 = bf16[2,216,768]{2,1,0:T(8,128)(2,1)S(1)} collective-permute-done((bf16[2,216,768]{2,1,0:T(8,128)(2,1)S(1)}, bf16[2,216,768]{2,1,0:T(8,128)(2,1)S(1)}, u32[]{:S(2)}, u32[]{:S(2)}) %collective-permute-start.6) | collective-permute-done | bytes 663584 | tf_op jit(solution)/shard_map/ppermute | solution.py:541
  59.1 3.1 collective-permute-start.8
  62.1 4.8 %collective-permute-done.4.rest_6_.rest_12_ = bf16[448,768]{1,0:T(8,128)(2,1)S(1)} collective-permute-done((bf16[448,768]{1,0:T(8,128)(2,1)S(1)}, bf16[448,768]{1,0:T(8,128)(2,1)S(1)}, u32[]{:S(2)}, u32[]{:S(2)}) %collective-permute-start.4) | collective-permute-done | bytes 688160 | tf_op jit(solution)/shard_map/ppermute | solution.py:541
  68.8 1.8 collective-permute-start.7
  70.6 2.0 collective-permute-done.8.rest_3_
  72.6 1.5 collective-permute-start.14
  74.1 1.5 collective-permute-start.15
  75.7 5.3 %collective-permute-done.7.rest_1_ = bf16[256,768]{1,0:T(8,128)(2,1)S(1)} collective-permute-done((bf16[256,768]{1,0:T(8,128)(2,1)S(1)}, bf16[256,768]{1,0:T(8,128)(2,1)S(1)}, u32[]{:S(2)}, u32[]{:S(2)}) %collective-permute-start.7) | collective-permute-done | bytes 393248 | tf_op jit(solution)/shard_map/ppermute | solution.py:541
  83.1 2.9 collective-permute-start.17
  86.1 2.2 collective-permute-start.18
  88.2 9.6 %project.1 = (f32[1024,768]{1,0:T(8,128)}, bf16[1024,768]{1,0:T(8,128)(2,1)}, bf16[1024,768]{1,0:T(8,128)(2,1)}, bf16[1024,768]{1,0:T(8,128)(2,1)}, bf16[1024,76...) custom-call(s32[1]{0:T(128)} %bitcast.me_ref, ...), custom_call_target="tpu_custom_call" | custom-call | flops 3623878656 | bytes 20000000 | tf_op jit(solution)/shard_map/project/pallas_call | solution.py:204
  97.8 8.7 %attn_fwd.2 = (bf16[1024,256]{1,0:T(8,128)(2,1)}, bf16[2,1024,128]{2,1,0:T(8,128)(2,1)}) custom-call(bf16[1024,768]{1,0:T(8,128)(2,1)} %get-tuple-element.222.q_ref.rest_0_, bf16[1024,768]{1,0:T(8,128)(2,1)} %get-tuple-element.186.k_ref.rest_1_, bf16[1024,768]{1,0:T(8,128)(2,1)} %get-tuple-element.187.v_ref.rest_2_, ...), custom_call_target="tpu_custom_call" | custom-call | flops 1073741824 | bytes 2621440 | tf_op jit(solution)/shard_map/attn_fwd/pallas_call | solution.py:51
  109.9 2.8 collective-permute-start.23
  112.7 15.2 %attn_fwd.3 = (bf16[1024,512]{1,0:T(8,128)(2,1)}, bf16[4,1024,128]{2,1,0:T(8,128)(2,1)}) custom-call(bf16[1024,768]{1,0:T(8,128)(2,1)} %get-tuple-element.222.q_ref.rest_0_, bf16[1024,768]{1,0:T(8,128)(2,1)} %get-tuple-element.186.k_ref.rest_1_, bf16[1024,768]{1,0:T(8,128)(2,1)} %get-tuple-element.187.v_ref.rest_2_, ...), custom_call_target="tpu_custom_call" | custom-call | flops 2147483648 | bytes 5242880 | tf_op jit(solution)/shard_map/attn_fwd/pallas_call | solution.py:51
  128.5 2.8 collective-permute-done.25.rest_17_
  132.4 51.8 %middle.1 = (bf16[256,768]{1,0:T(8,128)(2,1)}, bf16[256,768]{1,0:T(8,128)(2,1)}, bf16[256,768]{1,0:T(8,128)(2,1)}, bf16[256,768]{1,0:T(8,128)(2,1)}, f32[1024,76...) custom-call(s32[1]{0:T(128)} %bitcast.me_ref, ...), custom_call_target="tpu_custom_call" | custom-call | flops 32614907904 | bytes 60000000 | tf_op jit(solution)/shard_map/middle/pallas_call | solution.py:527
  184.4 3.9 %collective-permute-start.27 = (bf16[256,768]{1,0:T(8,128)(2,1)}, bf16[256,768]{1,0:T(8,128)(2,1)S(1)}, u32[]{:S(2)}, u32[]{:S(2)}) collective-permute-start(bf16[256,768]{1,0:T(8,128)(2,1)} %get-tuple-element.215), channel_id=1, source_target_pairs={{0,1},{1,0},{2,3},{3,2},{4,5},{5,4},{6,7},{7,6},{8,9},{9,8},{10,11... | collective-permute-start | bytes 1179656 | tf_op jit(solution)/shard_map/ppermute | solution.py:541
  188.3 14.6 %attn_bwd.1.rest_9_.rest_0_ = bf16[3,1024,256]{2,1,0:T(8,128)(2,1)} custom-call(bf16[1024,768]{1,0:T(8,128)(2,1)} %get-tuple-element.222.q_ref.rest_0_, bf16[1024,768]{1,0:T(8,128)(2,1)} %get-tuple-element.186.k_ref.rest_1_, bf16[1024,768]{1,0:T(8,128)(2,1)} %get-tuple-element.187.v_ref.rest_2_, bf16[1024,768]{1,0:T(8,128)(2,1)} %get-tuple-element.219.do_ref.rest_3_, ...), custom_call_target="tpu_custom_call" | custom-call | flops 2684354560 | bytes 4718592 | tf_op jit(solution)/shard_map/attn_bwd/pallas_call | solution.py:103
  202.9 5.2 %sum_three.2 = (bf16[864,768]{1,0:T(8,128)(2,1)}, bf16[864,768]{1,0:T(8,128)(2,1)}, bf16[864,768]{1,0:T(8,128)(2,1)}) custom-call(bf16[4,864,768]{2,1,0:T(8,128)(2,1)} %get-tuple-element.248.a1.a2.a3.a, bf16[4,864,768]{2,1,0:T(8,128)(2,1)} %collective-permute-done.26.b1.b2.b3.b, bf16[4,864,768]{2,1,0:T(8,128)(2,1)} %get-tuple-element.248.a1.a2.a3.a, ...), custom_call_target="tpu_custom_call" | custom-call | tf_op jit(solution)/shard_map/sum_three/pallas_call | solution.py:326
  208.1 1.6 collective-permute-start.30
  210.3 1.4 collective-permute-start.32
  212.6 1.5 collective-permute-start.29
  214.0 33.0 %attn_finish.1 = (bf16[3,1024,512]{2,1,0:T(8,128)(2,1)}, bf16[256,768]{1,0:T(8,128)(2,1)}, bf16[256,768]{1,0:T(8,128)(2,1)}, bf16[256,768]{1,0:T(8,128)(2,1)}, b...) custom-call(s32[1]{0:T(128)} %bitcast.me_ref, s32[4,2]{1,0:T(4,128)} %pad_add_fusion.info_ref, ...), custom_call_target="tpu_custom_call" | custom-call | flops 5368709120 | bytes 9437184 | tf_op jit(solution)/shard_map/attn_finish/pallas_call | solution.py:258
  247.1 1.6 collective-permute-start.33
  248.7 1.4 collective-permute-start.34
  250.1 10.5 %weight_grads.1 = (bf16[4,448,768]{2,1,0:T(8,128)(2,1)}, bf16[4,448,768]{2,1,0:T(8,128)(2,1)}) custom-call(s32[1]{0:T(128)} %bitcast.me_ref, bf16[1024,768]{1,0:T(8,128)(2,1)} %get-tuple-element.240.inp_ref, f32[8,768]{1,0:T(8,128)} %get-tuple-element.241.rows_ref, bf16[8,768]{1,0:T(8,128)(2,1)} %get-tuple-element.242.hid_ref, ...), custom_call_target="tpu_custom_call" | custom-call | flops 3623878656 | bytes 12000000 | tf_op jit(solution)/shard_map/weight_grads/pallas_call | solution.py:307
  260.6 5.9 %collective-permute-done.33 = bf16[256,768]{1,0:T(8,128)(2,1)} collective-permute-done((bf16[256,768]{1,0:T(8,128)(2,1)}, bf16[256,768]{1,0:T(8,128)(2,1)}, u32[]{:S(2)}, u32[]{:S(2)}) %collective-permute-start.33) | collective-permute-done | bytes 393248 | tf_op jit(solution)/shard_map/ppermute | solution.py:541
  266.5 2.6 collective-permute-done.34
  271.1 4.7 %sum_own.1 = (f32[2,216,768]{2,1,0:T(8,128)}, bf16[2,216,768]{2,1,0:T(8,128)(2,1)}) custom-call(s32[1]{0:T(128)} %bitcast.27.inner_ref, bf16[4,864,768]{2,1,0:T(8,128)(2,1)} %get-tuple-element.248.a1.a2.a3.a, bf16[4,864,768]{2,1,0:T(8,128)(2,1)} %collective-permute-done.26.b1.b2.b3.b, bf16[864,768]{1,0:T(8,128)(2,1)} %copy-done.4, ...), custom_call_target="tpu_custom_call" | custom-call | tf_op jit(solution)/shard_map/sum_own/pallas_call | solution.py:351
  278.2 2.3 collective-permute-start.41
  282.5 1.5 collective-permute-start.37
  285.2 7.8 %collective-permute-done.39 = bf16[2,216,768]{2,1,0:T(8,128)(2,1)S(1)} collective-permute-done((bf16[2,216,768]{2,1,0:T(8,128)(2,1)}, bf16[2,216,768]{2,1,0:T(8,128)(2,1)S(1)}, u32[]{:S(2)}, u32[]{:S(2)}) %collective-permute-start.39) | collective-permute-done | bytes 663584 | tf_op jit(solution)/shard_map/ppermute | solution.py:541
  293.3 1.7 collective-permute-start.40
  296.1 6.6 %collective-permute-done.41 = bf16[256,768]{1,0:T(8,128)(2,1)S(1)} collective-permute-done((bf16[256,768]{1,0:T(8,128)(2,1)S(1)}, bf16[256,768]{1,0:T(8,128)(2,1)S(1)}, u32[]{:S(2)}, u32[]{:S(2)}) %collective-permute-start.41) | collective-permute-done | bytes 393248 | tf_op jit(solution)/shard_map/ppermute | solution.py:541
  302.6 13.7 %collective-permute-done.40 = bf16[1,216,768]{2,1,0:T(8,128)(2,1)S(1)} collective-permute-done((bf16[1,216,768]{2,1,0:T(8,128)(2,1)S(1)}, bf16[1,216,768]{2,1,0:T(8,128)(2,1)S(1)}, u32[]{:S(2)}, u32[]{:S(2)}) %collective-permute-start.40) | collective-permute-done | bytes 331808 | tf_op jit(solution)/shard_map/ppermute | solution.py:541
  316.3 1.3 sum_direct.1
  317.6 1.6 collective-permute-start.42
  319.2 2.8 collective-permute-start.44
  326.8 6.4 %collective-permute-done.43.refs_2_ = bf16[112,768]{1,0:T(8,128)(2,1)S(1)} collective-permute-done((bf16[112,768]{1,0:T(8,128)(2,1)S(1)}, bf16[112,768]{1,0:T(8,128)(2,1)S(1)}, u32[]{:S(2)}, u32[]{:S(2)}) %collective-permute-start.43) | collective-permute-done | bytes 172064 | tf_op jit(solution)/shard_map/ppermute | solution.py:541
  (170 shorter events, 33.1 us)
Async XLA Ops:
  2.8 13.1 %collective-permute-start = (bf16[1,112,768]{2,1,0:T(8,128)(2,1)}, bf16[1,112,768]{2,1,0:T(8,128)(2,1)S(1)}, u32[]{:S(2)}, u32[]{:S(2)}) collective-permute-start(bf16[1,112,768]{2,1,0:T(8,128)(2,1)} %bitcast.67), channel_id=1, source_target_pairs={{0,2},{1,3},{2,0},{3,1},{4,6},{5,7},{6,4},{7,5},{8,10},{9,11},{10,... | collective-permute-start | bytes 516104 | tf_op jit(solution)/shard_map/ppermute | solution.py:541
  16.0 17.4 %collective-permute-start.2 = (bf16[1,216,768]{2,1,0:T(8,128)(2,1)S(1)}, bf16[1,216,768]{2,1,0:T(8,128)(2,1)S(1)}, u32[]{:S(2)}, u32[]{:S(2)}) collective-permute-start(bf16[1,216,768]{2,1,0:T(8,128)(2,1)S(1)} %bitcast.65), channel_id=1, source_target_pairs={{0,2},{1,3},{2,0},{3,1},{4,6},{5,7},{6,4},{7,5},{8,10},{9,11},{10,... | collective-permute-start | bytes 995336 | tf_op jit(solution)/shard_map/ppermute | solution.py:541
  16.7 17.2 %collective-permute-start.1 = (bf16[2,112,768]{2,1,0:T(8,128)(2,1)S(1)}, bf16[2,112,768]{2,1,0:T(8,128)(2,1)S(1)}, u32[]{:S(2)}, u32[]{:S(2)}) collective-permute-start(bf16[2,112,768]{2,1,0:T(8,128)(2,1)S(1)} %pad_maximum_fusion.4), channel_id=1, source_target_pairs={{0,1},{1,0},{2,3},{3,2},{4,5},{5,4},{6,7},{7,6},{8,9},{9,8},{10,11... | collective-permute-start | bytes 1032200 | tf_op jit(solution)/shard_map/ppermute | solution.py:541
  34.6 24.5 %copy-start.9 = (bf16[448,768]{1,0:T(8,128)(2,1)}, bf16[448,768]{1,0:T(8,128)(2,1)S(1)}, u32[]{:S(2)}) copy-start(bf16[448,768]{1,0:T(8,128)(2,1)S(1)} %pad_maximum_fusion.2.rest_4_.rest_10_) | copy-start | bytes 2064388
  35.2 23.7 %collective-permute-start.6 = (bf16[2,216,768]{2,1,0:T(8,128)(2,1)S(1)}, bf16[2,216,768]{2,1,0:T(8,128)(2,1)S(1)}, u32[]{:S(2)}, u32[]{:S(2)}) collective-permute-start(bf16[2,216,768]{2,1,0:T(8,128)(2,1)S(1)} %pad_maximum_fusion.3), channel_id=1, source_target_pairs={{0,1},{1,0},{2,3},{3,2},{4,5},{5,4},{6,7},{7,6},{8,9},{9,8},{10,11... | collective-permute-start | bytes 1990664 | tf_op jit(solution)/shard_map/ppermute | solution.py:541
  35.2 26.9 %collective-permute-start.3 = (bf16[448,768]{1,0:T(8,128)(2,1)S(1)}, bf16[448,768]{1,0:T(8,128)(2,1)S(1)}, u32[]{:S(2)}, u32[]{:S(2)}) collective-permute-start(bf16[448,768]{1,0:T(8,128)(2,1)S(1)} %pad_maximum_fusion.2.rest_4_.rest_10_), channel_id=1, source_target_pairs={{0,8},{1,9},{2,10},{3,11},{4,12},{5,13},{6,14},{7,15},{8,0},{9,1},... | collective-permute-start | bytes 2064392 | tf_op jit(solution)/shard_map/ppermute | solution.py:541
  36.7 30.3 %collective-permute-start.4 = (bf16[448,768]{1,0:T(8,128)(2,1)S(1)}, bf16[448,768]{1,0:T(8,128)(2,1)S(1)}, u32[]{:S(2)}, u32[]{:S(2)}) collective-permute-start(bf16[448,768]{1,0:T(8,128)(2,1)S(1)} %pad_maximum_fusion.2.rest_4_.rest_10_), channel_id=1, source_target_pairs={{0,16},{1,17},{2,18},{3,19},{4,20},{5,21},{6,22},{7,23},{8,24},{9,... | collective-permute-start | bytes 2064392 | tf_op jit(solution)/shard_map/ppermute | solution.py:541
  38.2 20.8 %collective-permute-start.5 = (bf16[256,768]{1,0:T(8,128)(2,1)S(1)}, bf16[256,768]{1,0:T(8,128)(2,1)S(1)}, u32[]{:S(2)}, u32[]{:S(2)}) collective-permute-start(bf16[256,768]{1,0:T(8,128)(2,1)S(1)} %get-tuple-element.172), channel_id=1, source_target_pairs={{0,2},{1,3},{2,0},{3,1},{4,6},{5,7},{6,4},{7,5},{8,10},{9,11},{10,... | collective-permute-start | bytes 1179656 | tf_op jit(solution)/shard_map/ppermute | solution.py:541
  41.8 32.3 %collective-permute-start.9 = (bf16[448,768]{1,0:T(8,128)(2,1)S(1)}, bf16[448,768]{1,0:T(8,128)(2,1)S(1)}, u32[]{:S(2)}, u32[]{:S(2)}) collective-permute-start(bf16[448,768]{1,0:T(8,128)(2,1)S(1)} %pad_maximum_fusion.2.rest_4_.rest_10_), channel_id=1, source_target_pairs={{0,24},{1,25},{2,26},{3,27},{4,28},{5,29},{6,30},{7,31},{8,16},{9,... | collective-permute-start | bytes 2064392 | tf_op jit(solution)/shard_map/ppermute | solution.py:541
  58.9 16.8 %collective-permute-start.10 = (bf16[448,768]{1,0:T(8,128)(2,1)S(1)}, bf16[448,768]{1,0:T(8,128)(2,1)S(1)}, u32[]{:S(2)}, u32[]{:S(2)}) collective-permute-start(bf16[448,768]{1,0:T(8,128)(2,1)S(1)} %pad_maximum_fusion.2.rest_4_.rest_10_), channel_id=1, source_target_pairs={{0,4},{1,5},{2,6},{3,7},{4,0},{5,1},{6,2},{7,3},{8,12},{9,13},{10,... | collective-permute-start | bytes 2064392 | tf_op jit(solution)/shard_map/ppermute | solution.py:541
  59.1 13.6 %collective-permute-start.8 = (bf16[256,768]{1,0:T(8,128)(2,1)S(1)}, bf16[256,768]{1,0:T(8,128)(2,1)S(1)}, u32[]{:S(2)}, u32[]{:S(2)}) collective-permute-start(bf16[256,768]{1,0:T(8,128)(2,1)S(1)} %get-tuple-element.177), channel_id=1, source_target_pairs={{0,3},{1,2},{2,1},{3,0},{4,7},{5,6},{6,5},{7,4},{8,11},{9,10},{10,... | collective-permute-start | bytes 1179656 | tf_op jit(solution)/shard_map/ppermute | solution.py:541
  67.5 13.7 %collective-permute-start.11 = (bf16[448,768]{1,0:T(8,128)(2,1)S(1)}, bf16[448,768]{1,0:T(8,128)(2,1)S(1)}, u32[]{:S(2)}, u32[]{:S(2)}) collective-permute-start(bf16[448,768]{1,0:T(8,128)(2,1)S(1)} %collective-permute-done.3.rest_5_.rest_11_), channel_id=1, source_target_pairs={{0,4},{1,5},{2,6},{3,7},{4,0},{5,1},{6,2},{7,3},{8,12},{9,13},{10,... | collective-permute-start | bytes 2064392 | tf_op jit(solution)/shard_map/ppermute | solution.py:541
  68.8 12.1 %collective-permute-start.7 = (bf16[256,768]{1,0:T(8,128)(2,1)S(1)}, bf16[256,768]{1,0:T(8,128)(2,1)S(1)}, u32[]{:S(2)}, u32[]{:S(2)}) collective-permute-start(bf16[256,768]{1,0:T(8,128)(2,1)S(1)} %get-tuple-element.175), channel_id=1, source_target_pairs={{0,1},{1,0},{2,3},{3,2},{4,5},{5,4},{6,7},{7,6},{8,9},{9,8},{10,11... | collective-permute-start | bytes 1179656 | tf_op jit(solution)/shard_map/ppermute | solution.py:541
  72.6 33.9 %collective-permute-start.14 = (bf16[864,768]{1,0:T(8,128)(2,1)S(1)}, bf16[864,768]{1,0:T(8,128)(2,1)}, u32[]{:S(2)}, u32[]{:S(2)}) collective-permute-start(bf16[864,768]{1,0:T(8,128)(2,1)S(1)} %pad_maximum_fusion.1.rest_8_), channel_id=1, source_target_pairs={{0,8},{1,9},{2,10},{3,11},{4,12},{5,13},{6,14},{7,15},{8,0},{9,1},... | collective-permute-start | bytes 3981320 | tf_op jit(solution)/shard_map/ppermute | solution.py:541
  74.1 32.4 %collective-permute-start.15 = (bf16[864,768]{1,0:T(8,128)(2,1)S(1)}, bf16[864,768]{1,0:T(8,128)(2,1)S(1)}, u32[]{:S(2)}, u32[]{:S(2)}) collective-permute-start(bf16[864,768]{1,0:T(8,128)(2,1)S(1)} %pad_maximum_fusion.1.rest_8_), channel_id=1, source_target_pairs={{0,16},{1,17},{2,18},{3,19},{4,20},{5,21},{6,22},{7,23},{8,24},{9,... | collective-permute-start | bytes 3981320 | tf_op jit(solution)/shard_map/ppermute | solution.py:541
  75.7 30.8 %collective-permute-start.16 = (bf16[864,768]{1,0:T(8,128)(2,1)S(1)}, bf16[864,768]{1,0:T(8,128)(2,1)}, u32[]{:S(2)}, u32[]{:S(2)}) collective-permute-start(bf16[864,768]{1,0:T(8,128)(2,1)S(1)} %pad_maximum_fusion.1.rest_8_), channel_id=1, source_target_pairs={{0,4},{1,5},{2,6},{3,7},{4,0},{5,1},{6,2},{7,3},{8,12},{9,13},{10,... | collective-permute-start | bytes 3981320 | tf_op jit(solution)/shard_map/ppermute | solution.py:541
  81.0 2.1 collective-permute-start.12
  81.2 4.9 %collective-permute-start.13 = (bf16[448,768]{1,0:T(8,128)(2,1)S(1)}, bf16[448,768]{1,0:T(8,128)(2,1)S(1)}, u32[]{:S(2)}, u32[]{:S(2)}) collective-permute-start(bf16[448,768]{1,0:T(8,128)(2,1)S(1)} %collective-permute-done.9.rest_7_.rest_13_), channel_id=1, source_target_pairs={{0,4},{1,5},{2,6},{3,7},{4,0},{5,1},{6,2},{7,3},{8,12},{9,13},{10,... | collective-permute-start | bytes 2064392 | tf_op jit(solution)/shard_map/ppermute | solution.py:541
  83.1 23.4 %collective-permute-start.17 = (bf16[256,768]{1,0:T(8,128)(2,1)S(1)}, bf16[256,768]{1,0:T(8,128)(2,1)}, u32[]{:S(2)}, u32[]{:S(2)}) collective-permute-start(bf16[256,768]{1,0:T(8,128)(2,1)S(1)} %get-tuple-element.183), channel_id=1, source_target_pairs={{0,1},{1,0},{2,3},{3,2},{4,5},{5,4},{6,7},{7,6},{8,9},{9,8},{10,11... | collective-permute-start | bytes 1179656 | tf_op jit(solution)/shard_map/ppermute | solution.py:541
  86.1 20.4 %collective-permute-start.18 = (bf16[256,768]{1,0:T(8,128)(2,1)S(1)}, bf16[256,768]{1,0:T(8,128)(2,1)}, u32[]{:S(2)}, u32[]{:S(2)}) collective-permute-start(bf16[256,768]{1,0:T(8,128)(2,1)S(1)} %get-tuple-element.184), channel_id=1, source_target_pairs={{0,2},{1,3},{2,0},{3,1},{4,6},{5,7},{6,4},{7,5},{8,10},{9,11},{10,... | collective-permute-start | bytes 1179656 | tf_op jit(solution)/shard_map/ppermute | solution.py:541
  106.5 21.4 %collective-permute-start.21 = (bf16[864,768]{1,0:T(8,128)(2,1)}, bf16[864,768]{1,0:T(8,128)(2,1)}, u32[]{:S(2)}, u32[]{:S(2)}) collective-permute-start(bf16[864,768]{1,0:T(8,128)(2,1)} %collective-permute-done.14.rest_9_), channel_id=1, source_target_pairs={{0,4},{1,5},{2,6},{3,7},{4,0},{5,1},{6,2},{7,3},{8,12},{9,13},{10,... | collective-permute-start | bytes 3981320 | tf_op jit(solution)/shard_map/ppermute | solution.py:541
  106.6 21.3 %collective-permute-start.22 = (bf16[864,768]{1,0:T(8,128)(2,1)S(1)}, bf16[864,768]{1,0:T(8,128)(2,1)}, u32[]{:S(2)}, u32[]{:S(2)}) collective-permute-start(bf16[864,768]{1,0:T(8,128)(2,1)S(1)} %collective-permute-done.15.rest_10_), channel_id=1, source_target_pairs={{0,4},{1,5},{2,6},{3,7},{4,0},{5,1},{6,2},{7,3},{8,12},{9,13},{10,... | collective-permute-start | bytes 3981320 | tf_op jit(solution)/shard_map/ppermute | solution.py:541
  107.2 20.7 %collective-permute-start.19 = (bf16[480,768]{1,0:T(8,128)(2,1)S(1)}, bf16[480,768]{1,0:T(8,128)(2,1)S(1)}, u32[]{:S(2)}, u32[]{:S(2)}) collective-permute-start(bf16[480,768]{1,0:T(8,128)(2,1)S(1)} %slice.89), channel_id=1, source_target_pairs={{0,8},{1,9},{2,10},{3,11},{4,12},{5,13},{6,14},{7,15},{8,0},{9,1},... | collective-permute-start | bytes 2211848 | tf_op jit(solution)/shard_map/ppermute | solution.py:541
  108.9 19.0 %collective-permute-start.20 = (bf16[384,768]{1,0:T(8,128)(2,1)S(1)}, bf16[384,768]{1,0:T(8,128)(2,1)}, u32[]{:S(2)}, u32[]{:S(2)}) collective-permute-start(bf16[384,768]{1,0:T(8,128)(2,1)S(1)} %slice.90), channel_id=1, source_target_pairs={{0,16},{1,17},{2,18},{3,19},{4,20},{5,21},{6,22},{7,23},{8,24},{9,... | collective-permute-start | bytes 1769480 | tf_op jit(solution)/shard_map/ppermute | solution.py:541
  109.9 18.0 %collective-permute-start.23 = (bf16[256,768]{1,0:T(8,128)(2,1)S(1)}, bf16[256,768]{1,0:T(8,128)(2,1)}, u32[]{:S(2)}, u32[]{:S(2)}) collective-permute-start(bf16[256,768]{1,0:T(8,128)(2,1)S(1)} %get-tuple-element.199), channel_id=1, source_target_pairs={{0,3},{1,2},{2,1},{3,0},{4,7},{5,6},{6,5},{7,4},{8,11},{9,10},{10,... | collective-permute-start | bytes 1179656 | tf_op jit(solution)/shard_map/ppermute | solution.py:541
  127.9 3.3 collective-permute-start.24
  128.0 3.3 collective-permute-start.25
  184.2 18.7 %collective-permute-start.26 = (bf16[4,864,768]{2,1,0:T(8,128)(2,1)}, bf16[4,864,768]{2,1,0:T(8,128)(2,1)}, u32[]{:S(2)}, u32[]{:S(2)}) collective-permute-start(bf16[4,864,768]{2,1,0:T(8,128)(2,1)} %get-tuple-element.214), channel_id=1, source_target_pairs={{0,4},{1,5},{2,6},{3,7},{4,0},{5,1},{6,2},{7,3},{8,12},{9,13},{10,... | collective-permute-start | bytes 15925256 | tf_op jit(solution)/shard_map/ppermute | solution.py:541
  184.4 18.5 %collective-permute-start.27 = (bf16[256,768]{1,0:T(8,128)(2,1)}, bf16[256,768]{1,0:T(8,128)(2,1)S(1)}, u32[]{:S(2)}, u32[]{:S(2)}) collective-permute-start(bf16[256,768]{1,0:T(8,128)(2,1)} %get-tuple-element.215), channel_id=1, source_target_pairs={{0,1},{1,0},{2,3},{3,2},{4,5},{5,4},{6,7},{7,6},{8,9},{9,8},{10,11... | collective-permute-start | bytes 1179656 | tf_op jit(solution)/shard_map/ppermute | solution.py:541
  208.1 61.0 %collective-permute-start.30 = (bf16[864,768]{1,0:T(8,128)(2,1)}, bf16[864,768]{1,0:T(8,128)(2,1)S(1)}, u32[]{:S(2)}, u32[]{:S(2)}) collective-permute-start(bf16[864,768]{1,0:T(8,128)(2,1)} %get-tuple-element.250), channel_id=1, source_target_pairs={{0,8},{1,9},{2,10},{3,11},{4,12},{5,13},{6,14},{7,15},{8,0},{9,1},... | collective-permute-start | bytes 3981320 | tf_op jit(solution)/shard_map/ppermute | solution.py:541
  209.7 59.5 %collective-permute-start.31 = (bf16[864,768]{1,0:T(8,128)(2,1)}, bf16[864,768]{1,0:T(8,128)(2,1)S(1)}, u32[]{:S(2)}, u32[]{:S(2)}) collective-permute-start(bf16[864,768]{1,0:T(8,128)(2,1)} %get-tuple-element.251), channel_id=1, source_target_pairs={{0,16},{1,17},{2,18},{3,19},{4,20},{5,21},{6,22},{7,23},{8,24},{9,... | collective-permute-start | bytes 3981320 | tf_op jit(solution)/shard_map/ppermute | solution.py:541
  210.3 58.9 %collective-permute-start.32 = (bf16[864,768]{1,0:T(8,128)(2,1)}, bf16[864,768]{1,0:T(8,128)(2,1)S(1)}, u32[]{:S(2)}, u32[]{:S(2)}) collective-permute-start(bf16[864,768]{1,0:T(8,128)(2,1)} %get-tuple-element.252), channel_id=1, source_target_pairs={{0,24},{1,25},{2,26},{3,27},{4,28},{5,29},{6,30},{7,31},{8,16},{9,... | collective-permute-start | bytes 3981320 | tf_op jit(solution)/shard_map/ppermute | solution.py:541
  211.6 35.4 %collective-permute-start.28 = (bf16[256,768]{1,0:T(8,128)(2,1)}, bf16[256,768]{1,0:T(8,128)(2,1)}, u32[]{:S(2)}, u32[]{:S(2)}) collective-permute-start(bf16[256,768]{1,0:T(8,128)(2,1)} %get-tuple-element.234), channel_id=1, source_target_pairs={{0,2},{1,3},{2,0},{3,1},{4,6},{5,7},{6,4},{7,5},{8,10},{9,11},{10,... | collective-permute-start | bytes 1179656 | tf_op jit(solution)/shard_map/ppermute | solution.py:541
  212.6 34.5 %collective-permute-start.29 = (bf16[256,768]{1,0:T(8,128)(2,1)}, bf16[256,768]{1,0:T(8,128)(2,1)}, u32[]{:S(2)}, u32[]{:S(2)}) collective-permute-start(bf16[256,768]{1,0:T(8,128)(2,1)} %get-tuple-element.235), channel_id=1, source_target_pairs={{0,3},{1,2},{2,1},{3,0},{4,7},{5,6},{6,5},{7,4},{8,11},{9,10},{10,... | collective-permute-start | bytes 1179656 | tf_op jit(solution)/shard_map/ppermute | solution.py:541
  247.1 19.4 %collective-permute-start.33 = (bf16[256,768]{1,0:T(8,128)(2,1)}, bf16[256,768]{1,0:T(8,128)(2,1)}, u32[]{:S(2)}, u32[]{:S(2)}) collective-permute-start(bf16[256,768]{1,0:T(8,128)(2,1)} %get-tuple-element.253), channel_id=1, source_target_pairs={{0,1},{1,0},{2,3},{3,2},{4,5},{5,4},{6,7},{7,6},{8,9},{9,8},{10,11... | collective-permute-start | bytes 1179656 | tf_op jit(solution)/shard_map/ppermute | solution.py:541
  248.7 20.4 %collective-permute-start.34 = (bf16[256,768]{1,0:T(8,128)(2,1)}, bf16[256,768]{1,0:T(8,128)(2,1)}, u32[]{:S(2)}, u32[]{:S(2)}) collective-permute-start(bf16[256,768]{1,0:T(8,128)(2,1)} %get-tuple-element.254), channel_id=1, source_target_pairs={{0,2},{1,3},{2,0},{3,1},{4,6},{5,7},{6,4},{7,5},{8,10},{9,11},{10,... | collective-permute-start | bytes 1179656 | tf_op jit(solution)/shard_map/ppermute | solution.py:541
  270.7 9.7 %collective-permute-start.35 = (bf16[4,448,768]{2,1,0:T(8,128)(2,1)}, bf16[4,448,768]{2,1,0:T(8,128)(2,1)S(1)}, u32[]{:S(2)}, u32[]{:S(2)}) collective-permute-start(bf16[4,448,768]{2,1,0:T(8,128)(2,1)} %get-tuple-element.256), channel_id=1, source_target_pairs={{0,4},{1,5},{2,6},{3,7},{4,0},{5,1},{6,2},{7,3},{8,12},{9,13},{10,... | collective-permute-start | bytes 8257544 | tf_op jit(solution)/shard_map/ppermute | solution.py:541
  275.8 17.2 %collective-permute-start.39 = (bf16[2,216,768]{2,1,0:T(8,128)(2,1)}, bf16[2,216,768]{2,1,0:T(8,128)(2,1)S(1)}, u32[]{:S(2)}, u32[]{:S(2)}) collective-permute-start(bf16[2,216,768]{2,1,0:T(8,128)(2,1)} %get-tuple-element.268), channel_id=1, source_target_pairs={{0,1},{1,0},{2,3},{3,2},{4,5},{5,4},{6,7},{7,6},{8,9},{9,8},{10,11... | collective-permute-start | bytes 1990664 | tf_op jit(solution)/shard_map/ppermute | solution.py:541
  278.2 14.9 %copy-start.7 = (f32[2,216,768]{2,1,0:T(8,128)S(1)}, f32[2,216,768]{2,1,0:T(8,128)}, u32[]{:S(2)}) copy-start(f32[2,216,768]{2,1,0:T(8,128)} %get-tuple-element.267) | copy-start | bytes 3981316
  278.2 24.5 %collective-permute-start.41 = (bf16[256,768]{1,0:T(8,128)(2,1)S(1)}, bf16[256,768]{1,0:T(8,128)(2,1)S(1)}, u32[]{:S(2)}, u32[]{:S(2)}) collective-permute-start(bf16[256,768]{1,0:T(8,128)(2,1)S(1)} %copy-done.27), channel_id=1, source_target_pairs={{0,3},{1,2},{2,1},{3,0},{4,7},{5,6},{6,5},{7,4},{8,11},{9,10},{10,... | collective-permute-start | bytes 1179656 | tf_op jit(solution)/shard_map/ppermute | solution.py:541
  281.6 34.7 %collective-permute-start.36 = (bf16[448,768]{1,0:T(8,128)(2,1)S(1)}, bf16[448,768]{1,0:T(8,128)(2,1)S(1)}, u32[]{:S(2)}, u32[]{:S(2)}) collective-permute-start(bf16[448,768]{1,0:T(8,128)(2,1)S(1)} %get-tuple-element.257), channel_id=1, source_target_pairs={{0,8},{1,9},{2,10},{3,11},{4,12},{5,13},{6,14},{7,15},{8,0},{9,1},... | collective-permute-start | bytes 2064392 | tf_op jit(solution)/shard_map/ppermute | solution.py:541
  282.5 33.8 %collective-permute-start.37 = (bf16[448,768]{1,0:T(8,128)(2,1)S(1)}, bf16[448,768]{1,0:T(8,128)(2,1)S(1)}, u32[]{:S(2)}, u32[]{:S(2)}) collective-permute-start(bf16[448,768]{1,0:T(8,128)(2,1)S(1)} %get-tuple-element.258), channel_id=1, source_target_pairs={{0,16},{1,17},{2,18},{3,19},{4,20},{5,21},{6,22},{7,23},{8,24},{9,... | collective-permute-start | bytes 2064392 | tf_op jit(solution)/shard_map/ppermute | solution.py:541
  284.0 32.3 %collective-permute-start.38 = (bf16[448,768]{1,0:T(8,128)(2,1)S(1)}, bf16[448,768]{1,0:T(8,128)(2,1)S(1)}, u32[]{:S(2)}, u32[]{:S(2)}) collective-permute-start(bf16[448,768]{1,0:T(8,128)(2,1)S(1)} %get-tuple-element.259), channel_id=1, source_target_pairs={{0,24},{1,25},{2,26},{3,27},{4,28},{5,29},{6,30},{7,31},{8,16},{9,... | collective-permute-start | bytes 2064392 | tf_op jit(solution)/shard_map/ppermute | solution.py:541
  293.3 23.0 %collective-permute-start.40 = (bf16[1,216,768]{2,1,0:T(8,128)(2,1)S(1)}, bf16[1,216,768]{2,1,0:T(8,128)(2,1)S(1)}, u32[]{:S(2)}, u32[]{:S(2)}) collective-permute-start(bf16[1,216,768]{2,1,0:T(8,128)(2,1)S(1)} %slice.108), channel_id=1, source_target_pairs={{0,2},{1,3},{2,0},{3,1},{4,6},{5,7},{6,4},{7,5},{8,10},{9,11},{10,... | collective-permute-start | bytes 995336 | tf_op jit(solution)/shard_map/ppermute | solution.py:541
  296.0 21.6 %copy-start.2 = (bf16[4,256,768]{2,1,0:T(8,128)(2,1)}, bf16[4,256,768]{2,1,0:T(8,128)(2,1)S(1)}, u32[]{:S(2)}) copy-start(bf16[4,256,768]{2,1,0:T(8,128)(2,1)S(1)} %bitcast_dynamic-update-slice_fusion) | copy-start | bytes 4718596
  317.6 9.2 %collective-permute-start.42 = (bf16[112,768]{1,0:T(8,128)(2,1)S(1)}, bf16[112,768]{1,0:T(8,128)(2,1)S(1)}, u32[]{:S(2)}, u32[]{:S(2)}) collective-permute-start(bf16[112,768]{1,0:T(8,128)(2,1)S(1)} %get-tuple-element.281), channel_id=1, source_target_pairs={{0,3},{1,2},{2,1},{3,0},{4,7},{5,6},{6,5},{7,4},{8,11},{9,10},{10,... | collective-permute-start | bytes 516104 | tf_op jit(solution)/shard_map/ppermute | solution.py:541
  319.2 14.0 %collective-permute-start.43 = (bf16[112,768]{1,0:T(8,128)(2,1)S(1)}, bf16[112,768]{1,0:T(8,128)(2,1)S(1)}, u32[]{:S(2)}, u32[]{:S(2)}) collective-permute-start(bf16[112,768]{1,0:T(8,128)(2,1)S(1)} %get-tuple-element.282), channel_id=1, source_target_pairs={{0,2},{1,3},{2,0},{3,1},{4,6},{5,7},{6,4},{7,5},{8,10},{9,11},{10,... | collective-permute-start | bytes 516104 | tf_op jit(solution)/shard_map/ppermute | solution.py:541
  319.2 14.0 %collective-permute-start.44 = (bf16[112,768]{1,0:T(8,128)(2,1)S(1)}, bf16[112,768]{1,0:T(8,128)(2,1)S(1)}, u32[]{:S(2)}, u32[]{:S(2)}) collective-permute-start(bf16[112,768]{1,0:T(8,128)(2,1)S(1)} %get-tuple-element.283), channel_id=1, source_target_pairs={{0,1},{1,0},{2,3},{3,2},{4,5},{5,4},{6,7},{7,6},{8,9},{9,8},{10,11... | collective-permute-start | bytes 516104 | tf_op jit(solution)/shard_map/ppermute | solution.py:541
  (28 other events, 138.5 us)
